TPU v7x, 128 devices: a whole 4x4x4 slice. The times are simulated.
128 devices in a mesh: seq: 32 (over z, x, core), ch: 4 (over y).
Axes of the slice: x: 4, y: 4, z: 4, core: 2. Of those that a mesh axis runs over, the one named last changes fastest.
Arguments:
- streams: bfloat16 [3, 4096, 4096], P(None, 'seq', 'ch'), may hold values from -6 to 6
- short_taps: float32 [3, 3, 4096], P(None, None, 'ch'), may hold values from -3 to 3
- long_filter: float32 [4096, 4096], P('seq', 'ch'), may hold values from -0.09375 to 0.09375
- skip_gain: float32 [4096], P('ch'), may hold values from -4 to 4
- out_weights: bfloat16 [4096, 8192], P('ch'), may hold values from -0.09375 to 0.09375
Outputs:
- block_out: bfloat16 [4096, 8192], P('seq', 'ch')
All inputs are finite; a program needn't handle non-finite values.
Results may differ from a plain program's by a relative error of at most 0.005.
Values may be sent and summed in bfloat16 or wider, within the bound.
No kernel may reach another device: no remote copies, remote signals or barrier semaphores. Data moves between devices by JAX's collectives and lax.ppermute only.
A program may use at most 128 MiB of HBM per device.

v0:
```python
import math

import jax
import jax.numpy as jnp
from jax import lax
from jax.sharding import PartitionSpec as P

SHORT = 3


highest = lax.Precision.HIGHEST


def swapped(shard, axis, apart):
    return lax.ppermute(shard, axis, [(i, i ^ 1 << apart) for i in range(lax.axis_size(axis))])


def shifted(shard, axis, by):
    length = lax.axis_size(axis)
    pairs = [(i, i + by) for i in range(length) if 0 <= i + by < length]
    return lax.ppermute(shard, axis, pairs)


def rotate(value, angle):
    cosine = jnp.cos(angle)
    sine = jnp.sin(angle)
    return jnp.stack([value[0] * cosine - value[1] * sine, value[0] * sine + value[1] * cosine])


def angles(first, second, modulus):
    product = first[:, None] * second[None, :] % modulus
    return 2.0 * math.pi / modulus * product.astype(jnp.float32)


def local_transform(flat, count, sign):
    index = jnp.arange(count, dtype=jnp.int32)
    angle = angles(index, index, count)
    cosine = jnp.cos(angle)
    sine = sign * jnp.sin(angle)
    matrix = jnp.concatenate(
        [jnp.concatenate([cosine, -sine], axis=1), jnp.concatenate([sine, cosine], axis=1)], axis=0
    )
    return jnp.dot(matrix, flat, precision=highest)


def spectral_middle(current, column, row_count, length):
    frequency = column + jnp.arange(2, dtype=jnp.int32)
    twist = angles(frequency, jnp.arange(row_count, dtype=jnp.int32), length)[:, :, None]
    current = rotate(current, -twist)
    width = current.shape[-1]
    flat = jnp.moveaxis(current, 3, 1).reshape(2 * row_count, 4 * width)
    spectrum = local_transform(flat, row_count, -1.0).reshape(2, row_count, 2, 2, width)
    signal_spec = spectrum[:, :, 0]
    filter_spec = spectrum[:, :, 1]
    product = jnp.stack(
        [
            signal_spec[0] * filter_spec[0] - signal_spec[1] * filter_spec[1],
            signal_spec[0] * filter_spec[1] + signal_spec[1] * filter_spec[0],
        ]
    )
    back = local_transform(product.reshape(2 * row_count, 2 * width), row_count, 1.0).reshape(
        2, row_count, 2, width
    )
    back = jnp.moveaxis(back, 1, 2)
    return rotate(back, twist)


def butterfly_conv(gated, long_filter):
    parts = lax.axis_size("seq")
    my_index = lax.axis_index("seq")
    row_count = gated.shape[0]
    length = 2 * parts * row_count
    levels = parts.bit_length() - 1
    signals = jnp.stack([gated, long_filter])
    theta = math.pi / parts * my_index.astype(jnp.float32)
    real_part = jnp.stack([signals, signals * jnp.cos(theta)], axis=1)
    imag_part = jnp.stack([jnp.zeros_like(signals), -signals * jnp.sin(theta)], axis=1)
    current = jnp.stack([real_part, imag_part])
    for level in reversed(range(levels)):
        half = 2**level
        partner = swapped(current, "seq", level)
        upper = my_index // half % 2 == 1
        angle = -math.pi / half * (my_index % half).astype(jnp.float32)
        current = jnp.where(upper, rotate(partner - current, angle), current + partner)
    bit_reversed = jnp.int32(0)
    for level in range(levels):
        bit_reversed = bit_reversed + my_index // 2**level % 2 * 2 ** (levels - 1 - level)
    back = spectral_middle(current, 2 * bit_reversed, row_count, length)
    for level in range(levels):
        half = 2**level
        partner = swapped(back, "seq", level)
        upper = my_index // half % 2 == 1
        angle = math.pi / half * (my_index % half).astype(jnp.float32)
        back = jnp.where(upper, partner - rotate(back, angle), back + rotate(partner, angle))
    return (back[0, 0] + jnp.cos(theta) * back[0, 1] - jnp.sin(theta) * back[1, 1]) / length


def on_device(streams, short_taps, long_filter, skip_gain, out_weights):
    row_count = streams.shape[1]
    earlier = shifted(streams[:, row_count - (SHORT - 1) :, :], "seq", 1)
    padded = jnp.concatenate([earlier, streams], axis=1).astype(jnp.float32)
    short = jnp.zeros(streams.shape, jnp.float32)
    for offset in range(SHORT):
        window = padded[:, SHORT - 1 - offset : SHORT - 1 - offset + row_count, :]
        short = short + short_taps[:, offset][:, None, :] * window
    gated = short[1] * short[2]
    conv = butterfly_conv(gated, long_filter)
    mixed = (short[0] * (conv + skip_gain[None, :] * gated)).astype(jnp.bfloat16)
    partial_sum = jnp.dot(mixed, out_weights, preferred_element_type=jnp.float32)
    return lax.psum_scatter(partial_sum, "ch", scatter_dimension=1, tiled=True).astype(jnp.bfloat16)


def solution(mesh):
    return jax.shard_map(
        on_device,
        mesh=mesh,
        in_specs=(
            P(None, "seq", "ch"),
            P(None, None, "ch"),
            P("seq", "ch"),
            P("ch"),
            P("ch", None),
        ),
        out_specs=P("seq", "ch"),
        check_vma=False,
    )
```

profile of v0, /device:TPU:0, one launch (start us, length us, event | category | flops | bytes accessed | tf_op | source)
XLA Modules:
  0.0 774.6 jit_solution(15967849989876455065)
XLA Ops:
  6.5 0.8 slice.194
  7.4 1.3 collective-permute-start
  8.7 0.9 fusion.40
  9.8 1.4 maximum_convert_fusion
  11.8 1.3 copy-done.19
  13.9 2.5 pad_maximum_fusion
  16.6 8.6 %collective-permute-start.1 = (f32[2,2,2,128,1024]{4,3,2,1,0:T(8,128)}, f32[2,2,2,128,1024]{4,3,2,1,0:T(8,128)}, u32[]{:S(2)}, u32[]{:S(2)}) collective-permute-start(f32[2,2,2,128,1024]{4,3,2,1,0:T(8,128)} %pad_maximum_fusion), channel_id=1, source_target_pairs={{0,64},{4,68},{8,72},{12,76},{16,80},{20,84},{24,88},{28,92},{32,9... | collective-permute-start | bytes 12582920 | tf_op jit(solution)/shard_map/ppermute | solution.py:15
  25.4 88.4 %collective-permute-done.1 = f32[2,2,2,128,1024]{4,3,2,1,0:T(8,128)} collective-permute-done((f32[2,2,2,128,1024]{4,3,2,1,0:T(8,128)}, f32[2,2,2,128,1024]{4,3,2,1,0:T(8,128)}, u32[]{:S(2)}, u32[]{:S(2)}) %collective-permute-start.1) | collective-permute-done | bytes 4194336 | tf_op jit(solution)/shard_map/ppermute | solution.py:15
  113.8 3.8 fusion.39
  117.6 0.6 multiply_subtract_fusion.5
  118.2 1.0 copy-done.1
  119.2 6.2 maximum_select_fusion
  125.4 1.3 collective-permute-start.2
  126.9 88.2 %collective-permute-done.2 = f32[2,2,2,128,1024]{4,3,2,1,0:T(8,128)} collective-permute-done((f32[2,2,2,128,1024]{4,3,2,1,0:T(8,128)}, f32[2,2,2,128,1024]{4,3,2,1,0:T(8,128)}, u32[]{:S(2)}, u32[]{:S(2)}) %collective-permute-start.2) | collective-permute-done | bytes 4194336 | tf_op jit(solution)/shard_map/ppermute | solution.py:15
  215.2 6.2 fusion.47
  221.4 1.0 multiply_subtract_fusion.4
  222.3 0.6 copy-done.2
  222.9 0.6 copy-done.4
  223.6 0.6 copy-done.6
  224.2 6.1 maximum_select_fusion.1
  230.3 4.8 collective-permute-start.3
  235.3 88.7 %collective-permute-done.3 = f32[2,2,2,128,1024]{4,3,2,1,0:T(8,128)} collective-permute-done((f32[2,2,2,128,1024]{4,3,2,1,0:T(8,128)}, f32[2,2,2,128,1024]{4,3,2,1,0:T(8,128)}, u32[]{:S(2)}, u32[]{:S(2)}) %collective-permute-start.3) | collective-permute-done | bytes 4194336 | tf_op jit(solution)/shard_map/ppermute | solution.py:15
  324.0 4.4 sub.149
  329.0 7.1 maximum_select_fusion.2
  336.0 2.7 collective-permute-start.4
  338.9 88.1 %collective-permute-done.4 = f32[2,2,2,128,1024]{4,3,2,1,0:T(8,128)} collective-permute-done((f32[2,2,2,128,1024]{4,3,2,1,0:T(8,128)}, f32[2,2,2,128,1024]{4,3,2,1,0:T(8,128)}, u32[]{:S(2)}, u32[]{:S(2)}) %collective-permute-start.4) | collective-permute-done | bytes 4194336 | tf_op jit(solution)/shard_map/ppermute | solution.py:15
  427.0 4.4 sub.151
  432.0 7.1 maximum_select_fusion.3
  440.6 6.5 collective-permute-done.5
  447.1 4.4 sub.153
  452.0 5.0 maximum_select_fusion.4
  456.9 0.7 multiply_subtract_fusion
  458.2 5.2 copy.6
  463.4 6.8 reshape.299
  470.2 5.7 copy.7
  475.8 5.7 fusion.41
  482.2 1.6 copy.8
  483.8 2.2 copy.15
  486.0 1.9 copy.9
  488.0 1.9 convolution_bitcast_fusion
  490.9 3.9 collective-permute-done.6
  495.2 0.9 copy-done.7
  496.1 2.3 fusion
  498.5 1.9 collective-permute-start.7
  500.6 1.9 multiply_subtract_fusion.13
  502.5 44.1 %collective-permute-done.7 = f32[2,2,128,1024]{3,2,1,0:T(8,128)} collective-permute-done((f32[2,2,128,1024]{3,2,1,0:T(8,128)}, f32[2,2,128,1024]{3,2,1,0:T(8,128)}, u32[]{:S(2)}, u32[]{:S(2)}) %collective-permute-start.7) | collective-permute-done | bytes 2097184 | tf_op jit(solution)/shard_map/ppermute | solution.py:15
  546.7 1.8 multiply_subtract_fusion.12
  548.5 3.9 fusion.1
  552.5 2.9 collective-permute-start.8
  555.6 1.8 multiply_subtract_fusion.11
  557.4 43.6 %collective-permute-done.8 = f32[2,2,128,1024]{3,2,1,0:T(8,128)S(1)} collective-permute-done((f32[2,2,128,1024]{3,2,1,0:T(8,128)}, f32[2,2,128,1024]{3,2,1,0:T(8,128)S(1)}, u32[]{:S(2)}, u32[]{:S(2)}) %collective-permute-start.8) | collective-permute-done | bytes 2097184 | tf_op jit(solution)/shard_map/ppermute | solution.py:15
  601.3 1.1 copy-done.16
  602.4 3.2 fusion.2
  605.6 1.4 collective-permute-start.9
  607.4 44.3 %collective-permute-done.9 = f32[2,2,128,1024]{3,2,1,0:T(8,128)} collective-permute-done((f32[2,2,128,1024]{3,2,1,0:T(8,128)S(1)}, f32[2,2,128,1024]{3,2,1,0:T(8,128)}, u32[]{:S(2)}, u32[]{:S(2)}) %collective-permute-start.9) | collective-permute-done | bytes 2097184 | tf_op jit(solution)/shard_map/ppermute | solution.py:15
  651.7 1.8 multiply_subtract_fusion.8
  653.5 3.9 fusion.3
  657.4 2.3 collective-permute-start.10
  659.9 1.8 multiply_subtract_fusion.7
  661.7 42.4 %collective-permute-done.10 = f32[2,2,128,1024]{3,2,1,0:T(8,128)S(1)} collective-permute-done((f32[2,2,128,1024]{3,2,1,0:T(8,128)}, f32[2,2,128,1024]{3,2,1,0:T(8,128)S(1)}, u32[]{:S(2)}, u32[]{:S(2)}) %collective-permute-start.10) | collective-permute-done | bytes 2097184 | tf_op jit(solution)/shard_map/ppermute | solution.py:15
  704.5 2.6 fusion.4
  707.1 10.4 %fusion.17 = f32[128,8192]{1,0:T(8,128)} fusion(bf16[1024,8192]{1,0:T(8,128)(2,1)} %param.9, f32[2,2,128,1024]{3,2,1,0:T(8,128)S(1)} %fusion.4, f32[3,128,1024]{2,1,0:T(8,128)} %copy-done.9, f32[1,128,1024]{2,1,0:T(8,128)S(1)} %copy-done.18, f32[1024]{0:T(1024)S(1)} %copy-done.20, f32[]{:T(128)S(6)} %sin.63, f32[]{:T(128)S(6)} %cos.63), kind=kOutput, calls=%fused_computation.91 | convolution fusion | flops 2148663296 | bytes 23597064 | tf_op jit(solution)/shard_map/dot_general | solution.py:109
  717.6 47.8 %reduce-scatter.2.cloned.1.call-done = f32[128,2048]{1,0:T(8,128)} async-done(((f32[128,8192]{1,0:T(8,128)}), f32[128,2048]{1,0:T(8,128)}) %reduce-scatter.2.cloned.1.call-update) | async-done | bytes 1048592 | tf_op jit(solution)/shard_map/reduce_scatter | solution.py:110
  765.4 2.1 convert_element_type.76
  (68 shorter events, 8.1 us)
Async XLA Ops:
  6.5 758.9 %reduce-scatter.2.cloned.1.call-start = ((), (), s32[]{:S(2)}) async-start(), calls=%async_computation.1 | async-start | bytes 5242880 | tf_op jit(solution)/shard_map/reduce_scatter | solution.py:110
  7.4 2.4 collective-permute-start
  11.7 1.6 copy-start.9
  11.7 1.4 copy-start.19
  11.8 1.7 copy-start.17
  13.9 2.7 copy-start
  16.6 97.2 %collective-permute-start.1 = (f32[2,2,2,128,1024]{4,3,2,1,0:T(8,128)}, f32[2,2,2,128,1024]{4,3,2,1,0:T(8,128)}, u32[]{:S(2)}, u32[]{:S(2)}) collective-permute-start(f32[2,2,2,128,1024]{4,3,2,1,0:T(8,128)} %pad_maximum_fusion), channel_id=1, source_target_pairs={{0,64},{4,68},{8,72},{12,76},{16,80},{20,84},{24,88},{28,92},{32,9... | collective-permute-start | bytes 12582920 | tf_op jit(solution)/shard_map/ppermute | solution.py:15
  117.6 1.6 copy-start.1
  118.2 7.2 copy-start.3
  118.2 7.2 copy-start.5
  125.4 89.7 %collective-permute-start.2 = (f32[2,2,2,128,1024]{4,3,2,1,0:T(8,128)}, f32[2,2,2,128,1024]{4,3,2,1,0:T(8,128)}, u32[]{:S(2)}, u32[]{:S(2)}) collective-permute-start(f32[2,2,2,128,1024]{4,3,2,1,0:T(8,128)} %maximum_select_fusion), channel_id=1, source_target_pairs={{0,32},{4,36},{8,40},{12,44},{16,48},{20,52},{24,56},{28,60},{32,0... | collective-permute-start | bytes 12582920 | tf_op jit(solution)/shard_map/ppermute | solution.py:15
  221.3 1.6 copy-start.2
  221.3 2.2 copy-start.4
  221.4 2.8 copy-start.6
  230.3 93.7 %collective-permute-start.3 = (f32[2,2,2,128,1024]{4,3,2,1,0:T(8,128)}, f32[2,2,2,128,1024]{4,3,2,1,0:T(8,128)}, u32[]{:S(2)}, u32[]{:S(2)}) collective-permute-start(f32[2,2,2,128,1024]{4,3,2,1,0:T(8,128)} %maximum_select_fusion.1), channel_id=1, source_target_pairs={{0,16},{4,20},{8,24},{12,28},{16,0},{20,4},{24,8},{28,12},{32,48},... | collective-permute-start | bytes 12582920 | tf_op jit(solution)/shard_map/ppermute | solution.py:15
  336.0 91.0 %collective-permute-start.4 = (f32[2,2,2,128,1024]{4,3,2,1,0:T(8,128)}, f32[2,2,2,128,1024]{4,3,2,1,0:T(8,128)}, u32[]{:S(2)}, u32[]{:S(2)}) collective-permute-start(f32[2,2,2,128,1024]{4,3,2,1,0:T(8,128)} %maximum_select_fusion.2), channel_id=1, source_target_pairs={{0,8},{4,12},{8,0},{12,4},{16,24},{20,28},{24,16},{28,20},{32,40},... | collective-permute-start | bytes 12582920 | tf_op jit(solution)/shard_map/ppermute | solution.py:15
  439.1 8.0 %collective-permute-start.5 = (f32[2,2,2,128,1024]{4,3,2,1,0:T(8,128)}, f32[2,2,2,128,1024]{4,3,2,1,0:T(8,128)}, u32[]{:S(2)}, u32[]{:S(2)}) collective-permute-start(f32[2,2,2,128,1024]{4,3,2,1,0:T(8,128)} %maximum_select_fusion.3), channel_id=1, source_target_pairs={{0,4},{4,0},{8,12},{12,8},{16,20},{20,16},{24,28},{28,24},{32,36},... | collective-permute-start | bytes 12582920 | tf_op jit(solution)/shard_map/ppermute | solution.py:15
  490.5 4.2 collective-permute-start.6
  490.9 4.3 copy-start.10
  494.8 1.4 copy-start.7
  495.1 3.3 copy-start.12
  495.2 3.3 copy-start.14
  498.5 48.2 %collective-permute-start.7 = (f32[2,2,128,1024]{3,2,1,0:T(8,128)}, f32[2,2,128,1024]{3,2,1,0:T(8,128)}, u32[]{:S(2)}, u32[]{:S(2)}) collective-permute-start(f32[2,2,128,1024]{3,2,1,0:T(8,128)} %fusion), channel_id=1, source_target_pairs={{0,8},{4,12},{8,0},{12,4},{16,24},{20,28},{24,16},{28,20},{32,40},... | collective-permute-start | bytes 6291464 | tf_op jit(solution)/shard_map/ppermute | solution.py:15
  500.6 47.9 %copy-start.15 = (f32[1,2,128,1024]{3,2,1,0:T(8,128)S(1)}, f32[1,2,128,1024]{3,2,1,0:T(8,128)}, u32[]{:S(2)}) copy-start(f32[1,2,128,1024]{3,2,1,0:T(8,128)} %copy-done.14) | copy-start | bytes 3145732
  502.5 46.0 %copy-start.8 = (f32[2,2,128,1024]{3,2,1,0:T(8,128)S(1)}, f32[2,2,128,1024]{3,2,1,0:T(8,128)}, u32[]{:S(2)}) copy-start(f32[2,2,128,1024]{3,2,1,0:T(8,128)} %copy-done.7) | copy-start | bytes 6291460
  502.5 46.0 %copy-start.11 = (f32[1,2,128,1024]{3,2,1,0:T(8,128)S(1)}, f32[1,2,128,1024]{3,2,1,0:T(8,128)}, u32[]{:S(2)}) copy-start(f32[1,2,128,1024]{3,2,1,0:T(8,128)} %copy-done.10) | copy-start | bytes 3145732
  502.5 46.0 %copy-start.13 = (f32[1,2,128,1024]{3,2,1,0:T(8,128)S(1)}, f32[1,2,128,1024]{3,2,1,0:T(8,128)}, u32[]{:S(2)}) copy-start(f32[1,2,128,1024]{3,2,1,0:T(8,128)} %copy-done.12) | copy-start | bytes 3145732
  552.5 48.6 %collective-permute-start.8 = (f32[2,2,128,1024]{3,2,1,0:T(8,128)}, f32[2,2,128,1024]{3,2,1,0:T(8,128)S(1)}, u32[]{:S(2)}, u32[]{:S(2)}) collective-permute-start(f32[2,2,128,1024]{3,2,1,0:T(8,128)} %fusion.1), channel_id=1, source_target_pairs={{0,16},{4,20},{8,24},{12,28},{16,0},{20,4},{24,8},{28,12},{32,48},... | collective-permute-start | bytes 6291464 | tf_op jit(solution)/shard_map/ppermute | solution.py:15
  601.0 1.4 copy-start.16
  605.6 46.1 %collective-permute-start.9 = (f32[2,2,128,1024]{3,2,1,0:T(8,128)S(1)}, f32[2,2,128,1024]{3,2,1,0:T(8,128)}, u32[]{:S(2)}, u32[]{:S(2)}) collective-permute-start(f32[2,2,128,1024]{3,2,1,0:T(8,128)S(1)} %fusion.2), channel_id=1, source_target_pairs={{0,32},{4,36},{8,40},{12,44},{16,48},{20,52},{24,56},{28,60},{32,0... | collective-permute-start | bytes 6291464 | tf_op jit(solution)/shard_map/ppermute | solution.py:15
  657.4 46.7 %collective-permute-start.10 = (f32[2,2,128,1024]{3,2,1,0:T(8,128)}, f32[2,2,128,1024]{3,2,1,0:T(8,128)S(1)}, u32[]{:S(2)}, u32[]{:S(2)}) collective-permute-start(f32[2,2,128,1024]{3,2,1,0:T(8,128)} %fusion.3), channel_id=1, source_target_pairs={{0,64},{4,68},{8,72},{12,76},{16,80},{20,84},{24,88},{28,92},{32,9... | collective-permute-start | bytes 6291464 | tf_op jit(solution)/shard_map/ppermute | solution.py:15
  704.5 2.7 copy-start.18
  704.5 2.7 copy-start.20
Sparse Core Ops, SparseCore 0:
  717.7 47.6 reduce-scatter.1
where the time goes:
time: 783 us; the launch traced here: 775 us
  waiting for transfers between devices  586 us (75%)
  other arithmetic  94.8 us (12%)
  local copies, waits for them, and re-layouts  31.8 us (4%)
  starting transfers between devices  28 us (4%)
  matrix products  18.1 us (2%)
  between operations  15.8 us (2%)
    ppermute x10, waiting for transfers between devices, swapped(): lax.ppermute(shard, axis, [(i, i ^ 1 << apart) for i in range(lax.axis_si...  538 us
    reduce_scatter x1, waiting for transfers between devices, on_device(): lax.psum_scatter(partial_sum, 'ch', scatter_dimension=1, tiled=True)  47.8 us
    select_n x5, other arithmetic, butterfly_conv(): jnp.where(upper, rotate(partner - current, angle), current + partner)  31.4 us
    ppermute x10, starting transfers between devices, swapped(): lax.ppermute(shard, axis, [(i, i ^ 1 << apart) for i in range(lax.axis_si...  26.7 us
    sub x5, other arithmetic, butterfly_conv(): partner - current  23.2 us
    select_n x5, other arithmetic, butterfly_conv(): jnp.where(upper, partner - rotate(back, angle), back + rotate(partner, an...  16 us
  transfers between devices with their start and end apart: 12, of which 11 were waited for; matrix products, arithmetic and copies ran while one was open for 1% of the time, Pallas kernels for 0%

commit v1 on v0

v1 whole, which is shorter than its diff:
```python
import functools
import math

import jax
import jax.numpy as jnp
import numpy as np
from jax import lax
from jax.experimental import pallas as pl
from jax.experimental.pallas import tpu as pltpu
from jax.sharding import PartitionSpec as P

SHORT = 3
STREAMS = 3
ROWS = 128
PARTS = 32
GROUP = 32
SLAB = 16
POINTS = PARTS * ROWS
f32 = jnp.float32
bf16 = jnp.bfloat16


def tables():
    r = np.arange(ROWS)
    angle = 2.0 * np.pi * (np.outer(r, r) % ROWS) / ROWS
    cosine, sine = np.cos(angle), np.sin(angle)
    matrix = np.block([[cosine, -sine], [sine, cosine]])
    high = matrix.astype(np.float32).astype(bf16)
    low = (matrix - high.astype(np.float64)).astype(np.float32).astype(bf16)
    j = np.arange(PARTS)
    twist = 2.0 * np.pi * np.outer(4 * j + 1, r) / (4 * POINTS)
    twists = np.stack([np.cos(twist), np.sin(twist)], axis=1).astype(np.float32)
    return high, low, twists


def turned(value, turns):
    real, imag = value
    eighth = turns * 8 % 8
    if eighth == 0:
        return real, imag
    if eighth == 2:
        return -imag, real
    if eighth == 4:
        return -real, -imag
    if eighth == 6:
        return imag, -real
    if eighth in (1, 3, 5, 7):
        half = math.sqrt(0.5)
        total, apart = (real + imag) * half, (real - imag) * half
        return {1: (apart, total), 3: (-total, apart), 5: (-apart, -total), 7: (total, -apart)}[int(eighth)]
    c, s = math.cos(2.0 * math.pi * turns), math.sin(2.0 * math.pi * turns)
    return real * c - imag * s, real * s + imag * c


def plus(a, b):
    return a[0] + b[0], a[1] + b[1]


def minus(a, b):
    return a[0] - b[0], a[1] - b[1]


def small_transform(values, sign):
    count = len(values)
    if count == 1:
        return values
    even = small_transform(values[0::2], sign)
    odd = small_transform(values[1::2], sign)
    odd = [turned(value, sign * k / count) for k, value in enumerate(odd)]
    return [plus(a, b) for a, b in zip(even, odd)] + [minus(a, b) for a, b in zip(even, odd)]


def exchange_kernel(streams_ref, filter_ref, out_ref):
    groups = out_ref.shape[0]
    for j in range(STREAMS + 1):
        block = streams_ref[j].astype(f32) if j < STREAMS else filter_ref[...]
        turned_block = block.T.astype(bf16).reshape(groups, GROUP, ROWS)
        out_ref[:, j * GROUP : (j + 1) * GROUP, :] = turned_block


def split(value):
    high = value.astype(bf16)
    return high, (value - high.astype(f32)).astype(bf16)


def conv_kernel(x_ref, taps_ref, skip_ref, high_ref, low_ref, twists_ref, out_ref, gated_ref, first_ref, left_ref, back_ref):
    lane = lax.broadcasted_iota(jnp.int32, (SLAB, ROWS), 1)

    def rows_of(j, offset):
        return pl.ds(pl.multiple_of(j * GROUP + offset, SLAB), SLAB)

    def short(stream, offset):
        taps = [taps_ref[stream * SHORT + i, pl.ds(offset, SLAB), :] for i in range(SHORT)]
        before = [jnp.zeros((SLAB, ROWS), f32)] * 2
        for s in range(PARTS):
            now = x_ref[s, rows_of(stream, offset), :].astype(f32)
            moved = [pltpu.roll(now, i, 1) for i in (1, 2)]
            total = taps[0] * now
            for i in (1, 2):
                total = total + taps[i] * jnp.where(lane < i, before[i - 1], moved[i - 1])
            before = moved
            yield total

    def forward(slot, offset, load):
        for a in range(8):
            values = []
            for q in range(4):
                value = load(a + 8 * q)
                angle = -2.0 * math.pi * q / 16
                values.append((value * math.cos(angle), value * math.sin(angle)) if q else (value, jnp.zeros_like(value)))
            for m, value in enumerate(small_transform(values, -1)):
                real, imag = turned(value, -a * (4 * m + 1) / 128)
                first_ref[m, a, 0] = real
                first_ref[m, a, 1] = imag
        for m in range(4):
            values = [(first_ref[m, a, 0], first_ref[m, a, 1]) for a in range(8)]
            for p, (real, imag) in enumerate(small_transform(values, -1)):
                j = 4 * p + m
                c, s = twists_ref[j, 0][None, :], twists_ref[j, 1][None, :]
                for half, part in enumerate((real * c + imag * s, imag * c - real * s)):
                    high, low = split(part)
                    left_ref[slot, 0, rows_of(j, offset), half * ROWS : (half + 1) * ROWS] = high
                    left_ref[slot, 1, rows_of(j, offset), half * ROWS : (half + 1) * ROWS] = low

    @pl.loop(0, GROUP // SLAB)
    def _(step):
        offset = pl.multiple_of(step * SLAB, SLAB)
        for s, (key, value) in enumerate(zip(short(1, offset), short(2, offset))):
            gated_ref[s, pl.ds(offset, SLAB), :] = key * value
        forward(0, offset, lambda s: gated_ref[s, pl.ds(offset, SLAB), :])
        forward(1, offset, lambda s: x_ref[s, rows_of(STREAMS, offset), :].astype(f32))

    def product(high, low):
        total = jnp.dot(low, high_ref[...], preferred_element_type=f32)
        total = total + jnp.dot(high, low_ref[...], preferred_element_type=f32)
        return total + jnp.dot(high, high_ref[...], preferred_element_type=f32)

    block = 256

    @pl.loop(0, PARTS * GROUP // block)
    def _(step):
        rows = pl.ds(pl.multiple_of(step * block, block), block)
        signal = product(left_ref[0, 0, rows, :], left_ref[0, 1, rows, :])
        taps = product(left_ref[1, 0, rows, :], left_ref[1, 1, rows, :])
        a, b = signal[:, :ROWS], signal[:, ROWS:]
        c, d = taps[:, :ROWS], taps[:, ROWS:]
        real, imag = split((a * c - b * d) * (1.0 / POINTS)), split((a * d + b * c) * (-1.0 / POINTS))
        high = jnp.concatenate([real[0], imag[0]], axis=1)
        low = jnp.concatenate([real[1], imag[1]], axis=1)
        back_ref[rows, :] = product(high, low)

    @pl.loop(0, GROUP // SLAB)
    def _(step):
        offset = pl.multiple_of(step * SLAB, SLAB)
        for m in range(4):
            values = []
            for p in range(8):
                j = 4 * p + m
                real = back_ref[rows_of(j, offset), :ROWS]
                imag = -back_ref[rows_of(j, offset), ROWS:]
                c, s = twists_ref[j, 0][None, :], twists_ref[j, 1][None, :]
                values.append((real * c - imag * s, real * s + imag * c))
            for a, value in enumerate(small_transform(values, 1)):
                real, imag = turned(value, a * (4 * m + 1) / 128)
                first_ref[m, a, 0] = real
                first_ref[m, a, 1] = imag
        skip = skip_ref[pl.ds(offset, SLAB), :]
        for a in range(8):
            values = [(first_ref[m, a, 0], first_ref[m, a, 1]) for m in range(4)]
            for q, (real, imag) in enumerate(small_transform(values, 1)):
                angle = 2.0 * math.pi * q / 16
                conv = real * math.cos(angle) - imag * math.sin(angle) if q else real
                s = a + 8 * q
                gated = gated_ref[s, pl.ds(offset, SLAB), :]
                gated_ref[s, pl.ds(offset, SLAB), :] = conv + skip * gated
        for s, query in enumerate(short(0, offset)):
            out_ref[s, pl.ds(offset, SLAB), :] = (query * gated_ref[s, pl.ds(offset, SLAB), :]).astype(bf16)


def far_kernel(index_ref, mixed_ref, weights_ref, out_ref, rows_ref):
    @pl.when(pl.program_id(0) == 0)
    def _():
        rows_ref[...] = mixed_ref[...].astype(f32).T.astype(bf16)

    out_ref[0] = jnp.dot(rows_ref[...], weights_ref[...], preferred_element_type=f32).astype(out_ref.dtype)


def near_kernel(index_ref, rows_ref, weights_ref, out_ref):
    out_ref[0] = jnp.dot(rows_ref[...], weights_ref[...], preferred_element_type=f32).astype(out_ref.dtype)


def adding_kernel(index_ref, rows_ref, weights_ref, up_ref, down_ref, out_ref):
    half = pl.num_programs(0) // 2
    arrived = jnp.where(pl.program_id(0) < half, up_ref[...], down_ref[...]).astype(f32)
    total = jnp.dot(rows_ref[...], weights_ref[...], preferred_element_type=f32)
    out_ref[0] = (total + arrived).astype(out_ref.dtype)


WIDE = 512


def share(kernel, index, rows, weights, dtype, arrived=(), first=False):
    count = index.shape[0]
    depth = weights.shape[0]
    half = count // 2
    row_spec = pl.BlockSpec(rows.shape, lambda i, index: (0, 0))
    in_specs = [row_spec, pl.BlockSpec((depth, WIDE), lambda i, index: (0, index[i]))]
    if arrived:
        in_specs.append(pl.BlockSpec((ROWS, WIDE), lambda i, index: (0, jnp.minimum(i, half - 1))))
        in_specs.append(pl.BlockSpec((ROWS, WIDE), lambda i, index: (0, jnp.maximum(i - half, 0))))
    out_shape = [jax.ShapeDtypeStruct((2, ROWS, half * WIDE), dtype)]
    out_specs = [pl.BlockSpec((1, ROWS, WIDE), lambda i, index: (i // half, 0, i % half))]
    if first:
        out_shape.append(jax.ShapeDtypeStruct((ROWS, depth), bf16))
        out_specs.append(pl.BlockSpec((ROWS, depth), lambda i, index: (0, 0)))
    return pl.pallas_call(
        kernel,
        grid_spec=pltpu.PrefetchScalarGridSpec(
            num_scalar_prefetch=1, grid=(count,), in_specs=in_specs, out_specs=out_specs
        ),
        out_shape=out_shape,
        cost_estimate=pl.CostEstimate(
            flops=2 * ROWS * depth * count * WIDE, bytes_accessed=2 * depth * count * WIDE, transcendentals=0
        ),
        compiler_params=pltpu.CompilerParams(vmem_limit_bytes=32 * 2**20),
    )(index, rows, weights, *arrived)


def project(mixed, weights):
    ring = lax.axis_size("ch")
    me = lax.axis_index("ch")
    up = [(i, (i + 1) % ring) for i in range(ring)]
    down = [(i, (i - 1) % ring) for i in range(ring)]
    blocks = weights.shape[1] // ring // WIDE
    half = blocks // 2

    def numbers(away, start, stop):
        return (me + away) % ring * blocks + jnp.arange(start, stop, dtype=jnp.int32)

    far, rows = share(far_kernel, numbers(2, 0, blocks), mixed, weights, bf16, first=True)
    far_up = lax.ppermute(far[0], "ch", up)
    far_down = lax.ppermute(far[1], "ch", down)
    index = jnp.concatenate([numbers(1, half, blocks), numbers(-1, 0, half)])
    (near,) = share(near_kernel, index, rows, weights, bf16)
    near_up = lax.ppermute(near[0], "ch", up)
    near_down = lax.ppermute(near[1], "ch", down)
    index = jnp.concatenate([numbers(1, 0, half), numbers(-1, half, blocks)])
    (both,) = share(adding_kernel, index, rows, weights, bf16, arrived=(far_up, far_down))
    both_up = lax.ppermute(both[0], "ch", up)
    both_down = lax.ppermute(both[1], "ch", down)
    (own,) = share(near_kernel, numbers(0, 0, blocks), rows, weights, f32)
    left = own[0] + both_up.astype(f32) + near_down.astype(f32)
    right = own[1] + near_up.astype(f32) + both_down.astype(f32)
    return jnp.concatenate([left, right], axis=1).astype(bf16)


def on_device(streams, short_taps, long_filter, skip_gain, out_weights):
    channels = streams.shape[2]
    wide = 256
    packed = pl.pallas_call(
        exchange_kernel,
        grid=(channels // wide,),
        in_specs=[
            pl.BlockSpec((STREAMS, ROWS, wide), lambda i: (0, 0, i)),
            pl.BlockSpec((ROWS, wide), lambda i: (0, i)),
        ],
        out_specs=pl.BlockSpec((wide // GROUP, (STREAMS + 1) * GROUP, ROWS), lambda i: (i, 0, 0)),
        out_shape=jax.ShapeDtypeStruct((PARTS, (STREAMS + 1) * GROUP, ROWS), bf16),
    )(streams, long_filter)
    first = lax.axis_index("seq") * GROUP
    taps = lax.dynamic_slice_in_dim(short_taps.reshape(STREAMS * SHORT, channels), first, GROUP, 1)
    taps = jnp.broadcast_to(taps[:, :, None], (STREAMS * SHORT, GROUP, ROWS))
    skip = jnp.broadcast_to(lax.dynamic_slice_in_dim(skip_gain, first, GROUP, 0)[:, None], (GROUP, ROWS))
    arrived = lax.all_to_all(packed, "seq", 0, 0, tiled=True)
    high, low, twists = tables()
    whole = pl.BlockSpec(memory_space=pltpu.VMEM)
    mixed = pl.pallas_call(
        conv_kernel,
        in_specs=[whole] * 6,
        out_specs=whole,
        out_shape=jax.ShapeDtypeStruct((PARTS, GROUP, ROWS), bf16),
        scratch_shapes=[
            pltpu.VMEM((PARTS, GROUP, ROWS), f32),
            pltpu.VMEM((4, 8, 2, SLAB, ROWS), f32),
            pltpu.VMEM((2, 2, PARTS * GROUP, 2 * ROWS), bf16),
            pltpu.VMEM((PARTS * GROUP, 2 * ROWS), f32),
        ],
        compiler_params=pltpu.CompilerParams(vmem_limit_bytes=32 * 2**20),
    )(arrived, taps, skip, jnp.asarray(high), jnp.asarray(low), jnp.asarray(twists))
    mixed = lax.all_to_all(mixed, "seq", 0, 0, tiled=True)
    return project(mixed.reshape(channels, ROWS), out_weights)


def solution(mesh):
    return jax.shard_map(
        on_device,
        mesh=mesh,
        in_specs=(
            P(None, "seq", "ch"),
            P(None, None, "ch"),
            P("seq", "ch"),
            P("ch"),
            P("ch", None),
        ),
        out_specs=P("seq", "ch"),
        check_vma=False,
    )
```

time: 783 us -> 90.2 us (0.12)
  waiting for transfers between devices: 586 us -> 24.7 us
  other arithmetic: 94.8 us -> 1.26 us
  Pallas kernels: 0 us -> 19.7 us
  matrix products: 18.1 us -> 0 us
  between operations: 15.8 us -> 0.18 us
  local copies, waits for them, and re-layouts: 31.8 us -> 21.8 us
    ppermute x11 -> x6, waiting for transfers between devices: 538 us -> 0.35 us  [the longest x1 0.34 us: project(): both_up = lax.ppermute(both[0], 'ch', up)]
    reduce_scatter x1 -> x0, waiting for transfers between devices: 47.8 us -> none  [on_device(): lax.psum_scatter(partial_sum, 'ch', scatter_dimension=1, tiled=True)]
    select_n x10 -> x0, other arithmetic: 47.4 us -> none  [the longest x5 31.4 us: butterfly_conv(): jnp.where(upper, rotate(partner - current, angle), current + partner)]
    sub x22 -> x0, other arithmetic: 38.3 us -> none  [the longest x5 23.2 us: butterfly_conv(): partner - current]
    all_to_all x0 -> x2, waiting for transfers between devices: none -> 24.4 us  [the longest x1 15.6 us: on_device(): arrived = lax.all_to_all(packed, 'seq', 0, 0, tiled=True)]
    pallas_call x0 -> x6, Pallas kernels: none -> 19.7 us  [the longest x4 9.77 us: share(): pl.pallas_call(kernel, grid_spec=pltpu.PrefetchScalarGridSpec(num_scalar_...]
    ppermute x11 -> x6, starting transfers between devices: 28 us -> 9.76 us  [the longest x1 3.31 us: project(): near_down = lax.ppermute(near[1], 'ch', down)]
    dot_general x3 -> x0, matrix products: 18.1 us -> none  [the longest x1 10.4 us: on_device(): jnp.dot(mixed, out_weights, preferred_element_type=jnp.float32)]
  transfers between devices with their start and end apart: 12 -> 8, of which waited for: 11 -> 3; matrix products, arithmetic and copies ran while one was open for 1% -> 2% of each run, Pallas kernels for 0% -> 8%
where the time goes in v1:
time: 90.2 us; the launch traced here: 89.5 us
  waiting for transfers between devices  24.7 us (27%)
  starting transfers between devices  21.9 us (24%)
  local copies, waits for them, and re-layouts  21.8 us (24%)
  Pallas kernels  19.7 us (22%)
  other arithmetic  1.26 us (1%)
    unnamed x12, local copies, waits for them, and re-layouts  19.9 us
    all_to_all x1, waiting for transfers between devices, on_device(): arrived = lax.all_to_all(packed, 'seq', 0, 0, tiled=True)  15.6 us
    pallas_call x4, Pallas kernels, share(): pl.pallas_call(kernel, grid_spec=pltpu.PrefetchScalarGridSpec(num_scalar_...  9.77 us
    all_to_all x1, waiting for transfers between devices, on_device(): mixed = lax.all_to_all(mixed, 'seq', 0, 0, tiled=True)  8.74 us
    all_to_all x1, starting transfers between devices, on_device(): arrived = lax.all_to_all(packed, 'seq', 0, 0, tiled=True)  8.25 us
    pallas_call x1, Pallas kernels, on_device(): pl.pallas_call(conv_kernel, in_specs=[whole] * 6, out_specs=whole, out_sh...  6.21 us
    all_to_all x1, starting transfers between devices, on_device(): mixed = lax.all_to_all(mixed, 'seq', 0, 0, tiled=True)  3.87 us
    pallas_call x1, Pallas kernels, on_device(): pl.pallas_call(exchange_kernel, grid=(channels // wide,), in_specs=[pl.Bl...  3.72 us
  transfers between devices with their start and end apart: 8, of which 3 were waited for; matrix products, arithmetic and copies ran while one was open for 2% of the time, Pallas kernels for 8%

profile of v1, /device:TPU:0, one launch (start us, length us, event | category | flops | bytes accessed | tf_op | source)
XLA Modules:
  0.0 89.5 jit_solution(2486310476905173440)
XLA Ops:
  0.0 3.7 %shard_map.82 = bf16[32,128,128]{2,1,0:T(8,128)(2,1)} custom-call(bf16[3,128,1024]{2,1,0:T(8,128)(2,1)} %streams_ref.1, f32[128,1024]{1,0:T(8,128)} %filter_ref.1), custom_call_target="tpu_custom_call" | custom-call | tf_op jit(solution)/shard_map/pallas_call | solution.py:260
  3.7 8.2 %all-to-all-start = ((bf16[32,128,128]{2,1,0:T(8,128)(2,1)}), bf16[32,128,128]{2,1,0:T(8,128)(2,1)S(1)}, u32[]{:S(2)}, u32[]{:S(2)}) async-start(bf16[32,128,128]{2,1,0:T(8,128)(2,1)} %shard_map.82), calls=%async_computation | async-start | bytes 2097152 | tf_op jit(solution)/shard_map/all_to_all | solution.py:274
  12.0 0.8 reshape.8
  12.8 0.8 dynamic_slice.7
  13.6 0.1 constant_dynamic-slice_fusion
  13.7 15.6 %all-to-all-done.x_ref = bf16[32,128,128]{2,1,0:T(8,128)(2,1)S(1)} async-done(((bf16[32,128,128]{2,1,0:T(8,128)(2,1)}), bf16[32,128,128]{2,1,0:T(8,128)(2,1)S(1)}, u32[]{:S(2)}, u32[]{:S(2)}) %all-to-all-start) | async-done | bytes 1048608 | tf_op jit(solution)/shard_map/all_to_all | solution.py:274
  29.3 0.1 broadcast_in_dim.5.skip_ref
  29.4 0.1 broadcast_in_dim.4.taps_ref
  29.5 0.0 copy-start.3
  29.5 0.9 %copy-done.3 = bf16[256,256]{1,0:T(8,128)(2,1)S(1)} copy-done((bf16[256,256]{1,0:T(8,128)(2,1)S(1)}, bf16[256,256]{1,0:T(8,128)(2,1)}, u32[]{:S(2)}) %copy-start.3) | copy-done | bytes 131096
  30.4 0.0 copy-start.4
  30.4 0.9 %copy-done.4 = bf16[256,256]{1,0:T(8,128)(2,1)S(1)} copy-done((bf16[256,256]{1,0:T(8,128)(2,1)S(1)}, bf16[256,256]{1,0:T(8,128)(2,1)}, u32[]{:S(2)}) %copy-start.4) | copy-done | bytes 131096
  31.3 0.0 copy-start.5
  31.3 0.8 copy-done.5
  32.1 6.2 %shard_map.83 = bf16[32,32,128]{2,1,0:T(8,128)(2,1)} custom-call(bf16[32,128,128]{2,1,0:T(8,128)(2,1)S(1)} %all-to-all-done.x_ref, f32[9,32,128]{2,1,0:T(8,128)S(1)} %broadcast_in_dim.4.taps_ref, f32[32,128]{1,0:T(8,128)S(1)} %broadcast_in_dim.5.skip_ref, bf16[256,256]{1,0:T(8,128)(2,1)S(1)} %copy-done.4, bf16[256,256]{1,0:T(8,128)(2,1)S(1)} %copy-done.3, ...), custom_call_target="tpu_custom_call" | custom-call | tf_op jit(solution)/shard_map/pallas_call | solution.py:277
  38.3 3.9 %all-to-all-start.1 = ((bf16[32,32,128]{2,1,0:T(8,128)(2,1)}), bf16[32,32,128]{2,1,0:T(8,128)(2,1)S(1)}, u32[]{:S(2)}, u32[]{:S(2)}) async-start(bf16[32,32,128]{2,1,0:T(8,128)(2,1)} %shard_map.83), calls=%async_computation.1 | async-start | bytes 524288 | tf_op jit(solution)/shard_map/all_to_all | solution.py:290
  42.2 0.1 pad_add_fusion.1.index_ref
  42.2 0.1 pad_add_fusion.index_ref
  42.3 8.7 %all-to-all-done.1 = bf16[32,32,128]{2,1,0:T(8,128)(2,1)S(1)} async-done(((bf16[32,32,128]{2,1,0:T(8,128)(2,1)}), bf16[32,32,128]{2,1,0:T(8,128)(2,1)S(1)}, u32[]{:S(2)}, u32[]{:S(2)}) %all-to-all-start.1) | async-done | bytes 262176 | tf_op jit(solution)/shard_map/all_to_all | solution.py:290
  51.1 0.0 copy-start
  51.1 5.8 %copy-done = bf16[1024,8192]{1,0:T(8,128)(2,1)S(1)} copy-done((bf16[1024,8192]{1,0:T(8,128)(2,1)S(1)}, bf16[1024,8192]{1,0:T(8,128)(2,1)}, u32[]{:S(2)}) %copy-start) | copy-done | bytes 16777240
  56.8 2.5 %shard_map.84 = (bf16[2,128,1024]{2,1,0:T(8,128)(2,1)S(1)}, bf16[128,1024]{1,0:T(8,128)(2,1)S(1)}) custom-call(s32[4]{0:T(128)S(1)} %iota_add_fusion.3.index_ref, bf16[1024,128]{1,0:T(8,128)(2,1)S(1)} %bitcast.29, bf16[1024,8192]{1,0:T(8,128)(2,1)S(1)} %copy-done), custom_call_target="tpu_custom_call" | custom-call | flops 536870912 | bytes 4194304 | tf_op jit(solution)/shard_map/pallas_call | solution.py:216
  59.4 3.1 %collective-permute-start.1 = (bf16[128,1024]{1,0:T(8,128)(2,1)S(1)}, bf16[128,1024]{1,0:T(8,128)(2,1)S(1)}, u32[]{:S(2)}, u32[]{:S(2)}) collective-permute-start(bf16[128,1024]{1,0:T(8,128)(2,1)S(1)} %get-tuple-element.15), channel_id=1, source_target_pairs={{0,3},{1,0},{2,1},{3,2},{4,7},{5,4},{6,5},{7,6},{8,11},{9,8},{10,9... | collective-permute-start | bytes 786440 | tf_op jit(solution)/shard_map/ppermute | solution.py:242
  62.5 0.0 collective-permute-start
  62.5 0.0 copy-start.1
  62.5 5.8 %copy-done.1 = bf16[1024,8192]{1,0:T(8,128)(2,1)S(1)} copy-done((bf16[1024,8192]{1,0:T(8,128)(2,1)S(1)}, bf16[1024,8192]{1,0:T(8,128)(2,1)}, u32[]{:S(2)}) %copy-start.1) | copy-done | bytes 16777240
  68.2 2.4 %shard_map.87 = bf16[2,128,1024]{2,1,0:T(8,128)(2,1)S(1)} custom-call(s32[4]{0:T(128)S(1)} %pad_add_fusion.1.index_ref, bf16[128,1024]{1,0:T(8,128)(2,1)S(1)} %get-tuple-element.7.rows_ref, bf16[1024,8192]{1,0:T(8,128)(2,1)S(1)} %copy-done.1), custom_call_target="tpu_custom_call" | custom-call | flops 536870912 | bytes 4194304 | tf_op jit(solution)/shard_map/pallas_call | solution.py:216
  70.7 3.3 %collective-permute-start.3 = (bf16[128,1024]{1,0:T(8,128)(2,1)S(1)}, bf16[128,1024]{1,0:T(8,128)(2,1)S(1)}, u32[]{:S(2)}, u32[]{:S(2)}) collective-permute-start(bf16[128,1024]{1,0:T(8,128)(2,1)S(1)} %get-tuple-element.13), channel_id=1, source_target_pairs={{0,3},{1,0},{2,1},{3,2},{4,7},{5,4},{6,5},{7,6},{8,11},{9,8},{10,9... | collective-permute-start | bytes 786440 | tf_op jit(solution)/shard_map/ppermute | solution.py:246
  74.0 0.0 collective-permute-start.4
  74.0 0.0 collective-permute-done.1.down_ref
  74.0 0.0 collective-permute-done.up_ref
  74.0 2.5 %shard_map.86 = bf16[2,128,1024]{2,1,0:T(8,128)(2,1)S(1)} custom-call(s32[4]{0:T(128)S(1)} %pad_add_fusion.index_ref, bf16[128,1024]{1,0:T(8,128)(2,1)S(1)} %get-tuple-element.7.rows_ref, bf16[1024,8192]{1,0:T(8,128)(2,1)S(1)} %copy-done.1, bf16[128,1024]{1,0:T(8,128)(2,1)S(1)} %collective-permute-done.up_ref, ...), custom_call_target="tpu_custom_call" | custom-call | flops 536870912 | bytes 4194304 | tf_op jit(solution)/shard_map/pallas_call | solution.py:216
  76.5 0.1 collective-permute-start.2
  76.6 3.3 %collective-permute-start.5 = (bf16[128,1024]{1,0:T(8,128)(2,1)S(1)}, bf16[128,1024]{1,0:T(8,128)(2,1)S(1)}, u32[]{:S(2)}, u32[]{:S(2)}) collective-permute-start(bf16[128,1024]{1,0:T(8,128)(2,1)S(1)} %get-tuple-element.12), channel_id=1, source_target_pairs={{0,3},{1,0},{2,1},{3,2},{4,7},{5,4},{6,5},{7,6},{8,11},{9,8},{10,9... | collective-permute-start | bytes 786440 | tf_op jit(solution)/shard_map/ppermute | solution.py:250
  79.9 0.0 copy-start.2
  79.9 5.8 %copy-done.2 = bf16[1024,8192]{1,0:T(8,128)(2,1)S(1)} copy-done((bf16[1024,8192]{1,0:T(8,128)(2,1)S(1)}, bf16[1024,8192]{1,0:T(8,128)(2,1)}, u32[]{:S(2)}) %copy-start.2) | copy-done | bytes 16777240
  85.7 2.4 %shard_map.85 = f32[2,128,1024]{2,1,0:T(8,128)S(1)} custom-call(s32[4]{0:T(128)S(1)} %iota_add_fusion.4.index_ref, bf16[128,1024]{1,0:T(8,128)(2,1)S(1)} %get-tuple-element.7.rows_ref, bf16[1024,8192]{1,0:T(8,128)(2,1)S(1)} %copy-done.2), custom_call_target="tpu_custom_call" | custom-call | flops 536870912 | bytes 4194304 | tf_op jit(solution)/shard_map/pallas_call | solution.py:216
  88.1 0.0 collective-permute-done.3
  88.1 0.0 collective-permute-done.4
  88.1 0.3 collective-permute-done.2
  88.4 0.0 collective-permute-done.5
  88.5 0.3 fusion.5
  88.7 0.8 pad_maximum_fusion
  (7 shorter events, 0.1 us)
Async XLA Ops:
  3.7 25.6 %all-to-all-start = ((bf16[32,128,128]{2,1,0:T(8,128)(2,1)}), bf16[32,128,128]{2,1,0:T(8,128)(2,1)S(1)}, u32[]{:S(2)}, u32[]{:S(2)}) async-start(bf16[32,128,128]{2,1,0:T(8,128)(2,1)} %shard_map.82), calls=%async_computation | async-start | bytes 2097152 | tf_op jit(solution)/shard_map/all_to_all | solution.py:274
  29.5 0.9 %copy-start.3 = (bf16[256,256]{1,0:T(8,128)(2,1)S(1)}, bf16[256,256]{1,0:T(8,128)(2,1)}, u32[]{:S(2)}) copy-start(bf16[256,256]{1,0:T(8,128)(2,1)} %constant.57.clone.low_ref) | copy-start | bytes 393220
  30.4 0.9 %copy-start.4 = (bf16[256,256]{1,0:T(8,128)(2,1)S(1)}, bf16[256,256]{1,0:T(8,128)(2,1)}, u32[]{:S(2)}) copy-start(bf16[256,256]{1,0:T(8,128)(2,1)} %constant.56.clone.high_ref) | copy-start | bytes 393220
  31.3 0.8 copy-start.5
  38.3 12.8 %all-to-all-start.1 = ((bf16[32,32,128]{2,1,0:T(8,128)(2,1)}), bf16[32,32,128]{2,1,0:T(8,128)(2,1)S(1)}, u32[]{:S(2)}, u32[]{:S(2)}) async-start(bf16[32,32,128]{2,1,0:T(8,128)(2,1)} %shard_map.83), calls=%async_computation.1 | async-start | bytes 524288 | tf_op jit(solution)/shard_map/all_to_all | solution.py:290
  51.1 5.8 %copy-start = (bf16[1024,8192]{1,0:T(8,128)(2,1)S(1)}, bf16[1024,8192]{1,0:T(8,128)(2,1)}, u32[]{:S(2)}) copy-start(bf16[1024,8192]{1,0:T(8,128)(2,1)} %weights_ref.7) | copy-start | bytes 50331652
  59.4 14.6 %collective-permute-start.1 = (bf16[128,1024]{1,0:T(8,128)(2,1)S(1)}, bf16[128,1024]{1,0:T(8,128)(2,1)S(1)}, u32[]{:S(2)}, u32[]{:S(2)}) collective-permute-start(bf16[128,1024]{1,0:T(8,128)(2,1)S(1)} %get-tuple-element.15), channel_id=1, source_target_pairs={{0,3},{1,0},{2,1},{3,2},{4,7},{5,4},{6,5},{7,6},{8,11},{9,8},{10,9... | collective-permute-start | bytes 786440 | tf_op jit(solution)/shard_map/ppermute | solution.py:242
  62.5 11.5 %collective-permute-start = (bf16[128,1024]{1,0:T(8,128)(2,1)S(1)}, bf16[128,1024]{1,0:T(8,128)(2,1)S(1)}, u32[]{:S(2)}, u32[]{:S(2)}) collective-permute-start(bf16[128,1024]{1,0:T(8,128)(2,1)S(1)} %get-tuple-element.16), channel_id=1, source_target_pairs={{0,1},{1,2},{2,3},{3,0},{4,5},{5,6},{6,7},{7,4},{8,9},{9,10},{10,1... | collective-permute-start | bytes 786440 | tf_op jit(solution)/shard_map/ppermute | solution.py:241
  62.5 5.8 %copy-start.1 = (bf16[1024,8192]{1,0:T(8,128)(2,1)S(1)}, bf16[1024,8192]{1,0:T(8,128)(2,1)}, u32[]{:S(2)}) copy-start(bf16[1024,8192]{1,0:T(8,128)(2,1)} %weights_ref.7) | copy-start | bytes 50331652
  70.7 17.4 %collective-permute-start.3 = (bf16[128,1024]{1,0:T(8,128)(2,1)S(1)}, bf16[128,1024]{1,0:T(8,128)(2,1)S(1)}, u32[]{:S(2)}, u32[]{:S(2)}) collective-permute-start(bf16[128,1024]{1,0:T(8,128)(2,1)S(1)} %get-tuple-element.13), channel_id=1, source_target_pairs={{0,3},{1,0},{2,1},{3,2},{4,7},{5,4},{6,5},{7,6},{8,11},{9,8},{10,9... | collective-permute-start | bytes 786440 | tf_op jit(solution)/shard_map/ppermute | solution.py:246
  74.0 14.1 %collective-permute-start.4 = (bf16[128,1024]{1,0:T(8,128)(2,1)S(1)}, bf16[128,1024]{1,0:T(8,128)(2,1)S(1)}, u32[]{:S(2)}, u32[]{:S(2)}) collective-permute-start(bf16[128,1024]{1,0:T(8,128)(2,1)S(1)} %get-tuple-element.14), channel_id=1, source_target_pairs={{0,1},{1,2},{2,3},{3,0},{4,5},{5,6},{6,7},{7,4},{8,9},{9,10},{10,1... | collective-permute-start | bytes 786440 | tf_op jit(solution)/shard_map/ppermute | solution.py:245
  76.5 11.9 %collective-permute-start.2 = (bf16[128,1024]{1,0:T(8,128)(2,1)S(1)}, bf16[128,1024]{1,0:T(8,128)(2,1)S(1)}, u32[]{:S(2)}, u32[]{:S(2)}) collective-permute-start(bf16[128,1024]{1,0:T(8,128)(2,1)S(1)} %get-tuple-element.11), channel_id=1, source_target_pairs={{0,1},{1,2},{2,3},{3,0},{4,5},{5,6},{6,7},{7,4},{8,9},{9,10},{10,1... | collective-permute-start | bytes 786440 | tf_op jit(solution)/shard_map/ppermute | solution.py:249
  76.6 11.9 %collective-permute-start.5 = (bf16[128,1024]{1,0:T(8,128)(2,1)S(1)}, bf16[128,1024]{1,0:T(8,128)(2,1)S(1)}, u32[]{:S(2)}, u32[]{:S(2)}) collective-permute-start(bf16[128,1024]{1,0:T(8,128)(2,1)S(1)} %get-tuple-element.12), channel_id=1, source_target_pairs={{0,3},{1,0},{2,1},{3,2},{4,7},{5,4},{6,5},{7,6},{8,11},{9,8},{10,9... | collective-permute-start | bytes 786440 | tf_op jit(solution)/shard_map/ppermute | solution.py:250
  79.9 5.8 %copy-start.2 = (bf16[1024,8192]{1,0:T(8,128)(2,1)S(1)}, bf16[1024,8192]{1,0:T(8,128)(2,1)}, u32[]{:S(2)}) copy-start(bf16[1024,8192]{1,0:T(8,128)(2,1)} %weights_ref.7) | copy-start | bytes 50331652

commit v2 on v1

--- a/solution.py
+++ b/solution.py
@@ -1,4 +1,3 @@
-import functools
 import math
 
 import jax
@@ -10,7 +9,6 @@
 from jax.sharding import PartitionSpec as P
 
 SHORT = 3
-STREAMS = 3
 ROWS = 128
 PARTS = 32
 GROUP = 32
@@ -70,12 +68,42 @@
     return [plus(a, b) for a, b in zip(even, odd)] + [minus(a, b) for a, b in zip(even, odd)]
 
 
-def exchange_kernel(streams_ref, filter_ref, out_ref):
-    groups = out_ref.shape[0]
-    for j in range(STREAMS + 1):
-        block = streams_ref[j].astype(f32) if j < STREAMS else filter_ref[...]
-        turned_block = block.T.astype(bf16).reshape(groups, GROUP, ROWS)
-        out_ref[:, j * GROUP : (j + 1) * GROUP, :] = turned_block
+def exchange_kernel(streams_ref, filter_ref, out_ref, token_ref, rows_ref, taps_ref, sems):
+    copies = [pltpu.make_async_copy(streams_ref.at[i + 1], rows_ref.at[i], sems.at[i]) for i in range(SENT - 1)]
+    copies.append(pltpu.make_async_copy(filter_ref, taps_ref, sems.at[SENT - 1]))
+    for copy in copies:
+        copy.start()
+    token_ref[...] = jnp.zeros_like(token_ref)
+    wide = 8 * GROUP
+    for j, copy in enumerate(copies):
+        copy.wait()
+        for first in range(0, PARTS * GROUP, wide):
+            here = slice(first, first + wide)
+            block = rows_ref[j, :, here] if j < SENT - 1 else taps_ref[:, here].astype(bf16)
+            parts = pl.ds(first // GROUP, wide // GROUP)
+            out_ref[parts, j * GROUP : (j + 1) * GROUP, :] = block.T.reshape(wide // GROUP, GROUP, ROWS)
+
+
+def stage_kernel(*refs):
+    sems = refs[-1]
+    count = sems.shape[0]
+    copies = [
+        pltpu.make_async_copy(source, target, sems.at[i])
+        for i, (source, target) in enumerate(zip(refs[1 : 1 + count], refs[1 + count : -1]))
+    ]
+    for copy in copies:
+        copy.start()
+    for copy in copies:
+        copy.wait()
+
+
+def query_kernel(query_ref, earlier_ref, taps_ref, out_ref):
+    now = query_ref[0].astype(f32)
+    row = lax.broadcasted_iota(jnp.int32, now.shape, 0)
+    last, before_last = earlier_ref[1:2, :], earlier_ref[0:1, :]
+    one = jnp.where(row == 0, last, pltpu.roll(now, 1, 0))
+    two = jnp.where(row == 0, before_last, jnp.where(row == 1, last, pltpu.roll(now, 2, 0)))
+    out_ref[...] = taps_ref[0, 0:1, :] * now + taps_ref[0, 1:2, :] * one + taps_ref[0, 2:3, :] * two
 
 
 def split(value):
@@ -125,10 +153,10 @@
     @pl.loop(0, GROUP // SLAB)
     def _(step):
         offset = pl.multiple_of(step * SLAB, SLAB)
-        for s, (key, value) in enumerate(zip(short(1, offset), short(2, offset))):
+        for s, (key, value) in enumerate(zip(short(0, offset), short(1, offset))):
             gated_ref[s, pl.ds(offset, SLAB), :] = key * value
         forward(0, offset, lambda s: gated_ref[s, pl.ds(offset, SLAB), :])
-        forward(1, offset, lambda s: x_ref[s, rows_of(STREAMS, offset), :].astype(f32))
+        forward(1, offset, lambda s: x_ref[s, rows_of(SENT - 1, offset), :].astype(f32))
 
     def product(high, low):
         total = jnp.dot(low, high_ref[...], preferred_element_type=f32)
@@ -172,112 +200,185 @@
                 conv = real * math.cos(angle) - imag * math.sin(angle) if q else real
                 s = a + 8 * q
                 gated = gated_ref[s, pl.ds(offset, SLAB), :]
-                gated_ref[s, pl.ds(offset, SLAB), :] = conv + skip * gated
-        for s, query in enumerate(short(0, offset)):
-            out_ref[s, pl.ds(offset, SLAB), :] = (query * gated_ref[s, pl.ds(offset, SLAB), :]).astype(bf16)
-
-
-def far_kernel(index_ref, mixed_ref, weights_ref, out_ref, rows_ref):
-    @pl.when(pl.program_id(0) == 0)
-    def _():
-        rows_ref[...] = mixed_ref[...].astype(f32).T.astype(bf16)
-
-    out_ref[0] = jnp.dot(rows_ref[...], weights_ref[...], preferred_element_type=f32).astype(out_ref.dtype)
-
-
-def near_kernel(index_ref, rows_ref, weights_ref, out_ref):
-    out_ref[0] = jnp.dot(rows_ref[...], weights_ref[...], preferred_element_type=f32).astype(out_ref.dtype)
-
-
-def adding_kernel(index_ref, rows_ref, weights_ref, up_ref, down_ref, out_ref):
-    half = pl.num_programs(0) // 2
-    arrived = jnp.where(pl.program_id(0) < half, up_ref[...], down_ref[...]).astype(f32)
-    total = jnp.dot(rows_ref[...], weights_ref[...], preferred_element_type=f32)
-    out_ref[0] = (total + arrived).astype(out_ref.dtype)
-
-
+                out_ref[s, pl.ds(offset, SLAB), :] = (conv + skip * gated).astype(bf16)
+
+
+def fetch(weights_ref, target_ref, sems, blocks):
+    copies = []
+    for i, block in enumerate(blocks):
+        source = weights_ref.at[:, pl.ds(pl.multiple_of(block * WIDE, WIDE), WIDE)]
+        copies.append(pltpu.make_async_copy(source, target_ref.at[:, i * WIDE : (i + 1) * WIDE], sems.at[i]))
+    for copy in copies:
+        copy.start()
+    return copies
+
+
+def part_of(rows_ref, held_ref, i):
+    return jnp.dot(rows_ref[...], held_ref[:, i * WIDE : (i + 1) * WIDE], preferred_element_type=f32)
+
+
+def first_block(me_ref, away):
+    return (me_ref[0] + away) % RING * BLOCKS
+
+
+def far_kernel(me_ref, outer_ref, query_ref, weights_ref, up_ref, down_ref, rows_ref, held_ref, sems):
+    away = first_block(me_ref, 2)
+    copies = fetch(weights_ref, held_ref, sems, [away + i for i in range(BLOCKS)])
+    rows_ref[...] = (query_ref[...] * outer_ref[...].astype(f32).T).astype(bf16)
+    for i, copy in enumerate(copies):
+        copy.wait()
+        out_ref = up_ref if i < HALF else down_ref
+        out_ref[:, i % HALF * WIDE : (i % HALF + 1) * WIDE] = part_of(rows_ref, held_ref, i).astype(bf16)
+
+
+def near_kernel(me_ref, rows_ref, weights_ref, up_ref, down_ref, later_ref, held_ref, sems):
+    above, below = first_block(me_ref, 1), first_block(me_ref, RING - 1)
+    now = [above + HALF + i for i in range(HALF)] + [below + i for i in range(HALF)]
+    later = [above + i for i in range(HALF)] + [below + HALF + i for i in range(HALF)]
+    copies = fetch(weights_ref, held_ref, sems, now)
+    more = fetch(weights_ref, later_ref, sems.at[BLOCKS:], later)
+    for i, copy in enumerate(copies):
+        copy.wait()
+        out_ref = up_ref if i < HALF else down_ref
+        out_ref[:, i % HALF * WIDE : (i % HALF + 1) * WIDE] = part_of(rows_ref, held_ref, i).astype(bf16)
+    for copy in more:
+        copy.wait()
+
+
+def adding_kernel(rows_ref, held_ref, far_up_ref, far_down_ref, up_ref, down_ref):
+    for i in range(BLOCKS):
+        out_ref, arrived_ref = (up_ref, far_up_ref) if i < HALF else (down_ref, far_down_ref)
+        here = slice(i % HALF * WIDE, (i % HALF + 1) * WIDE)
+        out_ref[:, here] = (part_of(rows_ref, held_ref, i) + arrived_ref[:, here].astype(f32)).astype(bf16)
+
+
+def own_kernel(me_ref, rows_ref, near_up_ref, near_down_ref, weights_ref, out_ref, held_ref, sems):
+    mine = first_block(me_ref, 0)
+    copies = fetch(weights_ref, held_ref, sems, [mine + i for i in range(BLOCKS)])
+    for i, copy in enumerate(copies):
+        copy.wait()
+        arrived_ref = near_down_ref if i < HALF else near_up_ref
+        here = slice(i % HALF * WIDE, (i % HALF + 1) * WIDE)
+        out_ref[:, i * WIDE : (i + 1) * WIDE] = part_of(rows_ref, held_ref, i) + arrived_ref[:, here].astype(f32)
+
+
+def last_kernel(own_ref, both_up_ref, both_down_ref, out_ref):
+    middle = out_ref.shape[1] // 2
+    for here, arrived_ref in ((slice(0, middle), both_up_ref), (slice(middle, 2 * middle), both_down_ref)):
+        out_ref[:, here] = (own_ref[:, here] + arrived_ref[...].astype(f32)).astype(bf16)
+
+
+RING = 4
 WIDE = 512
-
-
-def share(kernel, index, rows, weights, dtype, arrived=(), first=False):
-    count = index.shape[0]
-    depth = weights.shape[0]
-    half = count // 2
-    row_spec = pl.BlockSpec(rows.shape, lambda i, index: (0, 0))
-    in_specs = [row_spec, pl.BlockSpec((depth, WIDE), lambda i, index: (0, index[i]))]
-    if arrived:
-        in_specs.append(pl.BlockSpec((ROWS, WIDE), lambda i, index: (0, jnp.minimum(i, half - 1))))
-        in_specs.append(pl.BlockSpec((ROWS, WIDE), lambda i, index: (0, jnp.maximum(i - half, 0))))
-    out_shape = [jax.ShapeDtypeStruct((2, ROWS, half * WIDE), dtype)]
-    out_specs = [pl.BlockSpec((1, ROWS, WIDE), lambda i, index: (i // half, 0, i % half))]
-    if first:
-        out_shape.append(jax.ShapeDtypeStruct((ROWS, depth), bf16))
-        out_specs.append(pl.BlockSpec((ROWS, depth), lambda i, index: (0, 0)))
+BLOCKS = 4
+HALF = BLOCKS // 2
+SENT = 3
+VMEM = pl.BlockSpec(memory_space=pltpu.VMEM)
+SMEM = pl.BlockSpec(memory_space=pltpu.SMEM)
+HBM = pl.BlockSpec(memory_space=pltpu.HBM)
+
+
+def share(kernel, arrays, outs, fetched=0):
+    depth = arrays[-1].shape[0]
+    arrays, specs = list(arrays), [SMEM if array.ndim == 1 else VMEM for array in arrays]
+    scratch = []
+    if fetched:
+        arrays[-1] = pltpu.with_memory_space_constraint(arrays[-1], pltpu.HBM)
+        specs[-1] = HBM
+        scratch = [pltpu.VMEM((depth, BLOCKS * WIDE), bf16), pltpu.SemaphoreType.DMA((fetched,))]
     return pl.pallas_call(
         kernel,
-        grid_spec=pltpu.PrefetchScalarGridSpec(
-            num_scalar_prefetch=1, grid=(count,), in_specs=in_specs, out_specs=out_specs
-        ),
-        out_shape=out_shape,
-        cost_estimate=pl.CostEstimate(
-            flops=2 * ROWS * depth * count * WIDE, bytes_accessed=2 * depth * count * WIDE, transcendentals=0
-        ),
-        compiler_params=pltpu.CompilerParams(vmem_limit_bytes=32 * 2**20),
-    )(index, rows, weights, *arrived)
-
-
-def project(mixed, weights):
-    ring = lax.axis_size("ch")
-    me = lax.axis_index("ch")
-    up = [(i, (i + 1) % ring) for i in range(ring)]
-    down = [(i, (i - 1) % ring) for i in range(ring)]
-    blocks = weights.shape[1] // ring // WIDE
-    half = blocks // 2
-
-    def numbers(away, start, stop):
-        return (me + away) % ring * blocks + jnp.arange(start, stop, dtype=jnp.int32)
-
-    far, rows = share(far_kernel, numbers(2, 0, blocks), mixed, weights, bf16, first=True)
-    far_up = lax.ppermute(far[0], "ch", up)
-    far_down = lax.ppermute(far[1], "ch", down)
-    index = jnp.concatenate([numbers(1, half, blocks), numbers(-1, 0, half)])
-    (near,) = share(near_kernel, index, rows, weights, bf16)
-    near_up = lax.ppermute(near[0], "ch", up)
-    near_down = lax.ppermute(near[1], "ch", down)
-    index = jnp.concatenate([numbers(1, 0, half), numbers(-1, half, blocks)])
-    (both,) = share(adding_kernel, index, rows, weights, bf16, arrived=(far_up, far_down))
-    both_up = lax.ppermute(both[0], "ch", up)
-    both_down = lax.ppermute(both[1], "ch", down)
-    (own,) = share(near_kernel, numbers(0, 0, blocks), rows, weights, f32)
-    left = own[0] + both_up.astype(f32) + near_down.astype(f32)
-    right = own[1] + near_up.astype(f32) + both_down.astype(f32)
-    return jnp.concatenate([left, right], axis=1).astype(bf16)
+        in_specs=specs,
+        out_specs=[VMEM] * len(outs),
+        out_shape=[pltpu.VMEM(shape, dtype) for shape, dtype in outs],
+        scratch_shapes=scratch,
+        cost_estimate=pl.CostEstimate(flops=2**32, bytes_accessed=2**22, transcendentals=0),
+        compiler_params=pltpu.CompilerParams(vmem_limit_bytes=16 * 2**20),
+    )(*arrays)
+
+
+def project(outer, query, weights):
+    me = lax.axis_index("ch").astype(jnp.int32).reshape(1)
+    up = [(i, (i + 1) % RING) for i in range(RING)]
+    down = [(i, (i - 1) % RING) for i in range(RING)]
+    half = ((ROWS, HALF * WIDE), bf16)
+    held = ((weights.shape[0], BLOCKS * WIDE), bf16)
+    far_up, far_down, rows = share(
+        far_kernel, (me, outer, query, weights), [half, half, (query.shape, bf16)], BLOCKS
+    )
+    far_up = lax.ppermute(far_up, "ch", up)
+    far_down = lax.ppermute(far_down, "ch", down)
+    near_up, near_down, later = share(near_kernel, (me, rows, weights), [half, half, held], 2 * BLOCKS)
+    near_up = lax.ppermute(near_up, "ch", up)
+    near_down = lax.ppermute(near_down, "ch", down)
+    both_up, both_down = share(adding_kernel, (rows, later, far_up, far_down), [half, half])
+    both_up = lax.ppermute(both_up, "ch", up)
+    both_down = lax.ppermute(both_down, "ch", down)
+    (own,) = share(
+        own_kernel, (me, rows, near_up, near_down, weights), [((ROWS, BLOCKS * WIDE), f32)], BLOCKS
+    )
+    return pl.pallas_call(
+        last_kernel,
+        in_specs=[VMEM] * 3,
+        out_specs=VMEM,
+        out_shape=jax.ShapeDtypeStruct((ROWS, BLOCKS * WIDE), bf16),
+        compiler_params=pltpu.CompilerParams(vmem_limit_bytes=16 * 2**20),
+    )(own, both_up, both_down)
+
+
+def stage(after, *arrays):
+    arrays = [pltpu.with_memory_space_constraint(array, pltpu.HBM) for array in arrays]
+    return pl.pallas_call(
+        stage_kernel,
+        in_specs=[pl.BlockSpec(memory_space=pl.ANY)] + [HBM] * len(arrays),
+        out_specs=[VMEM] * len(arrays),
+        out_shape=[pltpu.VMEM(array.shape, array.dtype) for array in arrays],
+        scratch_shapes=[pltpu.SemaphoreType.DMA((len(arrays),))],
+        compiler_params=pltpu.CompilerParams(vmem_limit_bytes=16 * 2**20),
+    )(after, *arrays)
 
 
 def on_device(streams, short_taps, long_filter, skip_gain, out_weights):
     channels = streams.shape[2]
-    wide = 256
-    packed = pl.pallas_call(
+    packed, token = pl.pallas_call(
         exchange_kernel,
-        grid=(channels // wide,),
+        in_specs=[HBM, HBM],
+        out_specs=[VMEM, VMEM],
+        out_shape=[
+            jax.ShapeDtypeStruct((PARTS, SENT * GROUP, ROWS), bf16),
+            jax.ShapeDtypeStruct((8, ROWS), f32),
+        ],
+        scratch_shapes=[
+            pltpu.VMEM((SENT - 1, ROWS, channels), bf16),
+            pltpu.VMEM((ROWS, channels), f32),
+            pltpu.SemaphoreType.DMA((SENT,)),
+        ],
+        compiler_params=pltpu.CompilerParams(vmem_limit_bytes=8 * 2**20),
+    )(*(pltpu.with_memory_space_constraint(array, pltpu.HBM) for array in (streams, long_filter)))
+    high, low, twists = (jnp.asarray(table) for table in tables())
+    high, low, twists = stage(token, high, low, twists)
+    arrived = lax.all_to_all(packed, "seq", 0, 0, tiled=True)
+    earlier = lax.ppermute(streams[0, ROWS - (SHORT - 1) :], "seq", [(i, i + 1) for i in range(PARTS - 1)])
+    query = pl.pallas_call(
+        query_kernel,
+        grid=(1,),
         in_specs=[
-            pl.BlockSpec((STREAMS, ROWS, wide), lambda i: (0, 0, i)),
-            pl.BlockSpec((ROWS, wide), lambda i: (0, i)),
+            pl.BlockSpec((1, ROWS, channels), lambda i: (0, 0, 0)),
+            pl.BlockSpec((SHORT - 1, channels), lambda i: (0, 0)),
+            pl.BlockSpec(short_taps.shape, lambda i: (0, 0, 0)),
         ],
-        out_specs=pl.BlockSpec((wide // GROUP, (STREAMS + 1) * GROUP, ROWS), lambda i: (i, 0, 0)),
-        out_shape=jax.ShapeDtypeStruct((PARTS, (STREAMS + 1) * GROUP, ROWS), bf16),
-    )(streams, long_filter)
+        out_specs=pl.BlockSpec((ROWS, channels), lambda i: (0, 0)),
+        out_shape=pltpu.VMEM((ROWS, channels), f32),
+        compiler_params=pltpu.CompilerParams(vmem_limit_bytes=8 * 2**20),
+    )(streams, earlier.astype(f32), short_taps)
     first = lax.axis_index("seq") * GROUP
-    taps = lax.dynamic_slice_in_dim(short_taps.reshape(STREAMS * SHORT, channels), first, GROUP, 1)
-    taps = jnp.broadcast_to(taps[:, :, None], (STREAMS * SHORT, GROUP, ROWS))
+    taps = lax.dynamic_slice_in_dim(short_taps[1:].reshape((SENT - 1) * SHORT, channels), first, GROUP, 1)
+    taps = jnp.broadcast_to(taps[:, :, None], ((SENT - 1) * SHORT, GROUP, ROWS))
     skip = jnp.broadcast_to(lax.dynamic_slice_in_dim(skip_gain, first, GROUP, 0)[:, None], (GROUP, ROWS))
-    arrived = lax.all_to_all(packed, "seq", 0, 0, tiled=True)
-    high, low, twists = tables()
-    whole = pl.BlockSpec(memory_space=pltpu.VMEM)
-    mixed = pl.pallas_call(
+    outer = pl.pallas_call(
         conv_kernel,
-        in_specs=[whole] * 6,
-        out_specs=whole,
+        in_specs=[VMEM] * 6,
+        out_specs=VMEM,
         out_shape=jax.ShapeDtypeStruct((PARTS, GROUP, ROWS), bf16),
         scratch_shapes=[
             pltpu.VMEM((PARTS, GROUP, ROWS), f32),
@@ -285,10 +386,10 @@
             pltpu.VMEM((2, 2, PARTS * GROUP, 2 * ROWS), bf16),
             pltpu.VMEM((PARTS * GROUP, 2 * ROWS), f32),
         ],
-        compiler_params=pltpu.CompilerParams(vmem_limit_bytes=32 * 2**20),
-    )(arrived, taps, skip, jnp.asarray(high), jnp.asarray(low), jnp.asarray(twists))
-    mixed = lax.all_to_all(mixed, "seq", 0, 0, tiled=True)
-    return project(mixed.reshape(channels, ROWS), out_weights)
+        compiler_params=pltpu.CompilerParams(vmem_limit_bytes=16 * 2**20),
+    )(arrived, taps, skip, high, low, twists)
+    outer = lax.all_to_all(outer, "seq", 0, 0, tiled=True)
+    return project(outer.reshape(channels, ROWS), query, out_weights)
 
 
 def solution(mesh):

time: 90.2 us -> 69.9 us (0.77)
  local copies, waits for them, and re-layouts: 21.8 us -> 4.44 us
  waiting for transfers between devices: 24.7 us -> 20.9 us
  starting transfers between devices: 21.9 us -> 24.1 us
  other arithmetic: 1.26 us -> 0.01 us
    unnamed x12 -> x4, local copies, waits for them, and re-layouts: 19.9 us -> 1.93 us
    all_to_all x1, waiting for transfers between devices: 8.74 us -> 3.16 us  [on_device(): outer = lax.all_to_all(outer, 'seq', 0, 0, tiled=True)]
    ppermute x6 -> x7, waiting for transfers between devices: 0.35 us -> 5.85 us  [the longest x1 3.08 us: project(): near_up = lax.ppermute(near_up, 'ch', up)]
    all_to_all x1, waiting for transfers between devices: 15.6 us -> 11.9 us  [on_device(): arrived = lax.all_to_all(packed, 'seq', 0, 0, tiled=True)]
    ppermute x6 -> x7, starting transfers between devices: 9.76 us -> 12 us  [the longest x1 2.87 us: project(): near_down = lax.ppermute(near_down, 'ch', down)]
    concatenate x3 -> x0, other arithmetic: 0.98 us -> none  [the longest x1 0.83 us: project(): return jnp.concatenate([left, right], axis=1).astype(bf16)]
    pallas_call x6 -> x9, Pallas kernels: 19.7 us -> 19.7 us  [the longest x4 9.38 us: share(): pl.pallas_call(kernel, in_specs=specs, out_specs=[VMEM] * len(outs), out_...]
  transfers between devices with their start and end apart: 8 -> 9, of which waited for: 3 -> 5; matrix products, arithmetic and copies ran while one was open for 2% -> 3% of each run, Pallas kernels for 8% -> 12%
where the time goes in v2:
time: 69.9 us; the launch traced here: 69.3 us
  starting transfers between devices  24.1 us (34%)
  waiting for transfers between devices  20.9 us (30%)
  Pallas kernels  19.7 us (28%)
  local copies, waits for them, and re-layouts  4.44 us (6%)
    all_to_all x1, waiting for transfers between devices, on_device(): arrived = lax.all_to_all(packed, 'seq', 0, 0, tiled=True)  11.9 us
    pallas_call x4, Pallas kernels, share(): pl.pallas_call(kernel, in_specs=specs, out_specs=[VMEM] * len(outs), out_...  9.38 us
    all_to_all x1, starting transfers between devices, on_device(): arrived = lax.all_to_all(packed, 'seq', 0, 0, tiled=True)  8.26 us
    pallas_call x1, Pallas kernels, on_device(): pl.pallas_call(conv_kernel, in_specs=[VMEM] * 6, out_specs=VMEM, out_shap...  5.93 us
    all_to_all x1, starting transfers between devices, on_device(): outer = lax.all_to_all(outer, 'seq', 0, 0, tiled=True)  3.87 us
    all_to_all x1, waiting for transfers between devices, on_device(): outer = lax.all_to_all(outer, 'seq', 0, 0, tiled=True)  3.16 us
    ppermute x1, waiting for transfers between devices, project(): near_up = lax.ppermute(near_up, 'ch', up)  3.08 us
    ppermute x1, starting transfers between devices, project(): near_down = lax.ppermute(near_down, 'ch', down)  2.87 us
  transfers between devices with their start and end apart: 9, of which 5 were waited for; matrix products, arithmetic and copies ran while one was open for 3% of the time, Pallas kernels for 12%

profile of v2, /device:TPU:0, one launch (start us, length us, event | category | flops | bytes accessed | tf_op | source)
XLA Modules:
  0.0 69.3 jit_solution(1037992597200903516)
XLA Ops:
  0.0 2.2 %shard_map.82 = (bf16[32,96,128]{2,1,0:T(8,128)(2,1)}, f32[8,128]{1,0:T(8,128)S(1)}) custom-call(bf16[3,128,1024]{2,1,0:T(8,128)(2,1)} %query_ref.1, f32[128,1024]{1,0:T(8,128)} %filter_ref.1), custom_call_target="tpu_custom_call" | custom-call | tf_op jit(solution)/shard_map/pallas_call | solution.py:343
  2.3 8.3 %all-to-all-start = ((bf16[32,96,128]{2,1,0:T(8,128)(2,1)}), bf16[32,96,128]{2,1,0:T(8,128)(2,1)S(1)}, u32[]{:S(2)}, u32[]{:S(2)}) async-start(bf16[32,96,128]{2,1,0:T(8,128)(2,1)} %get-tuple-element.18), calls=%async_computation | async-start | bytes 1572864 | tf_op jit(solution)/shard_map/all_to_all | solution.py:360
  10.5 0.8 %slice.6 = f32[2,3,1024]{2,1,0:T(4,128)S(1)} slice(f32[3,3,1024]{2,1,0:T(4,128)} %taps_ref.1), slice={[1:3], [0:3], [0:1024]} | slice | bytes 49152 | tf_op jit(solution)/shard_map/slice | solution.py:375
  11.3 0.8 %dynamic_slice.7 = f32[32]{0:T(128)S(1)} dynamic-slice(f32[1024]{0:T(1024)} %param.11, s32[]{:T(128)S(6)} %select_n.4), dynamic_slice_sizes={32} | dynamic-slice | bytes 260 | tf_op jit(solution)/shard_map/dynamic_slice | solution.py:377
  12.1 1.0 %shard_map.83 = (bf16[256,256]{1,0:T(8,128)(2,1)S(1)}, bf16[256,256]{1,0:T(8,128)(2,1)S(1)}, f32[32,2,128]{2,1,0:T(2,128)S(1)}) custom-call(f32[8,128]{1,0:T(8,128)S(1)} %get-tuple-element.19.refs_0_, bf16[256,256]{1,0:T(8,128)(2,1)} %constant.21.clone.refs_1_, bf16[256,256]{1,0:T(8,128)(2,1)} %constant.22.clone.refs_2_, f32[32,2,128]{2,1,0:T(2,128)} %constant.23.clone.refs_3_), custom_call_target="tpu_custom_call" | custom-call | tf_op jit(solution)/shard_map/pallas_call | solution.py:331
  13.1 0.1 constant_dynamic-slice_fusion
  13.2 11.9 %all-to-all-done.x_ref = bf16[32,96,128]{2,1,0:T(8,128)(2,1)S(1)} async-done(((bf16[32,96,128]{2,1,0:T(8,128)(2,1)}), bf16[32,96,128]{2,1,0:T(8,128)(2,1)S(1)}, u32[]{:S(2)}, u32[]{:S(2)}) %all-to-all-start) | async-done | bytes 786464 | tf_op jit(solution)/shard_map/all_to_all | solution.py:360
  25.1 0.1 broadcast_in_dim.5.skip_ref
  25.1 0.1 broadcast_in_dim.4.taps_ref
  25.2 5.9 %shard_map.84 = bf16[32,32,128]{2,1,0:T(8,128)(2,1)} custom-call(bf16[32,96,128]{2,1,0:T(8,128)(2,1)S(1)} %all-to-all-done.x_ref, f32[6,32,128]{2,1,0:T(8,128)S(1)} %broadcast_in_dim.4.taps_ref, f32[32,128]{1,0:T(8,128)S(1)} %broadcast_in_dim.5.skip_ref, bf16[256,256]{1,0:T(8,128)(2,1)S(1)} %get-tuple-element.20.high_ref, ...), custom_call_target="tpu_custom_call" | custom-call | tf_op jit(solution)/shard_map/pallas_call | solution.py:378
  31.2 3.9 %all-to-all-start.1 = ((bf16[32,32,128]{2,1,0:T(8,128)(2,1)}), bf16[32,32,128]{2,1,0:T(8,128)(2,1)S(1)}, u32[]{:S(2)}, u32[]{:S(2)}) async-start(bf16[32,32,128]{2,1,0:T(8,128)(2,1)} %shard_map.84), calls=%async_computation.1 | async-start | bytes 524288 | tf_op jit(solution)/shard_map/all_to_all | solution.py:391
  35.0 0.7 %slice_bitcast_fusion = bf16[2,1024]{1,0:T(2,128)(2,1)S(1)} fusion(bf16[3,128,1024]{2,1,0:T(8,128)(2,1)} %query_ref.1), kind=kLoop, calls=%fused_computation | loop fusion | bytes 8192 | tf_op jit(solution)/shard_map/squeeze | solution.py:361
  35.8 2.1 %collective-permute-start = (bf16[2,1024]{1,0:T(2,128)(2,1)S(1)}, bf16[2,1024]{1,0:T(2,128)(2,1)S(1)}, u32[]{:S(2)}, u32[]{:S(2)}) collective-permute-start(bf16[2,1024]{1,0:T(2,128)(2,1)S(1)} %slice_bitcast_fusion), channel_id=1, source_target_pairs={{0,4},{4,8},{8,12},{12,16},{16,20},{20,24},{24,28},{28,32},{32,36}... | collective-permute-start | bytes 12296 | tf_op jit(solution)/shard_map/ppermute | solution.py:361
  37.8 0.8 %collective-permute-done = bf16[2,1024]{1,0:T(2,128)(2,1)S(1)} collective-permute-done((bf16[2,1024]{1,0:T(2,128)(2,1)S(1)}, bf16[2,1024]{1,0:T(2,128)(2,1)S(1)}, u32[]{:S(2)}, u32[]{:S(2)}) %collective-permute-start) | collective-permute-done | bytes 4128 | tf_op jit(solution)/shard_map/ppermute | solution.py:361
  38.6 0.0 copy-start
  38.6 1.1 %copy-done = bf16[3,128,1024]{2,1,0:T(8,128)(2,1)S(1)} copy-done((bf16[3,128,1024]{2,1,0:T(8,128)(2,1)S(1)}, bf16[3,128,1024]{2,1,0:T(8,128)(2,1)}, u32[]{:S(2)}) %copy-start) | copy-done | bytes 786456
  39.8 0.0 copy-start.1
  39.8 0.8 %copy-done.1 = f32[3,3,1024]{2,1,0:T(4,128)S(1)} copy-done((f32[3,3,1024]{2,1,0:T(4,128)S(1)}, f32[3,3,1024]{2,1,0:T(4,128)}, u32[]{:S(2)}) %copy-start.1) | copy-done | bytes 36888
  40.6 0.2 shard_map.85.query_ref
  40.8 3.2 %all-to-all-done.1 = bf16[32,32,128]{2,1,0:T(8,128)(2,1)S(1)} async-done(((bf16[32,32,128]{2,1,0:T(8,128)(2,1)}), bf16[32,32,128]{2,1,0:T(8,128)(2,1)S(1)}, u32[]{:S(2)}, u32[]{:S(2)}) %all-to-all-start.1) | async-done | bytes 262176 | tf_op jit(solution)/shard_map/all_to_all | solution.py:391
  43.9 2.6 %shard_map.86 = (bf16[128,1024]{1,0:T(8,128)(2,1)S(1)}, bf16[128,1024]{1,0:T(8,128)(2,1)S(1)}, bf16[128,1024]{1,0:T(8,128)(2,1)S(1)}) custom-call(s32[1]{0:T(128)} %bitcast.me_ref, bf16[1024,128]{1,0:T(8,128)(2,1)S(1)} %bitcast.4, f32[128,1024]{1,0:T(8,128)S(1)} %shard_map.85.query_ref, bf16[1024,8192]{1,0:T(8,128)(2,1)} %weights_ref.5), custom_call_target="tpu_custom_call" | custom-call | flops 4294967296 | bytes 4194304 | tf_op jit(solution)/shard_map/pallas_call | solution.py:289
  46.5 1.6 %collective-permute-start.3 = (bf16[128,1024]{1,0:T(8,128)(2,1)S(1)}, bf16[128,1024]{1,0:T(8,128)(2,1)S(1)}, u32[]{:S(2)}, u32[]{:S(2)}) collective-permute-start(bf16[128,1024]{1,0:T(8,128)(2,1)S(1)} %get-tuple-element.27), channel_id=1, source_target_pairs={{0,1},{1,2},{2,3},{3,0},{4,5},{5,6},{6,7},{7,4},{8,9},{9,10},{10,1... | collective-permute-start | bytes 786440 | tf_op jit(solution)/shard_map/ppermute | solution.py:309
  48.2 1.7 %collective-permute-start.4 = (bf16[128,1024]{1,0:T(8,128)(2,1)S(1)}, bf16[128,1024]{1,0:T(8,128)(2,1)S(1)}, u32[]{:S(2)}, u32[]{:S(2)}) collective-permute-start(bf16[128,1024]{1,0:T(8,128)(2,1)S(1)} %get-tuple-element.28), channel_id=1, source_target_pairs={{0,3},{1,0},{2,1},{3,2},{4,7},{5,4},{6,5},{7,6},{8,11},{9,8},{10,9... | collective-permute-start | bytes 786440 | tf_op jit(solution)/shard_map/ppermute | solution.py:310
  49.8 3.5 %shard_map.87 = (bf16[128,1024]{1,0:T(8,128)(2,1)S(1)}, bf16[128,1024]{1,0:T(8,128)(2,1)S(1)}, bf16[1024,2048]{1,0:T(8,128)(2,1)S(1)}) custom-call(s32[1]{0:T(128)} %bitcast.me_ref, bf16[128,1024]{1,0:T(8,128)(2,1)S(1)} %get-tuple-element.23.rows_ref, bf16[1024,8192]{1,0:T(8,128)(2,1)} %weights_ref.5), custom_call_target="tpu_custom_call" | custom-call | flops 4294967296 | bytes 4194304 | tf_op jit(solution)/shard_map/pallas_call | solution.py:289
  53.4 0.4 collective-permute-start.1
  53.8 2.9 %collective-permute-start.2 = (bf16[128,1024]{1,0:T(8,128)(2,1)S(1)}, bf16[128,1024]{1,0:T(8,128)(2,1)S(1)}, u32[]{:S(2)}, u32[]{:S(2)}) collective-permute-start(bf16[128,1024]{1,0:T(8,128)(2,1)S(1)} %get-tuple-element.25), channel_id=1, source_target_pairs={{0,3},{1,0},{2,1},{3,2},{4,7},{5,4},{6,5},{7,6},{8,11},{9,8},{10,9... | collective-permute-start | bytes 786440 | tf_op jit(solution)/shard_map/ppermute | solution.py:313
  56.7 0.0 collective-permute-done.3.far_up_ref
  56.7 0.0 collective-permute-done.4.far_down_ref
  56.7 0.7 %shard_map.89 = (bf16[128,1024]{1,0:T(8,128)(2,1)S(1)}, bf16[128,1024]{1,0:T(8,128)(2,1)S(1)}) custom-call(bf16[128,1024]{1,0:T(8,128)(2,1)S(1)} %get-tuple-element.23.rows_ref, bf16[1024,2048]{1,0:T(8,128)(2,1)S(1)} %get-tuple-element.26.held_ref, bf16[128,1024]{1,0:T(8,128)(2,1)S(1)} %collective-permute-done.3.far_up_ref, ...), custom_call_target="tpu_custom_call" | custom-call | flops 4294967296 | bytes 4194304 | tf_op jit(solution)/shard_map/pallas_call | solution.py:289
  57.5 1.8 %collective-permute-start.5 = (bf16[128,1024]{1,0:T(8,128)(2,1)S(1)}, bf16[128,1024]{1,0:T(8,128)(2,1)S(1)}, u32[]{:S(2)}, u32[]{:S(2)}) collective-permute-start(bf16[128,1024]{1,0:T(8,128)(2,1)S(1)} %get-tuple-element.29), channel_id=1, source_target_pairs={{0,1},{1,2},{2,3},{3,0},{4,5},{5,6},{6,7},{7,4},{8,9},{9,10},{10,1... | collective-permute-start | bytes 786440 | tf_op jit(solution)/shard_map/ppermute | solution.py:315
  59.2 1.5 %collective-permute-start.6 = (bf16[128,1024]{1,0:T(8,128)(2,1)S(1)}, bf16[128,1024]{1,0:T(8,128)(2,1)S(1)}, u32[]{:S(2)}, u32[]{:S(2)}) collective-permute-start(bf16[128,1024]{1,0:T(8,128)(2,1)S(1)} %get-tuple-element.30), channel_id=1, source_target_pairs={{0,3},{1,0},{2,1},{3,2},{4,7},{5,4},{6,5},{7,6},{8,11},{9,8},{10,9... | collective-permute-start | bytes 786440 | tf_op jit(solution)/shard_map/ppermute | solution.py:316
  60.8 3.1 %collective-permute-done.1.near_up_ref = bf16[128,1024]{1,0:T(8,128)(2,1)S(1)} collective-permute-done((bf16[128,1024]{1,0:T(8,128)(2,1)S(1)}, bf16[128,1024]{1,0:T(8,128)(2,1)S(1)}, u32[]{:S(2)}, u32[]{:S(2)}) %collective-permute-start.1) | collective-permute-done | bytes 262176 | tf_op jit(solution)/shard_map/ppermute | solution.py:312
  63.8 0.0 collective-permute-done.2.near_down_ref
  63.9 2.5 %shard_map.88.own_ref = f32[128,2048]{1,0:T(8,128)S(1)} custom-call(s32[1]{0:T(128)} %bitcast.me_ref, bf16[128,1024]{1,0:T(8,128)(2,1)S(1)} %get-tuple-element.23.rows_ref, bf16[128,1024]{1,0:T(8,128)(2,1)S(1)} %collective-permute-done.1.near_up_ref, bf16[128,1024]{1,0:T(8,128)(2,1)S(1)} %collective-permute-done.2.near_down_ref, bf16[1024,8192]{1,0:T(8,128)(2,1)} %weights_ref.5), custom_call_target="tpu_custom_call" | custom-call | flops 4294967296 | bytes 4194304 | tf_op jit(solution)/shard_map/pallas_call | solution.py:289
  66.4 1.9 %collective-permute-done.5.both_up_ref = bf16[128,1024]{1,0:T(8,128)(2,1)S(1)} collective-permute-done((bf16[128,1024]{1,0:T(8,128)(2,1)S(1)}, bf16[128,1024]{1,0:T(8,128)(2,1)S(1)}, u32[]{:S(2)}, u32[]{:S(2)}) %collective-permute-start.5) | collective-permute-done | bytes 262176 | tf_op jit(solution)/shard_map/ppermute | solution.py:315
  68.3 0.0 collective-permute-done.6.both_down_ref
  68.3 0.9 %shard_map.90 = bf16[128,2048]{1,0:T(8,128)(2,1)} custom-call(f32[128,2048]{1,0:T(8,128)S(1)} %shard_map.88.own_ref, bf16[128,1024]{1,0:T(8,128)(2,1)S(1)} %collective-permute-done.5.both_up_ref, bf16[128,1024]{1,0:T(8,128)(2,1)S(1)} %collective-permute-done.6.both_down_ref), custom_call_target="tpu_custom_call" | custom-call | tf_op jit(solution)/shard_map/pallas_call | solution.py:320
  (2 shorter events, 0.0 us)
Async XLA Ops:
  2.3 22.8 %all-to-all-start = ((bf16[32,96,128]{2,1,0:T(8,128)(2,1)}), bf16[32,96,128]{2,1,0:T(8,128)(2,1)S(1)}, u32[]{:S(2)}, u32[]{:S(2)}) async-start(bf16[32,96,128]{2,1,0:T(8,128)(2,1)} %get-tuple-element.18), calls=%async_computation | async-start | bytes 1572864 | tf_op jit(solution)/shard_map/all_to_all | solution.py:360
  31.2 12.8 %all-to-all-start.1 = ((bf16[32,32,128]{2,1,0:T(8,128)(2,1)}), bf16[32,32,128]{2,1,0:T(8,128)(2,1)S(1)}, u32[]{:S(2)}, u32[]{:S(2)}) async-start(bf16[32,32,128]{2,1,0:T(8,128)(2,1)} %shard_map.84), calls=%async_computation.1 | async-start | bytes 524288 | tf_op jit(solution)/shard_map/all_to_all | solution.py:391
  35.8 2.9 %collective-permute-start = (bf16[2,1024]{1,0:T(2,128)(2,1)S(1)}, bf16[2,1024]{1,0:T(2,128)(2,1)S(1)}, u32[]{:S(2)}, u32[]{:S(2)}) collective-permute-start(bf16[2,1024]{1,0:T(2,128)(2,1)S(1)} %slice_bitcast_fusion), channel_id=1, source_target_pairs={{0,4},{4,8},{8,12},{12,16},{16,20},{20,24},{24,28},{28,32},{32,36}... | collective-permute-start | bytes 12296 | tf_op jit(solution)/shard_map/ppermute | solution.py:361
  38.6 1.1 %copy-start = (bf16[3,128,1024]{2,1,0:T(8,128)(2,1)S(1)}, bf16[3,128,1024]{2,1,0:T(8,128)(2,1)}, u32[]{:S(2)}) copy-start(bf16[3,128,1024]{2,1,0:T(8,128)(2,1)} %query_ref.1) | copy-start | bytes 2359300
  39.8 0.8 %copy-start.1 = (f32[3,3,1024]{2,1,0:T(4,128)S(1)}, f32[3,3,1024]{2,1,0:T(4,128)}, u32[]{:S(2)}) copy-start(f32[3,3,1024]{2,1,0:T(4,128)} %taps_ref.1) | copy-start | bytes 110596
  46.5 10.2 %collective-permute-start.3 = (bf16[128,1024]{1,0:T(8,128)(2,1)S(1)}, bf16[128,1024]{1,0:T(8,128)(2,1)S(1)}, u32[]{:S(2)}, u32[]{:S(2)}) collective-permute-start(bf16[128,1024]{1,0:T(8,128)(2,1)S(1)} %get-tuple-element.27), channel_id=1, source_target_pairs={{0,1},{1,2},{2,3},{3,0},{4,5},{5,6},{6,7},{7,4},{8,9},{9,10},{10,1... | collective-permute-start | bytes 786440 | tf_op jit(solution)/shard_map/ppermute | solution.py:309
  48.2 8.5 %collective-permute-start.4 = (bf16[128,1024]{1,0:T(8,128)(2,1)S(1)}, bf16[128,1024]{1,0:T(8,128)(2,1)S(1)}, u32[]{:S(2)}, u32[]{:S(2)}) collective-permute-start(bf16[128,1024]{1,0:T(8,128)(2,1)S(1)} %get-tuple-element.28), channel_id=1, source_target_pairs={{0,3},{1,0},{2,1},{3,2},{4,7},{5,4},{6,5},{7,6},{8,11},{9,8},{10,9... | collective-permute-start | bytes 786440 | tf_op jit(solution)/shard_map/ppermute | solution.py:310
  53.4 10.5 %collective-permute-start.1 = (bf16[128,1024]{1,0:T(8,128)(2,1)S(1)}, bf16[128,1024]{1,0:T(8,128)(2,1)S(1)}, u32[]{:S(2)}, u32[]{:S(2)}) collective-permute-start(bf16[128,1024]{1,0:T(8,128)(2,1)S(1)} %get-tuple-element.24), channel_id=1, source_target_pairs={{0,1},{1,2},{2,3},{3,0},{4,5},{5,6},{6,7},{7,4},{8,9},{9,10},{10,1... | collective-permute-start | bytes 786440 | tf_op jit(solution)/shard_map/ppermute | solution.py:312
  53.8 10.0 %collective-permute-start.2 = (bf16[128,1024]{1,0:T(8,128)(2,1)S(1)}, bf16[128,1024]{1,0:T(8,128)(2,1)S(1)}, u32[]{:S(2)}, u32[]{:S(2)}) collective-permute-start(bf16[128,1024]{1,0:T(8,128)(2,1)S(1)} %get-tuple-element.25), channel_id=1, source_target_pairs={{0,3},{1,0},{2,1},{3,2},{4,7},{5,4},{6,5},{7,6},{8,11},{9,8},{10,9... | collective-permute-start | bytes 786440 | tf_op jit(solution)/shard_map/ppermute | solution.py:313
  57.5 10.9 %collective-permute-start.5 = (bf16[128,1024]{1,0:T(8,128)(2,1)S(1)}, bf16[128,1024]{1,0:T(8,128)(2,1)S(1)}, u32[]{:S(2)}, u32[]{:S(2)}) collective-permute-start(bf16[128,1024]{1,0:T(8,128)(2,1)S(1)} %get-tuple-element.29), channel_id=1, source_target_pairs={{0,1},{1,2},{2,3},{3,0},{4,5},{5,6},{6,7},{7,4},{8,9},{9,10},{10,1... | collective-permute-start | bytes 786440 | tf_op jit(solution)/shard_map/ppermute | solution.py:315
  59.2 9.1 %collective-permute-start.6 = (bf16[128,1024]{1,0:T(8,128)(2,1)S(1)}, bf16[128,1024]{1,0:T(8,128)(2,1)S(1)}, u32[]{:S(2)}, u32[]{:S(2)}) collective-permute-start(bf16[128,1024]{1,0:T(8,128)(2,1)S(1)} %get-tuple-element.30), channel_id=1, source_target_pairs={{0,3},{1,0},{2,1},{3,2},{4,7},{5,4},{6,5},{7,6},{8,11},{9,8},{10,9... | collective-permute-start | bytes 786440 | tf_op jit(solution)/shard_map/ppermute | solution.py:316

commit v3 on v2

v3 whole, which is shorter than its diff:
```python
import functools
import math

import jax
import jax.numpy as jnp
import numpy as np
from jax import lax
from jax.experimental import pallas as pl
from jax.experimental.pallas import tpu as pltpu
from jax.sharding import PartitionSpec as P

SHORT = 3
ROWS = 128
PARTS = 32
GROUP = 32
SLAB = 16
POINTS = PARTS * ROWS
f32 = jnp.float32
bf16 = jnp.bfloat16


def tables():
    r = np.arange(ROWS)
    angle = 2.0 * np.pi * (np.outer(r, r) % ROWS) / ROWS
    cosine, sine = np.cos(angle), np.sin(angle)
    matrix = np.block([[cosine, -sine], [sine, cosine]])
    high = matrix.astype(np.float32).astype(bf16)
    low = (matrix - high.astype(np.float64)).astype(np.float32).astype(bf16)
    j = np.arange(PARTS)
    twist = 2.0 * np.pi * np.outer(4 * j + 1, r) / (4 * POINTS)
    twists = np.stack([np.cos(twist), np.sin(twist)], axis=1).astype(np.float32)
    return high, low, twists


def turned(value, turns):
    real, imag = value
    eighth = turns * 8 % 8
    if eighth == 0:
        return real, imag
    if eighth == 2:
        return -imag, real
    if eighth == 4:
        return -real, -imag
    if eighth == 6:
        return imag, -real
    if eighth in (1, 3, 5, 7):
        half = math.sqrt(0.5)
        total, apart = (real + imag) * half, (real - imag) * half
        return {1: (apart, total), 3: (-total, apart), 5: (-apart, -total), 7: (total, -apart)}[int(eighth)]
    c, s = math.cos(2.0 * math.pi * turns), math.sin(2.0 * math.pi * turns)
    return real * c - imag * s, real * s + imag * c


def plus(a, b):
    return a[0] + b[0], a[1] + b[1]


def minus(a, b):
    return a[0] - b[0], a[1] - b[1]


def small_transform(values, sign):
    count = len(values)
    if count == 1:
        return values
    even = small_transform(values[0::2], sign)
    odd = small_transform(values[1::2], sign)
    odd = [turned(value, sign * k / count) for k, value in enumerate(odd)]
    return [plus(a, b) for a, b in zip(even, odd)] + [minus(a, b) for a, b in zip(even, odd)]


def exchange_kernel(streams_ref, filter_ref, out_ref, edge_ref, rows_ref, taps_ref, sems):
    copies = [pltpu.make_async_copy(streams_ref.at[i + 1], rows_ref.at[i], sems.at[i]) for i in range(SENT - 1)]
    copies.append(pltpu.make_async_copy(filter_ref, taps_ref, sems.at[SENT - 1]))
    edge = pltpu.make_async_copy(streams_ref.at[0, ROWS - EDGE :], edge_ref, sems.at[SENT])
    for copy in copies:
        copy.start()
    edge.start()
    wide = 8 * GROUP
    for j, copy in enumerate(copies):
        copy.wait()
        for first in range(0, PARTS * GROUP, wide):
            here = slice(first, first + wide)
            block = rows_ref[j, :, here] if j < SENT - 1 else taps_ref[:, here].astype(bf16)
            parts = pl.ds(first // GROUP, wide // GROUP)
            out_ref[parts, j * GROUP : (j + 1) * GROUP, :] = block.T.reshape(wide // GROUP, GROUP, ROWS)
    edge.wait()


def stage_kernel(*refs):
    sems = refs[-1]
    count = sems.shape[0]
    copies = [
        pltpu.make_async_copy(source, target, sems.at[i])
        for i, (source, target) in enumerate(zip(refs[1 : 1 + count], refs[1 + count : -1]))
    ]
    for copy in copies:
        copy.start()
    for copy in copies:
        copy.wait()


def query_kernel(streams_ref, edge_ref, taps_ref, held_ref, out_ref, rows_ref, sem):
    copy = pltpu.make_async_copy(streams_ref.at[0], rows_ref, sem.at[0])
    copy.start()
    copy.wait()
    now = rows_ref[...].astype(f32)
    earlier = edge_ref[...].astype(f32)
    row = lax.broadcasted_iota(jnp.int32, now.shape, 0)
    last, before_last = earlier[EDGE - 1 :, :], earlier[EDGE - 2 : EDGE - 1, :]
    one = jnp.where(row == 0, last, pltpu.roll(now, 1, 0))
    two = jnp.where(row == 0, before_last, jnp.where(row == 1, last, pltpu.roll(now, 2, 0)))
    out_ref[...] = taps_ref[0, 0:1, :] * now + taps_ref[0, 1:2, :] * one + taps_ref[0, 2:3, :] * two


def split(value):
    high = value.astype(bf16)
    return high, (value - high.astype(f32)).astype(bf16)


def conv_kernel(
    me_ref, x_ref, taps_ref, skip_ref, high_ref, low_ref, twists_ref, weights_ref,
    out_ref, held_ref, gated_ref, first_ref, left_ref, back_ref, sems,
):
    copies = fetch(weights_ref, held_ref, sems, 2, me_ref, LEFT)
    lane = lax.broadcasted_iota(jnp.int32, (SLAB, ROWS), 1)

    def rows_of(j, offset):
        return pl.ds(pl.multiple_of(j * GROUP + offset, SLAB), SLAB)

    def short(stream, offset):
        taps = [taps_ref[stream * SHORT + i, pl.ds(offset, SLAB), :] for i in range(SHORT)]
        before = [jnp.zeros((SLAB, ROWS), f32)] * 2
        for s in range(PARTS):
            now = x_ref[s, rows_of(stream, offset), :].astype(f32)
            moved = [pltpu.roll(now, i, 1) for i in (1, 2)]
            total = taps[0] * now
            for i in (1, 2):
                total = total + taps[i] * jnp.where(lane < i, before[i - 1], moved[i - 1])
            before = moved
            yield total

    def forward(slot, offset, load):
        for a in range(8):
            values = []
            for q in range(4):
                value = load(a + 8 * q)
                angle = -2.0 * math.pi * q / 16
                values.append((value * math.cos(angle), value * math.sin(angle)) if q else (value, jnp.zeros_like(value)))
            for m, value in enumerate(small_transform(values, -1)):
                real, imag = turned(value, -a * (4 * m + 1) / 128)
                first_ref[m, a, 0] = real
                first_ref[m, a, 1] = imag
        for m in range(4):
            values = [(first_ref[m, a, 0], first_ref[m, a, 1]) for a in range(8)]
            for p, (real, imag) in enumerate(small_transform(values, -1)):
                j = 4 * p + m
                c, s = twists_ref[j, 0][None, :], twists_ref[j, 1][None, :]
                for half, part in enumerate((real * c + imag * s, imag * c - real * s)):
                    high, low = split(part)
                    left_ref[slot, 0, rows_of(j, offset), half * ROWS : (half + 1) * ROWS] = high
                    left_ref[slot, 1, rows_of(j, offset), half * ROWS : (half + 1) * ROWS] = low

    @pl.loop(0, GROUP // SLAB)
    def _(step):
        offset = pl.multiple_of(step * SLAB, SLAB)
        for s, (key, value) in enumerate(zip(short(0, offset), short(1, offset))):
            gated_ref[s, pl.ds(offset, SLAB), :] = key * value
        forward(0, offset, lambda s: gated_ref[s, pl.ds(offset, SLAB), :])
        forward(1, offset, lambda s: x_ref[s, rows_of(SENT - 1, offset), :].astype(f32))

    matrix = jnp.concatenate([high_ref[...], low_ref[...], high_ref[...]], axis=0)

    def product(high, low):
        return jnp.dot(jnp.concatenate([low, high, high], axis=1), matrix, preferred_element_type=f32)

    block = 512

    for step in range(PARTS * GROUP // block):
        rows = pl.ds(step * block, block)
        signal = product(left_ref[0, 0, rows, :], left_ref[0, 1, rows, :])
        taps = product(left_ref[1, 0, rows, :], left_ref[1, 1, rows, :])
        a, b = signal[:, :ROWS], signal[:, ROWS:]
        c, d = taps[:, :ROWS], taps[:, ROWS:]
        real, imag = split((a * c - b * d) * (1.0 / POINTS)), split((a * d + b * c) * (-1.0 / POINTS))
        high = jnp.concatenate([real[0], imag[0]], axis=1)
        low = jnp.concatenate([real[1], imag[1]], axis=1)
        back_ref[rows, :] = product(high, low)

    @pl.loop(0, GROUP // SLAB)
    def _(step):
        offset = pl.multiple_of(step * SLAB, SLAB)
        for m in range(4):
            values = []
            for p in range(8):
                j = 4 * p + m
                real = back_ref[rows_of(j, offset), :ROWS]
                imag = -back_ref[rows_of(j, offset), ROWS:]
                c, s = twists_ref[j, 0][None, :], twists_ref[j, 1][None, :]
                values.append((real * c - imag * s, real * s + imag * c))
            for a, value in enumerate(small_transform(values, 1)):
                real, imag = turned(value, a * (4 * m + 1) / 128)
                first_ref[m, a, 0] = real
                first_ref[m, a, 1] = imag
        skip = skip_ref[pl.ds(offset, SLAB), :]
        for a in range(8):
            values = [(first_ref[m, a, 0], first_ref[m, a, 1]) for m in range(4)]
            for q, (real, imag) in enumerate(small_transform(values, 1)):
                angle = 2.0 * math.pi * q / 16
                conv = real * math.cos(angle) - imag * math.sin(angle) if q else real
                s = a + 8 * q
                gated = gated_ref[s, pl.ds(offset, SLAB), :]
                out_ref[s, pl.ds(offset, SLAB), :] = (conv + skip * gated).astype(bf16)

    for _, _, copy in copies:
        copy.wait()


def fetch(weights_ref, target_ref, sems, away, me_ref, pieces, first=0):
    columns = (me_ref[0] + away) % RING * WIDE
    copies = []
    for i, (start, stop) in enumerate(pieces):
        source = weights_ref.at[:, pl.ds(pl.multiple_of(columns + start, 128), stop - start)]
        target = target_ref.at[:, start - first : stop - first]
        copies.append((start, stop, pltpu.make_async_copy(source, target, sems.at[i])))
        copies[-1][2].start()
    return copies


def part_of(rows_ref, held_ref, start, stop):
    return jnp.dot(rows_ref[...], held_ref[:, start:stop], preferred_element_type=f32)


def far_kernel(me_ref, outer_ref, query_ref, first_ref, weights_ref, up_ref, down_ref, rows_ref, held_ref, sems):
    copies = fetch(weights_ref, held_ref, sems, 2, me_ref, RIGHT, UP)
    rows_ref[...] = (query_ref[...] * outer_ref[...].T.astype(f32)).astype(bf16)
    for start, stop in LEFT:
        up_ref[:, start:stop] = part_of(rows_ref, first_ref, start, stop).astype(bf16)
    for start, stop, copy in copies:
        copy.wait()
        here = slice(start - UP, stop - UP)
        down_ref[:, here] = part_of(rows_ref, held_ref, start - UP, stop - UP).astype(bf16)


def near_kernel(me_ref, rows_ref, weights_ref, up_ref, down_ref, later_ref, held_ref, sems):
    right = fetch(weights_ref, held_ref, sems, 1, me_ref, RIGHT)
    left = fetch(weights_ref, held_ref, sems.at[len(RIGHT) :], -1, me_ref, LEFT)
    later = fetch(weights_ref, later_ref, sems.at[len(RIGHT) + len(LEFT) :], 1, me_ref, LEFT)
    for start, stop, copy in right:
        copy.wait()
        up_ref[:, start - UP : stop - UP] = part_of(rows_ref, held_ref, start, stop).astype(bf16)
    for start, stop, copy in left:
        copy.wait()
        down_ref[:, start:stop] = part_of(rows_ref, held_ref, start, stop).astype(bf16)
    for _, _, copy in later:
        copy.wait()


def adding_kernel(me_ref, rows_ref, first_ref, far_up_ref, far_down_ref, weights_ref, up_ref, down_ref, held_ref, sems):
    copies = fetch(weights_ref, held_ref, sems, -1, me_ref, RIGHT, UP)
    for start, stop in LEFT:
        total = part_of(rows_ref, first_ref, start, stop)
        up_ref[:, start:stop] = (total + far_up_ref[:, start:stop].astype(f32)).astype(bf16)
    for start, stop, copy in copies:
        copy.wait()
        here = slice(start - UP, stop - UP)
        total = part_of(rows_ref, held_ref, start - UP, stop - UP)
        down_ref[:, here] = (total + far_down_ref[:, here].astype(f32)).astype(bf16)


def own_kernel(me_ref, rows_ref, near_up_ref, near_down_ref, weights_ref, out_ref, held_ref, sems):
    for start, stop, copy in fetch(weights_ref, held_ref, sems, 0, me_ref, LEFT + RIGHT):
        copy.wait()
        arrived = near_down_ref[:, start:stop] if start < UP else near_up_ref[:, start - UP : stop - UP]
        out_ref[:, start:stop] = part_of(rows_ref, held_ref, start, stop) + arrived.astype(f32)


def last_kernel(own_ref, both_up_ref, both_down_ref, out_ref):
    for part, arrived_ref in ((slice(0, UP), both_up_ref), (slice(UP, WIDE), both_down_ref)):
        out_ref[:, part] = (own_ref[:, part] + arrived_ref[...].astype(f32)).astype(bf16)


RING = 4
WIDE = 2048
UP = 1024
LEFT = ((0, 512), (512, UP))
RIGHT = ((UP, 1536), (1536, WIDE))
SENT = 3
EDGE = 16
VMEM = pl.BlockSpec(memory_space=pltpu.VMEM)
SMEM = pl.BlockSpec(memory_space=pltpu.SMEM)
HBM = pl.BlockSpec(memory_space=pltpu.HBM)


def share(kernel, arrays, outs, held):
    return pl.pallas_call(
        kernel,
        in_specs=[SMEM] + [VMEM] * (len(arrays) - 2) + [HBM],
        out_specs=[VMEM] * len(outs),
        out_shape=[pltpu.VMEM(shape, dtype) for shape, dtype in outs],
        scratch_shapes=[
            pltpu.VMEM((arrays[-1].shape[0], held), bf16),
            pltpu.SemaphoreType.DMA((2 * len(LEFT) + len(RIGHT),)),
        ],
        cost_estimate=pl.CostEstimate(flops=2**31, bytes_accessed=2**21, transcendentals=0),
        compiler_params=pltpu.CompilerParams(vmem_limit_bytes=16 * 2**20),
    )(*arrays)


def project(me, outer, query, weights, held):
    up = [(i, (i + 1) % RING) for i in range(RING)]
    down = [(i, (i - 1) % RING) for i in range(RING)]
    left, right = ((ROWS, UP), bf16), ((ROWS, WIDE - UP), bf16)
    far_up, far_down, rows = share(
        far_kernel, (me, outer, query, held, weights), [left, right, (query.shape, bf16)], WIDE - UP
    )
    far_up = lax.ppermute(far_up, "ch", up)
    far_down = lax.ppermute(far_down, "ch", down)
    later = ((weights.shape[0], UP), bf16)
    near_up, near_down, later = share(near_kernel, (me, rows, weights), [right, left, later], WIDE)
    near_up = lax.ppermute(near_up, "ch", up)
    near_down = lax.ppermute(near_down, "ch", down)
    both_up, both_down = share(
        adding_kernel, (me, rows, later, far_up, far_down, weights), [left, right], WIDE - UP
    )
    both_up = lax.ppermute(both_up, "ch", up)
    both_down = lax.ppermute(both_down, "ch", down)
    (own,) = share(own_kernel, (me, rows, near_up, near_down, weights), [((ROWS, WIDE), f32)], WIDE)
    return pl.pallas_call(
        last_kernel,
        in_specs=[VMEM] * 3,
        out_specs=VMEM,
        out_shape=jax.ShapeDtypeStruct((ROWS, WIDE), bf16),
        compiler_params=pltpu.CompilerParams(vmem_limit_bytes=16 * 2**20),
    )(own, both_up, both_down)


def stage(after, *arrays):
    arrays = [pltpu.with_memory_space_constraint(array, pltpu.HBM) for array in arrays]
    return pl.pallas_call(
        stage_kernel,
        in_specs=[pl.BlockSpec(memory_space=pl.ANY)] + [HBM] * len(arrays),
        out_specs=[VMEM] * len(arrays),
        out_shape=[pltpu.VMEM(array.shape, array.dtype) for array in arrays],
        scratch_shapes=[pltpu.SemaphoreType.DMA((len(arrays),))],
        compiler_params=pltpu.CompilerParams(vmem_limit_bytes=16 * 2**20),
    )(after, *arrays)


def convolve(*arrays):
    channels = arrays[-1].shape[0]
    return pl.pallas_call(
        conv_kernel,
        in_specs=[SMEM] + [VMEM] * 6 + [HBM],
        out_specs=[VMEM, VMEM],
        out_shape=[
            pltpu.VMEM((PARTS, GROUP, ROWS), bf16),
            pltpu.VMEM((channels, UP), bf16),
        ],
        scratch_shapes=[
            pltpu.VMEM((PARTS, GROUP, ROWS), f32),
            pltpu.VMEM((4, 8, 2, SLAB, ROWS), f32),
            pltpu.VMEM((2, 2, PARTS * GROUP, 2 * ROWS), bf16),
            pltpu.VMEM((PARTS * GROUP, 2 * ROWS), f32),
            pltpu.SemaphoreType.DMA((len(LEFT),)),
        ],
        compiler_params=pltpu.CompilerParams(vmem_limit_bytes=16 * 2**20),
    )(*arrays)


def on_device(streams, short_taps, long_filter, skip_gain, out_weights):
    channels = streams.shape[2]
    streams = pltpu.with_memory_space_constraint(streams, pltpu.HBM)
    weights = pltpu.with_memory_space_constraint(out_weights, pltpu.HBM)
    me = lax.axis_index("ch").astype(jnp.int32).reshape(1)
    packed, edge = pl.pallas_call(
        exchange_kernel,
        in_specs=[HBM, HBM],
        out_specs=[VMEM, VMEM],
        out_shape=[
            pltpu.VMEM((PARTS, SENT * GROUP, ROWS), bf16),
            pltpu.VMEM((EDGE, channels), bf16),
        ],
        scratch_shapes=[
            pltpu.VMEM((SENT - 1, ROWS, channels), bf16),
            pltpu.VMEM((ROWS, channels), f32),
            pltpu.SemaphoreType.DMA((SENT + 1,)),
        ],
        compiler_params=pltpu.CompilerParams(vmem_limit_bytes=8 * 2**20),
    )(streams, pltpu.with_memory_space_constraint(long_filter, pltpu.HBM))
    high, low, twists = (jnp.asarray(table) for table in tables())
    high, low, twists, short_taps = stage(edge, high, low, twists, short_taps)
    arrived = lax.all_to_all(packed, "seq", 0, 0, tiled=True)
    edge = lax.ppermute(edge, "seq", [(i, i + 1) for i in range(PARTS - 1)])
    first = lax.axis_index("seq") * GROUP
    taps = lax.dynamic_slice_in_dim(short_taps[1:].reshape((SENT - 1) * SHORT, channels), first, GROUP, 1)
    taps = jnp.broadcast_to(taps[:, :, None], ((SENT - 1) * SHORT, GROUP, ROWS))
    skip = jnp.broadcast_to(lax.dynamic_slice_in_dim(skip_gain, first, GROUP, 0)[:, None], (GROUP, ROWS))
    outer, held = convolve(me, arrived, taps, skip, high, low, twists, weights)
    query = pl.pallas_call(
        query_kernel,
        in_specs=[HBM, VMEM, VMEM, VMEM],
        out_specs=VMEM,
        out_shape=pltpu.VMEM((ROWS, channels), f32),
        scratch_shapes=[pltpu.VMEM((ROWS, channels), bf16), pltpu.SemaphoreType.DMA((1,))],
        compiler_params=pltpu.CompilerParams(vmem_limit_bytes=8 * 2**20),
    )(streams, edge, short_taps, held)
    outer = lax.all_to_all(outer, "seq", 0, 0, tiled=True)
    return project(me, outer.reshape(channels, ROWS), query, weights, held)


def solution(mesh):
    return jax.shard_map(
        on_device,
        mesh=mesh,
        in_specs=(
            P(None, "seq", "ch"),
            P(None, None, "ch"),
            P("seq", "ch"),
            P("ch"),
            P("ch", None),
        ),
        out_specs=P("seq", "ch"),
        check_vma=False,
    )
```

time: 69.9 us -> 67.5 us (0.966)
  local copies, waits for them, and re-layouts: 4.44 us -> 1.01 us
  waiting for transfers between devices: 20.9 us -> 21.9 us
    ppermute x1, waiting for transfers between devices: 3.08 us -> 0.01 us  [project(): near_up = lax.ppermute(near_up, 'ch', up)]
    unnamed x4 -> x0, local copies, waits for them, and re-layouts: 1.93 us -> none
    all_to_all x1, waiting for transfers between devices: 3.16 us -> 4.82 us  [on_device(): outer = lax.all_to_all(outer, 'seq', 0, 0, tiled=True)]
    ppermute x1, waiting for transfers between devices: 0.04 us -> 0.99 us  [project(): far_down = lax.ppermute(far_down, 'ch', down)]
    slice x1, local copies, waits for them, and re-layouts: 0.77 us -> 0.01 us  [on_device(): short_taps[1:].reshape((SENT - 1) * SHORT, channels)]
    all_to_all x1, waiting for transfers between devices: 11.9 us -> 12.7 us  [on_device(): arrived = lax.all_to_all(packed, 'seq', 0, 0, tiled=True)]
    squeeze x1 -> x0, local copies, waits for them, and re-layouts: 0.73 us -> none  [on_device(): streams[0, ROWS - (SHORT - 1):]]
  transfers between devices with their start and end apart: 9 -> 9, of which waited for: 5 -> 6; matrix products, arithmetic and copies ran while one was open for 3% -> 1% of each run, Pallas kernels for 12% -> 15%
where the time goes in v3:
time: 67.5 us; the launch traced here: 67.1 us
  starting transfers between devices  24.1 us (36%)
  waiting for transfers between devices  21.9 us (32%)
  Pallas kernels  19.9 us (29%)
  local copies, waits for them, and re-layouts  1.01 us (1%)
    all_to_all x1, waiting for transfers between devices, on_device(): arrived = lax.all_to_all(packed, 'seq', 0, 0, tiled=True)  12.7 us
    pallas_call x4, Pallas kernels, share(): pl.pallas_call(kernel, in_specs=[SMEM] + [VMEM] * (len(arrays) - 2) + [HB...  9.79 us
    all_to_all x1, starting transfers between devices, on_device(): arrived = lax.all_to_all(packed, 'seq', 0, 0, tiled=True)  8.26 us
    all_to_all x1, waiting for transfers between devices, on_device(): outer = lax.all_to_all(outer, 'seq', 0, 0, tiled=True)  4.82 us
    pallas_call x1, Pallas kernels, convolve(): pl.pallas_call(conv_kernel, in_specs=[SMEM] + [VMEM] * 6 + [HBM], out_spe...  4.79 us
    all_to_all x1, starting transfers between devices, on_device(): outer = lax.all_to_all(outer, 'seq', 0, 0, tiled=True)  3.88 us
    ppermute x1, starting transfers between devices, project(): near_down = lax.ppermute(near_down, 'ch', down)  2.87 us
    pallas_call x1, Pallas kernels, on_device(): pl.pallas_call(exchange_kernel, in_specs=[HBM, HBM], out_specs=[VMEM, VME...  2.26 us
  transfers between devices with their start and end apart: 9, of which 6 were waited for; matrix products, arithmetic and copies ran while one was open for 1% of the time, Pallas kernels for 15%

profile of v3, /device:TPU:0, one launch (start us, length us, event | category | flops | bytes accessed | tf_op | source)
XLA Modules:
  0.0 67.1 jit_solution(8107287213246113838)
XLA Ops:
  0.0 2.3 %shard_map.82 = (bf16[32,96,128]{2,1,0:T(8,128)(2,1)}, bf16[16,1024]{1,0:T(8,128)(2,1)S(1)}) custom-call(bf16[3,128,1024]{2,1,0:T(8,128)(2,1)} %streams_ref.3, f32[128,1024]{1,0:T(8,128)} %filter_ref.1), custom_call_target="tpu_custom_call" | custom-call | tf_op jit(solution)/shard_map/pallas_call | solution.py:376
  2.3 8.3 %all-to-all-start = ((bf16[32,96,128]{2,1,0:T(8,128)(2,1)}), bf16[32,96,128]{2,1,0:T(8,128)(2,1)S(1)}, u32[]{:S(2)}, u32[]{:S(2)}) async-start(bf16[32,96,128]{2,1,0:T(8,128)(2,1)} %get-tuple-element.21), calls=%async_computation | async-start | bytes 1572864 | tf_op jit(solution)/shard_map/all_to_all | solution.py:393
  10.5 1.0 %shard_map.83 = (bf16[256,256]{1,0:T(8,128)(2,1)S(1)}, bf16[256,256]{1,0:T(8,128)(2,1)S(1)}, f32[32,2,128]{2,1,0:T(2,128)S(1)}, f32[3,3,1024]{2,1,0:T(4,128)S(1)}) custom-call(bf16[16,1024]{1,0:T(8,128)(2,1)S(1)} %get-tuple-element.22.refs_0_, bf16[256,256]{1,0:T(8,128)(2,1)} %constant.21.clone.refs_1_, bf16[256,256]{1,0:T(8,128)(2,1)} %constant.22.clone.refs_2_, ...), custom_call_target="tpu_custom_call" | custom-call | tf_op jit(solution)/shard_map/pallas_call | solution.py:340
  11.6 0.8 %dynamic_slice.7 = f32[32]{0:T(128)S(1)} dynamic-slice(f32[1024]{0:T(1024)} %param.11, s32[]{:T(128)S(6)} %select_n.4), dynamic_slice_sizes={32} | dynamic-slice | bytes 260 | tf_op jit(solution)/shard_map/dynamic_slice | solution.py:398
  12.4 0.1 constant_dynamic-slice_fusion
  12.4 12.7 %all-to-all-done.x_ref = bf16[32,96,128]{2,1,0:T(8,128)(2,1)S(1)} async-done(((bf16[32,96,128]{2,1,0:T(8,128)(2,1)}), bf16[32,96,128]{2,1,0:T(8,128)(2,1)S(1)}, u32[]{:S(2)}, u32[]{:S(2)}) %all-to-all-start) | async-done | bytes 786464 | tf_op jit(solution)/shard_map/all_to_all | solution.py:393
  25.1 0.1 broadcast_in_dim.5.skip_ref
  25.2 0.1 broadcast_in_dim.4.taps_ref
  25.3 4.8 %shard_map.84 = (bf16[32,32,128]{2,1,0:T(8,128)(2,1)}, bf16[1024,1024]{1,0:T(8,128)(2,1)S(1)}) custom-call(s32[1]{0:T(128)} %bitcast.me_ref, bf16[32,96,128]{2,1,0:T(8,128)(2,1)S(1)} %all-to-all-done.x_ref, f32[6,32,128]{2,1,0:T(8,128)S(1)} %broadcast_in_dim.4.taps_ref, f32[32,128]{1,0:T(8,128)S(1)} %broadcast_in_dim.5.skip_ref, ...), custom_call_target="tpu_custom_call" | custom-call | tf_op jit(solution)/shard_map/pallas_call | solution.py:352
  30.0 3.9 %all-to-all-start.1 = ((bf16[32,32,128]{2,1,0:T(8,128)(2,1)}), bf16[32,32,128]{2,1,0:T(8,128)(2,1)S(1)}, u32[]{:S(2)}, u32[]{:S(2)}) async-start(bf16[32,32,128]{2,1,0:T(8,128)(2,1)} %get-tuple-element.27), calls=%async_computation.1 | async-start | bytes 524288 | tf_op jit(solution)/shard_map/all_to_all | solution.py:408
  33.9 2.1 %collective-permute-start = (bf16[16,1024]{1,0:T(8,128)(2,1)S(1)}, bf16[16,1024]{1,0:T(8,128)(2,1)S(1)}, u32[]{:S(2)}, u32[]{:S(2)}) collective-permute-start(bf16[16,1024]{1,0:T(8,128)(2,1)S(1)} %get-tuple-element.22.refs_0_), channel_id=1, source_target_pairs={{0,4},{4,8},{8,12},{12,16},{16,20},{20,24},{24,28},{28,32},{32,36}... | collective-permute-start | bytes 98312 | tf_op jit(solution)/shard_map/ppermute | solution.py:394
  36.0 0.8 %collective-permute-done.edge_ref = bf16[16,1024]{1,0:T(8,128)(2,1)S(1)} collective-permute-done((bf16[16,1024]{1,0:T(8,128)(2,1)S(1)}, bf16[16,1024]{1,0:T(8,128)(2,1)S(1)}, u32[]{:S(2)}, u32[]{:S(2)}) %collective-permute-start) | collective-permute-done | bytes 32800 | tf_op jit(solution)/shard_map/ppermute | solution.py:394
  36.9 1.2 %shard_map.85.query_ref = f32[128,1024]{1,0:T(8,128)S(1)} custom-call(bf16[3,128,1024]{2,1,0:T(8,128)(2,1)} %streams_ref.3, bf16[16,1024]{1,0:T(8,128)(2,1)S(1)} %collective-permute-done.edge_ref, f32[3,3,1024]{2,1,0:T(4,128)S(1)} %get-tuple-element.23.taps_ref, bf16[1024,1024]{1,0:T(8,128)(2,1)S(1)} %get-tuple-element.28.held_ref.first_ref), custom_call_target="tpu_custom_call" | custom-call | tf_op jit(solution)/shard_map/pallas_call | solution.py:400
  38.0 4.8 %all-to-all-done.1 = bf16[32,32,128]{2,1,0:T(8,128)(2,1)S(1)} async-done(((bf16[32,32,128]{2,1,0:T(8,128)(2,1)}), bf16[32,32,128]{2,1,0:T(8,128)(2,1)S(1)}, u32[]{:S(2)}, u32[]{:S(2)}) %all-to-all-start.1) | async-done | bytes 262176 | tf_op jit(solution)/shard_map/all_to_all | solution.py:408
  42.8 2.1 %shard_map.86 = (bf16[128,1024]{1,0:T(8,128)(2,1)S(1)}, bf16[128,1024]{1,0:T(8,128)(2,1)S(1)}, bf16[128,1024]{1,0:T(8,128)(2,1)S(1)}) custom-call(s32[1]{0:T(128)} %bitcast.me_ref, bf16[1024,128]{1,0:T(8,128)(2,1)S(1)} %bitcast.2, f32[128,1024]{1,0:T(8,128)S(1)} %shard_map.85.query_ref, bf16[1024,1024]{1,0:T(8,128)(2,1)S(1)} %get-tuple-element.28.held_ref.first_ref, ...), custom_call_target="tpu_custom_call" | custom-call | flops 2147483648 | bytes 2097152 | tf_op jit(solution)/shard_map/pallas_call | solution.py:296
  45.0 1.6 %collective-permute-start.3 = (bf16[128,1024]{1,0:T(8,128)(2,1)S(1)}, bf16[128,1024]{1,0:T(8,128)(2,1)S(1)}, u32[]{:S(2)}, u32[]{:S(2)}) collective-permute-start(bf16[128,1024]{1,0:T(8,128)(2,1)S(1)} %get-tuple-element.33), channel_id=1, source_target_pairs={{0,1},{1,2},{2,3},{3,0},{4,5},{5,6},{6,7},{7,4},{8,9},{9,10},{10,1... | collective-permute-start | bytes 786440 | tf_op jit(solution)/shard_map/ppermute | solution.py:317
  46.6 1.7 %collective-permute-start.4 = (bf16[128,1024]{1,0:T(8,128)(2,1)S(1)}, bf16[128,1024]{1,0:T(8,128)(2,1)S(1)}, u32[]{:S(2)}, u32[]{:S(2)}) collective-permute-start(bf16[128,1024]{1,0:T(8,128)(2,1)S(1)} %get-tuple-element.34), channel_id=1, source_target_pairs={{0,3},{1,0},{2,1},{3,2},{4,7},{5,4},{6,5},{7,6},{8,11},{9,8},{10,9... | collective-permute-start | bytes 786440 | tf_op jit(solution)/shard_map/ppermute | solution.py:318
  48.3 2.9 %shard_map.87 = (bf16[128,1024]{1,0:T(8,128)(2,1)S(1)}, bf16[128,1024]{1,0:T(8,128)(2,1)S(1)}, bf16[1024,1024]{1,0:T(8,128)(2,1)S(1)}) custom-call(s32[1]{0:T(128)} %bitcast.me_ref, bf16[128,1024]{1,0:T(8,128)(2,1)S(1)} %get-tuple-element.29.rows_ref, bf16[1024,8192]{1,0:T(8,128)(2,1)} %weights_ref.9), custom_call_target="tpu_custom_call" | custom-call | flops 2147483648 | bytes 2097152 | tf_op jit(solution)/shard_map/pallas_call | solution.py:296
  51.2 0.4 collective-permute-start.1
  51.6 2.9 %collective-permute-start.2 = (bf16[128,1024]{1,0:T(8,128)(2,1)S(1)}, bf16[128,1024]{1,0:T(8,128)(2,1)S(1)}, u32[]{:S(2)}, u32[]{:S(2)}) collective-permute-start(bf16[128,1024]{1,0:T(8,128)(2,1)S(1)} %get-tuple-element.31), channel_id=1, source_target_pairs={{0,3},{1,0},{2,1},{3,2},{4,7},{5,4},{6,5},{7,6},{8,11},{9,8},{10,9... | collective-permute-start | bytes 786440 | tf_op jit(solution)/shard_map/ppermute | solution.py:322
  54.5 0.3 collective-permute-done.3.far_up_ref
  54.8 1.0 %collective-permute-done.4.far_down_ref = bf16[128,1024]{1,0:T(8,128)(2,1)S(1)} collective-permute-done((bf16[128,1024]{1,0:T(8,128)(2,1)S(1)}, bf16[128,1024]{1,0:T(8,128)(2,1)S(1)}, u32[]{:S(2)}, u32[]{:S(2)}) %collective-permute-start.4) | collective-permute-done | bytes 262176 | tf_op jit(solution)/shard_map/ppermute | solution.py:318
  55.8 2.2 %shard_map.89 = (bf16[128,1024]{1,0:T(8,128)(2,1)S(1)}, bf16[128,1024]{1,0:T(8,128)(2,1)S(1)}) custom-call(s32[1]{0:T(128)} %bitcast.me_ref, bf16[128,1024]{1,0:T(8,128)(2,1)S(1)} %get-tuple-element.29.rows_ref, bf16[1024,1024]{1,0:T(8,128)(2,1)S(1)} %get-tuple-element.32.first_ref, bf16[128,1024]{1,0:T(8,128)(2,1)S(1)} %collective-permute-done.3.far_up_ref, ...), custom_call_target="tpu_custom_call" | custom-call | flops 2147483648 | bytes 2097152 | tf_op jit(solution)/shard_map/pallas_call | solution.py:296
  58.0 1.6 %collective-permute-start.5 = (bf16[128,1024]{1,0:T(8,128)(2,1)S(1)}, bf16[128,1024]{1,0:T(8,128)(2,1)S(1)}, u32[]{:S(2)}, u32[]{:S(2)}) collective-permute-start(bf16[128,1024]{1,0:T(8,128)(2,1)S(1)} %get-tuple-element.35), channel_id=1, source_target_pairs={{0,1},{1,2},{2,3},{3,0},{4,5},{5,6},{6,7},{7,4},{8,9},{9,10},{10,1... | collective-permute-start | bytes 786440 | tf_op jit(solution)/shard_map/ppermute | solution.py:326
  59.6 1.7 %collective-permute-start.6 = (bf16[128,1024]{1,0:T(8,128)(2,1)S(1)}, bf16[128,1024]{1,0:T(8,128)(2,1)S(1)}, u32[]{:S(2)}, u32[]{:S(2)}) collective-permute-start(bf16[128,1024]{1,0:T(8,128)(2,1)S(1)} %get-tuple-element.36), channel_id=1, source_target_pairs={{0,3},{1,0},{2,1},{3,2},{4,7},{5,4},{6,5},{7,6},{8,11},{9,8},{10,9... | collective-permute-start | bytes 786440 | tf_op jit(solution)/shard_map/ppermute | solution.py:327
  61.3 0.0 collective-permute-done.1.near_up_ref
  61.3 0.0 collective-permute-done.2.near_down_ref
  61.3 2.6 %shard_map.88.own_ref = f32[128,2048]{1,0:T(8,128)S(1)} custom-call(s32[1]{0:T(128)} %bitcast.me_ref, bf16[128,1024]{1,0:T(8,128)(2,1)S(1)} %get-tuple-element.29.rows_ref, bf16[128,1024]{1,0:T(8,128)(2,1)S(1)} %collective-permute-done.1.near_up_ref, bf16[128,1024]{1,0:T(8,128)(2,1)S(1)} %collective-permute-done.2.near_down_ref, bf16[1024,8192]{1,0:T(8,128)(2,1)} %weights_ref.9), custom_call_target="tpu_custom_call" | custom-call | flops 2147483648 | bytes 2097152 | tf_op jit(solution)/shard_map/pallas_call | solution.py:296
  63.9 2.2 %collective-permute-done.5.both_up_ref = bf16[128,1024]{1,0:T(8,128)(2,1)S(1)} collective-permute-done((bf16[128,1024]{1,0:T(8,128)(2,1)S(1)}, bf16[128,1024]{1,0:T(8,128)(2,1)S(1)}, u32[]{:S(2)}, u32[]{:S(2)}) %collective-permute-start.5) | collective-permute-done | bytes 262176 | tf_op jit(solution)/shard_map/ppermute | solution.py:326
  66.1 0.0 collective-permute-done.6.both_down_ref
  66.1 0.9 %shard_map.90 = bf16[128,2048]{1,0:T(8,128)(2,1)} custom-call(f32[128,2048]{1,0:T(8,128)S(1)} %shard_map.88.own_ref, bf16[128,1024]{1,0:T(8,128)(2,1)S(1)} %collective-permute-done.5.both_up_ref, bf16[128,1024]{1,0:T(8,128)(2,1)S(1)} %collective-permute-done.6.both_down_ref), custom_call_target="tpu_custom_call" | custom-call | tf_op jit(solution)/shard_map/pallas_call | solution.py:329
  (2 shorter events, 0.0 us)
Async XLA Ops:
  2.3 22.8 %all-to-all-start = ((bf16[32,96,128]{2,1,0:T(8,128)(2,1)}), bf16[32,96,128]{2,1,0:T(8,128)(2,1)S(1)}, u32[]{:S(2)}, u32[]{:S(2)}) async-start(bf16[32,96,128]{2,1,0:T(8,128)(2,1)} %get-tuple-element.21), calls=%async_computation | async-start | bytes 1572864 | tf_op jit(solution)/shard_map/all_to_all | solution.py:393
  30.0 12.8 %all-to-all-start.1 = ((bf16[32,32,128]{2,1,0:T(8,128)(2,1)}), bf16[32,32,128]{2,1,0:T(8,128)(2,1)S(1)}, u32[]{:S(2)}, u32[]{:S(2)}) async-start(bf16[32,32,128]{2,1,0:T(8,128)(2,1)} %get-tuple-element.27), calls=%async_computation.1 | async-start | bytes 524288 | tf_op jit(solution)/shard_map/all_to_all | solution.py:408
  33.9 2.9 %collective-permute-start = (bf16[16,1024]{1,0:T(8,128)(2,1)S(1)}, bf16[16,1024]{1,0:T(8,128)(2,1)S(1)}, u32[]{:S(2)}, u32[]{:S(2)}) collective-permute-start(bf16[16,1024]{1,0:T(8,128)(2,1)S(1)} %get-tuple-element.22.refs_0_), channel_id=1, source_target_pairs={{0,4},{4,8},{8,12},{12,16},{16,20},{20,24},{24,28},{28,32},{32,36}... | collective-permute-start | bytes 98312 | tf_op jit(solution)/shard_map/ppermute | solution.py:394
  45.0 9.8 %collective-permute-start.3 = (bf16[128,1024]{1,0:T(8,128)(2,1)S(1)}, bf16[128,1024]{1,0:T(8,128)(2,1)S(1)}, u32[]{:S(2)}, u32[]{:S(2)}) collective-permute-start(bf16[128,1024]{1,0:T(8,128)(2,1)S(1)} %get-tuple-element.33), channel_id=1, source_target_pairs={{0,1},{1,2},{2,3},{3,0},{4,5},{5,6},{6,7},{7,4},{8,9},{9,10},{10,1... | collective-permute-start | bytes 786440 | tf_op jit(solution)/shard_map/ppermute | solution.py:317
  46.6 9.2 %collective-permute-start.4 = (bf16[128,1024]{1,0:T(8,128)(2,1)S(1)}, bf16[128,1024]{1,0:T(8,128)(2,1)S(1)}, u32[]{:S(2)}, u32[]{:S(2)}) collective-permute-start(bf16[128,1024]{1,0:T(8,128)(2,1)S(1)} %get-tuple-element.34), channel_id=1, source_target_pairs={{0,3},{1,0},{2,1},{3,2},{4,7},{5,4},{6,5},{7,6},{8,11},{9,8},{10,9... | collective-permute-start | bytes 786440 | tf_op jit(solution)/shard_map/ppermute | solution.py:318
  51.2 10.1 %collective-permute-start.1 = (bf16[128,1024]{1,0:T(8,128)(2,1)S(1)}, bf16[128,1024]{1,0:T(8,128)(2,1)S(1)}, u32[]{:S(2)}, u32[]{:S(2)}) collective-permute-start(bf16[128,1024]{1,0:T(8,128)(2,1)S(1)} %get-tuple-element.30), channel_id=1, source_target_pairs={{0,1},{1,2},{2,3},{3,0},{4,5},{5,6},{6,7},{7,4},{8,9},{9,10},{10,1... | collective-permute-start | bytes 786440 | tf_op jit(solution)/shard_map/ppermute | solution.py:321
  51.6 9.7 %collective-permute-start.2 = (bf16[128,1024]{1,0:T(8,128)(2,1)S(1)}, bf16[128,1024]{1,0:T(8,128)(2,1)S(1)}, u32[]{:S(2)}, u32[]{:S(2)}) collective-permute-start(bf16[128,1024]{1,0:T(8,128)(2,1)S(1)} %get-tuple-element.31), channel_id=1, source_target_pairs={{0,3},{1,0},{2,1},{3,2},{4,7},{5,4},{6,5},{7,6},{8,11},{9,8},{10,9... | collective-permute-start | bytes 786440 | tf_op jit(solution)/shard_map/ppermute | solution.py:322
  58.0 8.1 %collective-permute-start.5 = (bf16[128,1024]{1,0:T(8,128)(2,1)S(1)}, bf16[128,1024]{1,0:T(8,128)(2,1)S(1)}, u32[]{:S(2)}, u32[]{:S(2)}) collective-permute-start(bf16[128,1024]{1,0:T(8,128)(2,1)S(1)} %get-tuple-element.35), channel_id=1, source_target_pairs={{0,1},{1,2},{2,3},{3,0},{4,5},{5,6},{6,7},{7,4},{8,9},{9,10},{10,1... | collective-permute-start | bytes 786440 | tf_op jit(solution)/shard_map/ppermute | solution.py:326
  59.6 6.5 %collective-permute-start.6 = (bf16[128,1024]{1,0:T(8,128)(2,1)S(1)}, bf16[128,1024]{1,0:T(8,128)(2,1)S(1)}, u32[]{:S(2)}, u32[]{:S(2)}) collective-permute-start(bf16[128,1024]{1,0:T(8,128)(2,1)S(1)} %get-tuple-element.36), channel_id=1, source_target_pairs={{0,3},{1,0},{2,1},{3,2},{4,7},{5,4},{6,5},{7,6},{8,11},{9,8},{10,9... | collective-permute-start | bytes 786440 | tf_op jit(solution)/shard_map/ppermute | solution.py:327

commit v4 on v3

--- a/solution.py
+++ b/solution.py
@@ -88,14 +88,29 @@
 
 
 def stage_kernel(*refs):
-    sems = refs[-1]
-    count = sems.shape[0]
+    sems, bounce_ref = refs[-1], refs[-2]
+    tables_in, weights_ref = refs[1 : 1 + TABLES], refs[1 + TABLES]
+    tables_out = refs[2 + TABLES : 2 + 2 * TABLES]
+    rest_ref, near_ref, later_ref = refs[-5:-2]
     copies = [
-        pltpu.make_async_copy(source, target, sems.at[i])
-        for i, (source, target) in enumerate(zip(refs[1 : 1 + count], refs[1 + count : -1]))
+        pltpu.make_async_copy(source, target, sems.at[i]) for i, (source, target) in enumerate(zip(tables_in, tables_out))
     ]
     for copy in copies:
         copy.start()
+    count, arriving = TABLES, []
+    for target_ref, at, away, pieces, first in (
+        (near_ref, 0, 1, RIGHT, 0), (near_ref, 0, RING - 1, LEFT, 0), (rest_ref, WIDE, 2, RIGHT, UP),
+        (later_ref, 2 * WIDE - UP, 1, LEFT, 0), (later_ref, 2 * WIDE - UP, RING - 1, RIGHT, 0),
+    ):
+        held_ref = bounce_ref.at[:, at : at + target_ref.shape[1]]
+        for start, stop, copy in fetch(weights_ref, held_ref, sems.at[count:], away, pieces, first):
+            here = slice(start - first, stop - first)
+            arriving.append((copy, pltpu.make_async_copy(held_ref.at[:, here], target_ref.at[:, here], sems.at[count])))
+            count += 1
+    for copy, onward in arriving:
+        copy.wait()
+        onward.start()
+        copies.append(onward)
     for copy in copies:
         copy.wait()
 
@@ -119,10 +134,10 @@
 
 
 def conv_kernel(
-    me_ref, x_ref, taps_ref, skip_ref, high_ref, low_ref, twists_ref, weights_ref,
+    x_ref, taps_ref, skip_ref, high_ref, low_ref, twists_ref, weights_ref,
     out_ref, held_ref, gated_ref, first_ref, left_ref, back_ref, sems,
 ):
-    copies = fetch(weights_ref, held_ref, sems, 2, me_ref, LEFT)
+    copies = fetch(weights_ref, held_ref, sems, 2, LEFT)
     lane = lax.broadcasted_iota(jnp.int32, (SLAB, ROWS), 1)
 
     def rows_of(j, offset):
@@ -174,18 +189,18 @@
     def product(high, low):
         return jnp.dot(jnp.concatenate([low, high, high], axis=1), matrix, preferred_element_type=f32)
 
-    block = 512
-
-    for step in range(PARTS * GROUP // block):
-        rows = pl.ds(step * block, block)
+    block = 256
+    blocks = [pl.ds(start, block) for start in range(0, PARTS * GROUP, block)]
+    for rows in blocks:
         signal = product(left_ref[0, 0, rows, :], left_ref[0, 1, rows, :])
         taps = product(left_ref[1, 0, rows, :], left_ref[1, 1, rows, :])
         a, b = signal[:, :ROWS], signal[:, ROWS:]
         c, d = taps[:, :ROWS], taps[:, ROWS:]
         real, imag = split((a * c - b * d) * (1.0 / POINTS)), split((a * d + b * c) * (-1.0 / POINTS))
-        high = jnp.concatenate([real[0], imag[0]], axis=1)
-        low = jnp.concatenate([real[1], imag[1]], axis=1)
-        back_ref[rows, :] = product(high, low)
+        left_ref[0, 0, rows, :] = jnp.concatenate([real[0], imag[0]], axis=1)
+        left_ref[0, 1, rows, :] = jnp.concatenate([real[1], imag[1]], axis=1)
+    for rows in blocks:
+        back_ref[rows, :] = product(left_ref[0, 0, rows, :], left_ref[0, 1, rows, :])
 
     @pl.loop(0, GROUP // SLAB)
     def _(step):
@@ -216,8 +231,8 @@
         copy.wait()
 
 
-def fetch(weights_ref, target_ref, sems, away, me_ref, pieces, first=0):
-    columns = (me_ref[0] + away) % RING * WIDE
+def fetch(weights_ref, target_ref, sems, away, pieces, first=0):
+    columns = (lax.axis_index("ch") + away) % RING * WIDE
     copies = []
     for i, (start, stop) in enumerate(pieces):
         source = weights_ref.at[:, pl.ds(pl.multiple_of(columns + start, 128), stop - start)]
@@ -231,45 +246,36 @@
     return jnp.dot(rows_ref[...], held_ref[:, start:stop], preferred_element_type=f32)
 
 
-def far_kernel(me_ref, outer_ref, query_ref, first_ref, weights_ref, up_ref, down_ref, rows_ref, held_ref, sems):
-    copies = fetch(weights_ref, held_ref, sems, 2, me_ref, RIGHT, UP)
+def mixing_kernel(outer_ref, query_ref, held_ref, up_ref, rows_ref):
     rows_ref[...] = (query_ref[...] * outer_ref[...].T.astype(f32)).astype(bf16)
     for start, stop in LEFT:
-        up_ref[:, start:stop] = part_of(rows_ref, first_ref, start, stop).astype(bf16)
-    for start, stop, copy in copies:
-        copy.wait()
+        up_ref[:, start:stop] = part_of(rows_ref, held_ref, start, stop).astype(bf16)
+
+
+def far_kernel(rows_ref, rest_ref, down_ref):
+    for start, stop in RIGHT:
+        down_ref[:, start - UP : stop - UP] = part_of(rows_ref, rest_ref, start - UP, stop - UP).astype(bf16)
+
+
+def near_kernel(rows_ref, near_ref, up_ref, down_ref):
+    for start, stop in RIGHT:
+        up_ref[:, start - UP : stop - UP] = part_of(rows_ref, near_ref, start, stop).astype(bf16)
+    for start, stop in LEFT:
+        down_ref[:, start:stop] = part_of(rows_ref, near_ref, start, stop).astype(bf16)
+
+
+def adding_kernel(rows_ref, later_ref, far_up_ref, far_down_ref, up_ref, down_ref):
+    for start, stop in LEFT:
+        total = part_of(rows_ref, later_ref, start, stop)
+        up_ref[:, start:stop] = (total + far_up_ref[:, start:stop].astype(f32)).astype(bf16)
+    for start, stop in RIGHT:
         here = slice(start - UP, stop - UP)
-        down_ref[:, here] = part_of(rows_ref, held_ref, start - UP, stop - UP).astype(bf16)
-
-
-def near_kernel(me_ref, rows_ref, weights_ref, up_ref, down_ref, later_ref, held_ref, sems):
-    right = fetch(weights_ref, held_ref, sems, 1, me_ref, RIGHT)
-    left = fetch(weights_ref, held_ref, sems.at[len(RIGHT) :], -1, me_ref, LEFT)
-    later = fetch(weights_ref, later_ref, sems.at[len(RIGHT) + len(LEFT) :], 1, me_ref, LEFT)
-    for start, stop, copy in right:
-        copy.wait()
-        up_ref[:, start - UP : stop - UP] = part_of(rows_ref, held_ref, start, stop).astype(bf16)
-    for start, stop, copy in left:
-        copy.wait()
-        down_ref[:, start:stop] = part_of(rows_ref, held_ref, start, stop).astype(bf16)
-    for _, _, copy in later:
-        copy.wait()
-
-
-def adding_kernel(me_ref, rows_ref, first_ref, far_up_ref, far_down_ref, weights_ref, up_ref, down_ref, held_ref, sems):
-    copies = fetch(weights_ref, held_ref, sems, -1, me_ref, RIGHT, UP)
-    for start, stop in LEFT:
-        total = part_of(rows_ref, first_ref, start, stop)
-        up_ref[:, start:stop] = (total + far_up_ref[:, start:stop].astype(f32)).astype(bf16)
-    for start, stop, copy in copies:
-        copy.wait()
-        here = slice(start - UP, stop - UP)
-        total = part_of(rows_ref, held_ref, start - UP, stop - UP)
+        total = part_of(rows_ref, later_ref, start, stop)
         down_ref[:, here] = (total + far_down_ref[:, here].astype(f32)).astype(bf16)
 
 
-def own_kernel(me_ref, rows_ref, near_up_ref, near_down_ref, weights_ref, out_ref, held_ref, sems):
-    for start, stop, copy in fetch(weights_ref, held_ref, sems, 0, me_ref, LEFT + RIGHT):
+def own_kernel(rows_ref, near_up_ref, near_down_ref, weights_ref, out_ref, held_ref, sems):
+    for start, stop, copy in fetch(weights_ref, held_ref, sems, 0, LEFT + RIGHT):
         copy.wait()
         arrived = near_down_ref[:, start:stop] if start < UP else near_up_ref[:, start - UP : stop - UP]
         out_ref[:, start:stop] = part_of(rows_ref, held_ref, start, stop) + arrived.astype(f32)
@@ -280,6 +286,7 @@
         out_ref[:, part] = (own_ref[:, part] + arrived_ref[...].astype(f32)).astype(bf16)
 
 
+TABLES = 4
 RING = 4
 WIDE = 2048
 UP = 1024
@@ -288,14 +295,13 @@
 SENT = 3
 EDGE = 16
 VMEM = pl.BlockSpec(memory_space=pltpu.VMEM)
-SMEM = pl.BlockSpec(memory_space=pltpu.SMEM)
 HBM = pl.BlockSpec(memory_space=pltpu.HBM)
 
 
 def share(kernel, arrays, outs, held):
     return pl.pallas_call(
         kernel,
-        in_specs=[SMEM] + [VMEM] * (len(arrays) - 2) + [HBM],
+        in_specs=[VMEM] * (len(arrays) - 1) + [HBM],
         out_specs=[VMEM] * len(outs),
         out_shape=[pltpu.VMEM(shape, dtype) for shape, dtype in outs],
         scratch_shapes=[
@@ -307,25 +313,32 @@
     )(*arrays)
 
 
-def project(me, outer, query, weights, held):
+def plain(kernel, arrays, outs):
+    return pl.pallas_call(
+        kernel,
+        in_specs=[VMEM] * len(arrays),
+        out_specs=[VMEM] * len(outs),
+        out_shape=[pltpu.VMEM(shape, dtype) for shape, dtype in outs],
+        cost_estimate=pl.CostEstimate(flops=2**31, bytes_accessed=2**21, transcendentals=0),
+        compiler_params=pltpu.CompilerParams(vmem_limit_bytes=8 * 2**20),
+    )(*arrays)
+
+
+def project(outer, query, weights, held, rest, near, later):
     up = [(i, (i + 1) % RING) for i in range(RING)]
     down = [(i, (i - 1) % RING) for i in range(RING)]
     left, right = ((ROWS, UP), bf16), ((ROWS, WIDE - UP), bf16)
-    far_up, far_down, rows = share(
-        far_kernel, (me, outer, query, held, weights), [left, right, (query.shape, bf16)], WIDE - UP
-    )
+    far_up, rows = plain(mixing_kernel, (outer, query, held), [left, (query.shape, bf16)])
     far_up = lax.ppermute(far_up, "ch", up)
+    (far_down,) = plain(far_kernel, (rows, rest), [right])
     far_down = lax.ppermute(far_down, "ch", down)
-    later = ((weights.shape[0], UP), bf16)
-    near_up, near_down, later = share(near_kernel, (me, rows, weights), [right, left, later], WIDE)
+    near_up, near_down = plain(near_kernel, (rows, near), [right, left])
     near_up = lax.ppermute(near_up, "ch", up)
     near_down = lax.ppermute(near_down, "ch", down)
-    both_up, both_down = share(
-        adding_kernel, (me, rows, later, far_up, far_down, weights), [left, right], WIDE - UP
-    )
+    both_up, both_down = plain(adding_kernel, (rows, later, far_up, far_down), [left, right])
     both_up = lax.ppermute(both_up, "ch", up)
     both_down = lax.ppermute(both_down, "ch", down)
-    (own,) = share(own_kernel, (me, rows, near_up, near_down, weights), [((ROWS, WIDE), f32)], WIDE)
+    (own,) = share(own_kernel, (rows, near_up, near_down, weights), [((ROWS, WIDE), f32)], WIDE)
     return pl.pallas_call(
         last_kernel,
         in_specs=[VMEM] * 3,
@@ -335,23 +348,27 @@
     )(own, both_up, both_down)
 
 
-def stage(after, *arrays):
+def stage(after, weights, *arrays):
     arrays = [pltpu.with_memory_space_constraint(array, pltpu.HBM) for array in arrays]
+    parts = [pltpu.HBM((weights.shape[0], wide), bf16) for wide in (WIDE - UP, WIDE, WIDE)]
     return pl.pallas_call(
         stage_kernel,
-        in_specs=[pl.BlockSpec(memory_space=pl.ANY)] + [HBM] * len(arrays),
-        out_specs=[VMEM] * len(arrays),
-        out_shape=[pltpu.VMEM(array.shape, array.dtype) for array in arrays],
-        scratch_shapes=[pltpu.SemaphoreType.DMA((len(arrays),))],
+        in_specs=[pl.BlockSpec(memory_space=pl.ANY)] + [HBM] * (len(arrays) + 1),
+        out_specs=[VMEM] * len(arrays) + [HBM] * len(parts),
+        out_shape=[pltpu.VMEM(array.shape, array.dtype) for array in arrays] + parts,
+        scratch_shapes=[
+            pltpu.VMEM((weights.shape[0], 3 * WIDE - UP), bf16),
+            pltpu.SemaphoreType.DMA((len(arrays) + 2 * len(LEFT) + 3 * len(RIGHT),)),
+        ],
         compiler_params=pltpu.CompilerParams(vmem_limit_bytes=16 * 2**20),
-    )(after, *arrays)
+    )(after, *arrays, weights)
 
 
 def convolve(*arrays):
     channels = arrays[-1].shape[0]
     return pl.pallas_call(
         conv_kernel,
-        in_specs=[SMEM] + [VMEM] * 6 + [HBM],
+        in_specs=[VMEM] * 6 + [HBM],
         out_specs=[VMEM, VMEM],
         out_shape=[
             pltpu.VMEM((PARTS, GROUP, ROWS), bf16),
@@ -372,7 +389,6 @@
     channels = streams.shape[2]
     streams = pltpu.with_memory_space_constraint(streams, pltpu.HBM)
     weights = pltpu.with_memory_space_constraint(out_weights, pltpu.HBM)
-    me = lax.axis_index("ch").astype(jnp.int32).reshape(1)
     packed, edge = pl.pallas_call(
         exchange_kernel,
         in_specs=[HBM, HBM],
@@ -389,14 +405,14 @@
         compiler_params=pltpu.CompilerParams(vmem_limit_bytes=8 * 2**20),
     )(streams, pltpu.with_memory_space_constraint(long_filter, pltpu.HBM))
     high, low, twists = (jnp.asarray(table) for table in tables())
-    high, low, twists, short_taps = stage(edge, high, low, twists, short_taps)
+    high, low, twists, short_taps, *parts = stage(edge, weights, high, low, twists, short_taps)
     arrived = lax.all_to_all(packed, "seq", 0, 0, tiled=True)
     edge = lax.ppermute(edge, "seq", [(i, i + 1) for i in range(PARTS - 1)])
     first = lax.axis_index("seq") * GROUP
     taps = lax.dynamic_slice_in_dim(short_taps[1:].reshape((SENT - 1) * SHORT, channels), first, GROUP, 1)
     taps = jnp.broadcast_to(taps[:, :, None], ((SENT - 1) * SHORT, GROUP, ROWS))
     skip = jnp.broadcast_to(lax.dynamic_slice_in_dim(skip_gain, first, GROUP, 0)[:, None], (GROUP, ROWS))
-    outer, held = convolve(me, arrived, taps, skip, high, low, twists, weights)
+    outer, held = convolve(arrived, taps, skip, high, low, twists, weights)
     query = pl.pallas_call(
         query_kernel,
         in_specs=[HBM, VMEM, VMEM, VMEM],
@@ -406,7 +422,7 @@
         compiler_params=pltpu.CompilerParams(vmem_limit_bytes=8 * 2**20),
     )(streams, edge, short_taps, held)
     outer = lax.all_to_all(outer, "seq", 0, 0, tiled=True)
-    return project(me, outer.reshape(channels, ROWS), query, weights, held)
+    return project(outer.reshape(channels, ROWS), query, weights, held, *parts)
 
 
 def solution(mesh):

time: 67.5 us -> 66.7 us (0.988)
  waiting for transfers between devices: 21.9 us -> 16.9 us
  Pallas kernels: 19.9 us -> 22.2 us
  starting transfers between devices: 24.1 us -> 25.5 us
    pallas_call x1, Pallas kernels: 1.01 us -> 8.52 us  [stage(): pl.pallas_call(stage_kernel, in_specs=[pl.BlockSpec(memory_space=pl.ANY)]...]
    all_to_all x1, waiting for transfers between devices: 12.7 us -> 5.14 us  [on_device(): arrived = lax.all_to_all(packed, 'seq', 0, 0, tiled=True)]
    pallas_call x5 -> x6, Pallas kernels: 14.6 us -> 9.35 us  [the longest x1 4.4 us: convolve(): pl.pallas_call(conv_kernel, in_specs=[VMEM] * 6 + [HBM], out_specs=[VMEM,...]
    ppermute x1, waiting for transfers between devices: 0.31 us -> 1.65 us  [project(): far_up = lax.ppermute(far_up, 'ch', up)]
    ppermute x1, waiting for transfers between devices: 0.01 us -> 1.1 us  [project(): near_down = lax.ppermute(near_down, 'ch', down)]
    ppermute x1, starting transfers between devices: 1.66 us -> 2.53 us  [project(): far_down = lax.ppermute(far_down, 'ch', down)]
    ppermute x1, waiting for transfers between devices: 0.01 us -> 0.81 us  [project(): both_down = lax.ppermute(both_down, 'ch', down)]
    ppermute x1, waiting for transfers between devices: 2.23 us -> 1.52 us  [project(): both_up = lax.ppermute(both_up, 'ch', up)]
  transfers between devices with their start and end apart: 9 -> 9, of which waited for: 6 -> 8; matrix products, arithmetic and copies ran while one was open for 1% -> 1% of each run, Pallas kernels for 15% -> 22%
where the time goes in v4:
time: 66.7 us; the launch traced here: 65.7 us
  starting transfers between devices  25.5 us (38%)
  Pallas kernels  22.2 us (33%)
  waiting for transfers between devices  16.9 us (25%)
  local copies, waits for them, and re-layouts  1.02 us (2%)
    pallas_call x1, Pallas kernels, stage(): pl.pallas_call(stage_kernel, in_specs=[pl.BlockSpec(memory_space=pl.ANY)]...  8.52 us
    all_to_all x1, starting transfers between devices, on_device(): arrived = lax.all_to_all(packed, 'seq', 0, 0, tiled=True)  8.26 us
    all_to_all x1, waiting for transfers between devices, on_device(): arrived = lax.all_to_all(packed, 'seq', 0, 0, tiled=True)  5.14 us
    all_to_all x1, waiting for transfers between devices, on_device(): outer = lax.all_to_all(outer, 'seq', 0, 0, tiled=True)  4.82 us
    pallas_call x1, Pallas kernels, convolve(): pl.pallas_call(conv_kernel, in_specs=[VMEM] * 6 + [HBM], out_specs=[VMEM,...  4.4 us
    all_to_all x1, starting transfers between devices, on_device(): outer = lax.all_to_all(outer, 'seq', 0, 0, tiled=True)  3.88 us
    ppermute x1, starting transfers between devices, project(): near_down = lax.ppermute(near_down, 'ch', down)  3.22 us
    pallas_call x1, Pallas kernels, share(): pl.pallas_call(kernel, in_specs=[VMEM] * (len(arrays) - 1) + [HBM], out_s...  2.57 us
  transfers between devices with their start and end apart: 9, of which 8 were waited for; matrix products, arithmetic and copies ran while one was open for 1% of the time, Pallas kernels for 22%

profile of v4, /device:TPU:0, one launch (start us, length us, event | category | flops | bytes accessed | tf_op | source)
XLA Modules:
  0.0 65.7 jit_solution(383743613626764399)
XLA Ops:
  0.0 2.2 %shard_map.82 = (bf16[32,96,128]{2,1,0:T(8,128)(2,1)}, bf16[16,1024]{1,0:T(8,128)(2,1)S(1)}) custom-call(bf16[3,128,1024]{2,1,0:T(8,128)(2,1)} %streams_ref.3, f32[128,1024]{1,0:T(8,128)} %filter_ref.1), custom_call_target="tpu_custom_call" | custom-call | tf_op jit(solution)/shard_map/pallas_call | solution.py:392
  2.3 8.3 %all-to-all-start = ((bf16[32,96,128]{2,1,0:T(8,128)(2,1)}), bf16[32,96,128]{2,1,0:T(8,128)(2,1)S(1)}, u32[]{:S(2)}, u32[]{:S(2)}) async-start(bf16[32,96,128]{2,1,0:T(8,128)(2,1)} %get-tuple-element.22), calls=%async_computation | async-start | bytes 1572864 | tf_op jit(solution)/shard_map/all_to_all | solution.py:409
  10.5 8.5 %shard_map.83 = (bf16[256,256]{1,0:T(8,128)(2,1)S(1)}, bf16[256,256]{1,0:T(8,128)(2,1)S(1)}, f32[32,2,128]{2,1,0:T(2,128)S(1)}, f32[3,3,1024]{2,1,0:T(4,128)S(1)...) custom-call(bf16[16,1024]{1,0:T(8,128)(2,1)S(1)} %get-tuple-element.23.refs_0_, ...), custom_call_target="tpu_custom_call" | custom-call | tf_op jit(solution)/shard_map/pallas_call | solution.py:354
  19.1 0.8 %dynamic_slice.7 = f32[32]{0:T(128)S(1)} dynamic-slice(f32[1024]{0:T(1024)} %param.11, s32[]{:T(128)S(6)} %select_n.4), dynamic_slice_sizes={32} | dynamic-slice | bytes 260 | tf_op jit(solution)/shard_map/dynamic_slice | solution.py:414
  19.9 0.1 constant_dynamic-slice_fusion
  19.9 5.1 %all-to-all-done.x_ref = bf16[32,96,128]{2,1,0:T(8,128)(2,1)S(1)} async-done(((bf16[32,96,128]{2,1,0:T(8,128)(2,1)}), bf16[32,96,128]{2,1,0:T(8,128)(2,1)S(1)}, u32[]{:S(2)}, u32[]{:S(2)}) %all-to-all-start) | async-done | bytes 786464 | tf_op jit(solution)/shard_map/all_to_all | solution.py:409
  25.1 0.1 broadcast_in_dim.5.skip_ref
  25.2 0.1 broadcast_in_dim.4.taps_ref
  25.2 4.4 %shard_map.84 = (bf16[32,32,128]{2,1,0:T(8,128)(2,1)}, bf16[1024,1024]{1,0:T(8,128)(2,1)S(1)}) custom-call(bf16[32,96,128]{2,1,0:T(8,128)(2,1)S(1)} %all-to-all-done.x_ref, f32[6,32,128]{2,1,0:T(8,128)S(1)} %broadcast_in_dim.4.taps_ref, f32[32,128]{1,0:T(8,128)S(1)} %broadcast_in_dim.5.skip_ref, bf16[256,256]{1,0:T(8,128)(2,1)S(1)} %get-tuple-element.25.high_ref, ...), custom_call_target="tpu_custom_call" | custom-call | tf_op jit(solution)/shard_map/pallas_call | solution.py:369
  29.6 3.9 %all-to-all-start.1 = ((bf16[32,32,128]{2,1,0:T(8,128)(2,1)}), bf16[32,32,128]{2,1,0:T(8,128)(2,1)S(1)}, u32[]{:S(2)}, u32[]{:S(2)}) async-start(bf16[32,32,128]{2,1,0:T(8,128)(2,1)} %get-tuple-element.28), calls=%async_computation.1 | async-start | bytes 524288 | tf_op jit(solution)/shard_map/all_to_all | solution.py:424
  33.5 2.1 %collective-permute-start = (bf16[16,1024]{1,0:T(8,128)(2,1)S(1)}, bf16[16,1024]{1,0:T(8,128)(2,1)S(1)}, u32[]{:S(2)}, u32[]{:S(2)}) collective-permute-start(bf16[16,1024]{1,0:T(8,128)(2,1)S(1)} %get-tuple-element.23.refs_0_), channel_id=1, source_target_pairs={{0,4},{4,8},{8,12},{12,16},{16,20},{20,24},{24,28},{28,32},{32,36}... | collective-permute-start | bytes 98312 | tf_op jit(solution)/shard_map/ppermute | solution.py:410
  35.6 0.8 %collective-permute-done.edge_ref = bf16[16,1024]{1,0:T(8,128)(2,1)S(1)} collective-permute-done((bf16[16,1024]{1,0:T(8,128)(2,1)S(1)}, bf16[16,1024]{1,0:T(8,128)(2,1)S(1)}, u32[]{:S(2)}, u32[]{:S(2)}) %collective-permute-start) | collective-permute-done | bytes 32800 | tf_op jit(solution)/shard_map/ppermute | solution.py:410
  36.5 1.2 %shard_map.85.query_ref = f32[128,1024]{1,0:T(8,128)S(1)} custom-call(bf16[3,128,1024]{2,1,0:T(8,128)(2,1)} %streams_ref.3, bf16[16,1024]{1,0:T(8,128)(2,1)S(1)} %collective-permute-done.edge_ref, f32[3,3,1024]{2,1,0:T(4,128)S(1)} %get-tuple-element.24.taps_ref, bf16[1024,1024]{1,0:T(8,128)(2,1)S(1)} %get-tuple-element.29.held_ref), custom_call_target="tpu_custom_call" | custom-call | tf_op jit(solution)/shard_map/pallas_call | solution.py:416
  37.6 4.8 %all-to-all-done.1 = bf16[32,32,128]{2,1,0:T(8,128)(2,1)S(1)} async-done(((bf16[32,32,128]{2,1,0:T(8,128)(2,1)}), bf16[32,32,128]{2,1,0:T(8,128)(2,1)S(1)}, u32[]{:S(2)}, u32[]{:S(2)}) %all-to-all-start.1) | async-done | bytes 262176 | tf_op jit(solution)/shard_map/all_to_all | solution.py:424
  42.4 0.0 copy-start.2
  42.4 0.5 shard_map.86
  42.9 0.0 copy-start.1
  42.9 1.6 %collective-permute-start.3 = (bf16[128,1024]{1,0:T(8,128)(2,1)S(1)}, bf16[128,1024]{1,0:T(8,128)(2,1)S(1)}, u32[]{:S(2)}, u32[]{:S(2)}) collective-permute-start(bf16[128,1024]{1,0:T(8,128)(2,1)S(1)} %get-tuple-element.35), channel_id=1, source_target_pairs={{0,1},{1,2},{2,3},{3,0},{4,5},{5,6},{6,7},{7,4},{8,9},{9,10},{10,1... | collective-permute-start | bytes 786440 | tf_op jit(solution)/shard_map/ppermute | solution.py:332
  44.6 0.0 copy-done.2
  44.6 0.5 shard_map.89
  45.0 0.0 copy-start
  45.1 2.5 %collective-permute-start.4 = (bf16[128,1024]{1,0:T(8,128)(2,1)S(1)}, bf16[128,1024]{1,0:T(8,128)(2,1)S(1)}, u32[]{:S(2)}, u32[]{:S(2)}) collective-permute-start(bf16[128,1024]{1,0:T(8,128)(2,1)S(1)} %shard_map.89), channel_id=1, source_target_pairs={{0,3},{1,0},{2,1},{3,2},{4,7},{5,4},{6,5},{7,6},{8,11},{9,8},{10,9... | collective-permute-start | bytes 786440 | tf_op jit(solution)/shard_map/ppermute | solution.py:334
  47.6 0.0 copy-done.1
  47.6 0.7 %shard_map.87 = (bf16[128,1024]{1,0:T(8,128)(2,1)S(1)}, bf16[128,1024]{1,0:T(8,128)(2,1)S(1)}) custom-call(bf16[128,1024]{1,0:T(8,128)(2,1)S(1)} %get-tuple-element.30.rows_ref, bf16[1024,2048]{1,0:T(8,128)(2,1)S(1)} %copy-done.1), custom_call_target="tpu_custom_call" | custom-call | flops 2147483648 | bytes 2097152 | tf_op jit(solution)/shard_map/pallas_call | solution.py:317
  48.3 0.1 collective-permute-start.1
  48.4 3.2 %collective-permute-start.2 = (bf16[128,1024]{1,0:T(8,128)(2,1)S(1)}, bf16[128,1024]{1,0:T(8,128)(2,1)S(1)}, u32[]{:S(2)}, u32[]{:S(2)}) collective-permute-start(bf16[128,1024]{1,0:T(8,128)(2,1)S(1)} %get-tuple-element.33), channel_id=1, source_target_pairs={{0,3},{1,0},{2,1},{3,2},{4,7},{5,4},{6,5},{7,6},{8,11},{9,8},{10,9... | collective-permute-start | bytes 786440 | tf_op jit(solution)/shard_map/ppermute | solution.py:337
  51.6 1.7 %collective-permute-done.3.far_up_ref = bf16[128,1024]{1,0:T(8,128)(2,1)S(1)} collective-permute-done((bf16[128,1024]{1,0:T(8,128)(2,1)S(1)}, bf16[128,1024]{1,0:T(8,128)(2,1)S(1)}, u32[]{:S(2)}, u32[]{:S(2)}) %collective-permute-start.3) | collective-permute-done | bytes 262176 | tf_op jit(solution)/shard_map/ppermute | solution.py:332
  53.3 1.0 %collective-permute-done.4.far_down_ref = bf16[128,1024]{1,0:T(8,128)(2,1)S(1)} collective-permute-done((bf16[128,1024]{1,0:T(8,128)(2,1)S(1)}, bf16[128,1024]{1,0:T(8,128)(2,1)S(1)}, u32[]{:S(2)}, u32[]{:S(2)}) %collective-permute-start.4) | collective-permute-done | bytes 262176 | tf_op jit(solution)/shard_map/ppermute | solution.py:334
  54.3 0.0 copy-done
  54.3 0.7 %shard_map.90 = (bf16[128,1024]{1,0:T(8,128)(2,1)S(1)}, bf16[128,1024]{1,0:T(8,128)(2,1)S(1)}) custom-call(bf16[128,1024]{1,0:T(8,128)(2,1)S(1)} %get-tuple-element.30.rows_ref, bf16[1024,2048]{1,0:T(8,128)(2,1)S(1)} %copy-done, bf16[128,1024]{1,0:T(8,128)(2,1)S(1)} %collective-permute-done.3.far_up_ref, ...), custom_call_target="tpu_custom_call" | custom-call | flops 2147483648 | bytes 2097152 | tf_op jit(solution)/shard_map/pallas_call | solution.py:317
  55.0 1.6 %collective-permute-start.5 = (bf16[128,1024]{1,0:T(8,128)(2,1)S(1)}, bf16[128,1024]{1,0:T(8,128)(2,1)S(1)}, u32[]{:S(2)}, u32[]{:S(2)}) collective-permute-start(bf16[128,1024]{1,0:T(8,128)(2,1)S(1)} %get-tuple-element.37), channel_id=1, source_target_pairs={{0,1},{1,2},{2,3},{3,0},{4,5},{5,6},{6,7},{7,4},{8,9},{9,10},{10,1... | collective-permute-start | bytes 786440 | tf_op jit(solution)/shard_map/ppermute | solution.py:339
  56.7 2.1 %collective-permute-start.6 = (bf16[128,1024]{1,0:T(8,128)(2,1)S(1)}, bf16[128,1024]{1,0:T(8,128)(2,1)S(1)}, u32[]{:S(2)}, u32[]{:S(2)}) collective-permute-start(bf16[128,1024]{1,0:T(8,128)(2,1)S(1)} %get-tuple-element.38), channel_id=1, source_target_pairs={{0,3},{1,0},{2,1},{3,2},{4,7},{5,4},{6,5},{7,6},{8,11},{9,8},{10,9... | collective-permute-start | bytes 786440 | tf_op jit(solution)/shard_map/ppermute | solution.py:340
  58.8 0.0 collective-permute-done.1.near_up_ref
  58.8 1.1 %collective-permute-done.2.near_down_ref = bf16[128,1024]{1,0:T(8,128)(2,1)S(1)} collective-permute-done((bf16[128,1024]{1,0:T(8,128)(2,1)S(1)}, bf16[128,1024]{1,0:T(8,128)(2,1)S(1)}, u32[]{:S(2)}, u32[]{:S(2)}) %collective-permute-start.2) | collective-permute-done | bytes 262176 | tf_op jit(solution)/shard_map/ppermute | solution.py:337
  59.9 2.6 %shard_map.88.own_ref = f32[128,2048]{1,0:T(8,128)S(1)} custom-call(bf16[128,1024]{1,0:T(8,128)(2,1)S(1)} %get-tuple-element.30.rows_ref, bf16[128,1024]{1,0:T(8,128)(2,1)S(1)} %collective-permute-done.1.near_up_ref, bf16[128,1024]{1,0:T(8,128)(2,1)S(1)} %collective-permute-done.2.near_down_ref, bf16[1024,8192]{1,0:T(8,128)(2,1)} %weights_ref.3), custom_call_target="tpu_custom_call" | custom-call | flops 2147483648 | bytes 2097152 | tf_op jit(solution)/shard_map/pallas_call | solution.py:302
  62.5 1.5 %collective-permute-done.5.both_up_ref = bf16[128,1024]{1,0:T(8,128)(2,1)S(1)} collective-permute-done((bf16[128,1024]{1,0:T(8,128)(2,1)S(1)}, bf16[128,1024]{1,0:T(8,128)(2,1)S(1)}, u32[]{:S(2)}, u32[]{:S(2)}) %collective-permute-start.5) | collective-permute-done | bytes 262176 | tf_op jit(solution)/shard_map/ppermute | solution.py:339
  64.0 0.8 %collective-permute-done.6.both_down_ref = bf16[128,1024]{1,0:T(8,128)(2,1)S(1)} collective-permute-done((bf16[128,1024]{1,0:T(8,128)(2,1)S(1)}, bf16[128,1024]{1,0:T(8,128)(2,1)S(1)}, u32[]{:S(2)}, u32[]{:S(2)}) %collective-permute-start.6) | collective-permute-done | bytes 262176 | tf_op jit(solution)/shard_map/ppermute | solution.py:340
  64.8 0.9 %shard_map.91 = bf16[128,2048]{1,0:T(8,128)(2,1)} custom-call(f32[128,2048]{1,0:T(8,128)S(1)} %shard_map.88.own_ref, bf16[128,1024]{1,0:T(8,128)(2,1)S(1)} %collective-permute-done.5.both_up_ref, bf16[128,1024]{1,0:T(8,128)(2,1)S(1)} %collective-permute-done.6.both_down_ref), custom_call_target="tpu_custom_call" | custom-call | tf_op jit(solution)/shard_map/pallas_call | solution.py:342
  (2 shorter events, 0.0 us)
Async XLA Ops:
  2.3 22.8 %all-to-all-start = ((bf16[32,96,128]{2,1,0:T(8,128)(2,1)}), bf16[32,96,128]{2,1,0:T(8,128)(2,1)S(1)}, u32[]{:S(2)}, u32[]{:S(2)}) async-start(bf16[32,96,128]{2,1,0:T(8,128)(2,1)} %get-tuple-element.22), calls=%async_computation | async-start | bytes 1572864 | tf_op jit(solution)/shard_map/all_to_all | solution.py:409
  29.6 12.8 %all-to-all-start.1 = ((bf16[32,32,128]{2,1,0:T(8,128)(2,1)}), bf16[32,32,128]{2,1,0:T(8,128)(2,1)S(1)}, u32[]{:S(2)}, u32[]{:S(2)}) async-start(bf16[32,32,128]{2,1,0:T(8,128)(2,1)} %get-tuple-element.28), calls=%async_computation.1 | async-start | bytes 524288 | tf_op jit(solution)/shard_map/all_to_all | solution.py:424
  33.5 2.9 %collective-permute-start = (bf16[16,1024]{1,0:T(8,128)(2,1)S(1)}, bf16[16,1024]{1,0:T(8,128)(2,1)S(1)}, u32[]{:S(2)}, u32[]{:S(2)}) collective-permute-start(bf16[16,1024]{1,0:T(8,128)(2,1)S(1)} %get-tuple-element.23.refs_0_), channel_id=1, source_target_pairs={{0,4},{4,8},{8,12},{12,16},{16,20},{20,24},{24,28},{28,32},{32,36}... | collective-permute-start | bytes 98312 | tf_op jit(solution)/shard_map/ppermute | solution.py:410
  42.4 2.1 %copy-start.2 = (bf16[1024,1024]{1,0:T(8,128)(2,1)S(1)}, bf16[1024,1024]{1,0:T(8,128)(2,1)}, u32[]{:S(2)}) copy-start(bf16[1024,1024]{1,0:T(8,128)(2,1)} %get-tuple-element.36.rest_ref) | copy-start | bytes 6291460
  42.9 4.7 %copy-start.1 = (bf16[1024,2048]{1,0:T(8,128)(2,1)S(1)}, bf16[1024,2048]{1,0:T(8,128)(2,1)}, u32[]{:S(2)}) copy-start(bf16[1024,2048]{1,0:T(8,128)(2,1)} %get-tuple-element.31.near_ref) | copy-start | bytes 12582916
  42.9 10.3 %collective-permute-start.3 = (bf16[128,1024]{1,0:T(8,128)(2,1)S(1)}, bf16[128,1024]{1,0:T(8,128)(2,1)S(1)}, u32[]{:S(2)}, u32[]{:S(2)}) collective-permute-start(bf16[128,1024]{1,0:T(8,128)(2,1)S(1)} %get-tuple-element.35), channel_id=1, source_target_pairs={{0,1},{1,2},{2,3},{3,0},{4,5},{5,6},{6,7},{7,4},{8,9},{9,10},{10,1... | collective-permute-start | bytes 786440 | tf_op jit(solution)/shard_map/ppermute | solution.py:332
  45.0 9.3 %copy-start = (bf16[1024,2048]{1,0:T(8,128)(2,1)S(1)}, bf16[1024,2048]{1,0:T(8,128)(2,1)}, u32[]{:S(2)}) copy-start(bf16[1024,2048]{1,0:T(8,128)(2,1)} %get-tuple-element.34.later_ref) | copy-start | bytes 12582916
  45.1 9.2 %collective-permute-start.4 = (bf16[128,1024]{1,0:T(8,128)(2,1)S(1)}, bf16[128,1024]{1,0:T(8,128)(2,1)S(1)}, u32[]{:S(2)}, u32[]{:S(2)}) collective-permute-start(bf16[128,1024]{1,0:T(8,128)(2,1)S(1)} %shard_map.89), channel_id=1, source_target_pairs={{0,3},{1,0},{2,1},{3,2},{4,7},{5,4},{6,5},{7,6},{8,11},{9,8},{10,9... | collective-permute-start | bytes 786440 | tf_op jit(solution)/shard_map/ppermute | solution.py:334
  48.3 10.5 %collective-permute-start.1 = (bf16[128,1024]{1,0:T(8,128)(2,1)S(1)}, bf16[128,1024]{1,0:T(8,128)(2,1)S(1)}, u32[]{:S(2)}, u32[]{:S(2)}) collective-permute-start(bf16[128,1024]{1,0:T(8,128)(2,1)S(1)} %get-tuple-element.32), channel_id=1, source_target_pairs={{0,1},{1,2},{2,3},{3,0},{4,5},{5,6},{6,7},{7,4},{8,9},{9,10},{10,1... | collective-permute-start | bytes 786440 | tf_op jit(solution)/shard_map/ppermute | solution.py:336
  48.4 11.5 %collective-permute-start.2 = (bf16[128,1024]{1,0:T(8,128)(2,1)S(1)}, bf16[128,1024]{1,0:T(8,128)(2,1)S(1)}, u32[]{:S(2)}, u32[]{:S(2)}) collective-permute-start(bf16[128,1024]{1,0:T(8,128)(2,1)S(1)} %get-tuple-element.33), channel_id=1, source_target_pairs={{0,3},{1,0},{2,1},{3,2},{4,7},{5,4},{6,5},{7,6},{8,11},{9,8},{10,9... | collective-permute-start | bytes 786440 | tf_op jit(solution)/shard_map/ppermute | solution.py:337
  55.0 9.0 %collective-permute-start.5 = (bf16[128,1024]{1,0:T(8,128)(2,1)S(1)}, bf16[128,1024]{1,0:T(8,128)(2,1)S(1)}, u32[]{:S(2)}, u32[]{:S(2)}) collective-permute-start(bf16[128,1024]{1,0:T(8,128)(2,1)S(1)} %get-tuple-element.37), channel_id=1, source_target_pairs={{0,1},{1,2},{2,3},{3,0},{4,5},{5,6},{6,7},{7,4},{8,9},{9,10},{10,1... | collective-permute-start | bytes 786440 | tf_op jit(solution)/shard_map/ppermute | solution.py:339
  56.7 8.1 %collective-permute-start.6 = (bf16[128,1024]{1,0:T(8,128)(2,1)S(1)}, bf16[128,1024]{1,0:T(8,128)(2,1)S(1)}, u32[]{:S(2)}, u32[]{:S(2)}) collective-permute-start(bf16[128,1024]{1,0:T(8,128)(2,1)S(1)} %get-tuple-element.38), channel_id=1, source_target_pairs={{0,3},{1,0},{2,1},{3,2},{4,7},{5,4},{6,5},{7,6},{8,11},{9,8},{10,9... | collective-permute-start | bytes 786440 | tf_op jit(solution)/shard_map/ppermute | solution.py:340

commit v5 on v4

--- a/solution.py
+++ b/solution.py
@@ -289,9 +289,9 @@
 TABLES = 4
 RING = 4
 WIDE = 2048
-UP = 1024
-LEFT = ((0, 512), (512, UP))
-RIGHT = ((UP, 1536), (1536, WIDE))
+UP = 1152
+LEFT = ((0, 640), (640, UP))
+RIGHT = ((UP, 1664), (1664, WIDE))
 SENT = 3
 EDGE = 16
 VMEM = pl.BlockSpec(memory_space=pltpu.VMEM)

time: 66.7 us -> 66 us (0.990)
  waiting for transfers between devices: 16.9 us -> 17.9 us
  starting transfers between devices: 25.5 us -> 24.8 us
    ppermute x1, waiting for transfers between devices: 1.65 us -> 0.45 us  [project(): far_up = lax.ppermute(far_up, 'ch', up)]
    ppermute x1, waiting for transfers between devices: 1.03 us -> 2.03 us  [project(): far_down = lax.ppermute(far_down, 'ch', down)]
    ppermute x1, waiting for transfers between devices: 1.52 us -> 0.73 us  [project(): both_up = lax.ppermute(both_up, 'ch', up)]
    all_to_all x1, waiting for transfers between devices: 5.14 us -> 5.93 us  [on_device(): arrived = lax.all_to_all(packed, 'seq', 0, 0, tiled=True)]
    pallas_call x1, Pallas kernels: 8.52 us -> 7.74 us  [stage(): pl.pallas_call(stage_kernel, in_specs=[pl.BlockSpec(memory_space=pl.ANY)]...]
    ppermute x1, waiting for transfers between devices: 0.01 us -> 0.78 us  [project(): near_up = lax.ppermute(near_up, 'ch', up)]
  transfers between devices with their start and end apart: 9 -> 9, of which waited for: 8 -> 9; matrix products, arithmetic and copies ran while one was open for 1% -> 1% of each run, Pallas kernels for 22% -> 21%
where the time goes in v5:
time: 66 us; the launch traced here: 65.6 us
  starting transfers between devices  24.8 us (38%)
  Pallas kernels  21.7 us (33%)
  waiting for transfers between devices  17.9 us (27%)
  local copies, waits for them, and re-layouts  1.02 us (2%)
    all_to_all x1, starting transfers between devices, on_device(): arrived = lax.all_to_all(packed, 'seq', 0, 0, tiled=True)  8.26 us
    pallas_call x1, Pallas kernels, stage(): pl.pallas_call(stage_kernel, in_specs=[pl.BlockSpec(memory_space=pl.ANY)]...  7.74 us
    all_to_all x1, waiting for transfers between devices, on_device(): arrived = lax.all_to_all(packed, 'seq', 0, 0, tiled=True)  5.93 us
    all_to_all x1, waiting for transfers between devices, on_device(): outer = lax.all_to_all(outer, 'seq', 0, 0, tiled=True)  4.82 us
    pallas_call x1, Pallas kernels, convolve(): pl.pallas_call(conv_kernel, in_specs=[VMEM] * 6 + [HBM], out_specs=[VMEM,...  4.4 us
    all_to_all x1, starting transfers between devices, on_device(): outer = lax.all_to_all(outer, 'seq', 0, 0, tiled=True)  3.88 us
    ppermute x1, starting transfers between devices, project(): near_down = lax.ppermute(near_down, 'ch', down)  3.22 us
    pallas_call x1, Pallas kernels, share(): pl.pallas_call(kernel, in_specs=[VMEM] * (len(arrays) - 1) + [HBM], out_s...  2.7 us
  transfers between devices with their start and end apart: 9, of which 9 were waited for; matrix products, arithmetic and copies ran while one was open for 1% of the time, Pallas kernels for 21%

profile of v5, /device:TPU:0, one launch (start us, length us, event | category | flops | bytes accessed | tf_op | source)
XLA Modules:
  0.0 65.6 jit_solution(4094782139640306870)
XLA Ops:
  0.0 2.2 %shard_map.82 = (bf16[32,96,128]{2,1,0:T(8,128)(2,1)}, bf16[16,1024]{1,0:T(8,128)(2,1)S(1)}) custom-call(bf16[3,128,1024]{2,1,0:T(8,128)(2,1)} %streams_ref.3, f32[128,1024]{1,0:T(8,128)} %filter_ref.1), custom_call_target="tpu_custom_call" | custom-call | tf_op jit(solution)/shard_map/pallas_call | solution.py:392
  2.2 8.3 %all-to-all-start = ((bf16[32,96,128]{2,1,0:T(8,128)(2,1)}), bf16[32,96,128]{2,1,0:T(8,128)(2,1)S(1)}, u32[]{:S(2)}, u32[]{:S(2)}) async-start(bf16[32,96,128]{2,1,0:T(8,128)(2,1)} %get-tuple-element.22), calls=%async_computation | async-start | bytes 1572864 | tf_op jit(solution)/shard_map/all_to_all | solution.py:409
  10.5 7.7 %shard_map.83 = (bf16[256,256]{1,0:T(8,128)(2,1)S(1)}, bf16[256,256]{1,0:T(8,128)(2,1)S(1)}, f32[32,2,128]{2,1,0:T(2,128)S(1)}, f32[3,3,1024]{2,1,0:T(4,128)S(1)...) custom-call(bf16[16,1024]{1,0:T(8,128)(2,1)S(1)} %get-tuple-element.23.refs_0_, ...), custom_call_target="tpu_custom_call" | custom-call | tf_op jit(solution)/shard_map/pallas_call | solution.py:354
  18.3 0.8 %dynamic_slice.7 = f32[32]{0:T(128)S(1)} dynamic-slice(f32[1024]{0:T(1024)} %param.11, s32[]{:T(128)S(6)} %select_n.4), dynamic_slice_sizes={32} | dynamic-slice | bytes 260 | tf_op jit(solution)/shard_map/dynamic_slice | solution.py:414
  19.1 0.1 constant_dynamic-slice_fusion
  19.1 5.9 %all-to-all-done.x_ref = bf16[32,96,128]{2,1,0:T(8,128)(2,1)S(1)} async-done(((bf16[32,96,128]{2,1,0:T(8,128)(2,1)}), bf16[32,96,128]{2,1,0:T(8,128)(2,1)S(1)}, u32[]{:S(2)}, u32[]{:S(2)}) %all-to-all-start) | async-done | bytes 786464 | tf_op jit(solution)/shard_map/all_to_all | solution.py:409
  25.1 0.1 broadcast_in_dim.5.skip_ref
  25.1 0.1 broadcast_in_dim.4.taps_ref
  25.2 4.4 %shard_map.84 = (bf16[32,32,128]{2,1,0:T(8,128)(2,1)}, bf16[1024,1152]{1,0:T(8,128)(2,1)S(1)}) custom-call(bf16[32,96,128]{2,1,0:T(8,128)(2,1)S(1)} %all-to-all-done.x_ref, f32[6,32,128]{2,1,0:T(8,128)S(1)} %broadcast_in_dim.4.taps_ref, f32[32,128]{1,0:T(8,128)S(1)} %broadcast_in_dim.5.skip_ref, bf16[256,256]{1,0:T(8,128)(2,1)S(1)} %get-tuple-element.25.high_ref, ...), custom_call_target="tpu_custom_call" | custom-call | tf_op jit(solution)/shard_map/pallas_call | solution.py:369
  29.6 3.9 %all-to-all-start.1 = ((bf16[32,32,128]{2,1,0:T(8,128)(2,1)}), bf16[32,32,128]{2,1,0:T(8,128)(2,1)S(1)}, u32[]{:S(2)}, u32[]{:S(2)}) async-start(bf16[32,32,128]{2,1,0:T(8,128)(2,1)} %get-tuple-element.28), calls=%async_computation.1 | async-start | bytes 524288 | tf_op jit(solution)/shard_map/all_to_all | solution.py:424
  33.5 2.1 %collective-permute-start = (bf16[16,1024]{1,0:T(8,128)(2,1)S(1)}, bf16[16,1024]{1,0:T(8,128)(2,1)S(1)}, u32[]{:S(2)}, u32[]{:S(2)}) collective-permute-start(bf16[16,1024]{1,0:T(8,128)(2,1)S(1)} %get-tuple-element.23.refs_0_), channel_id=1, source_target_pairs={{0,4},{4,8},{8,12},{12,16},{16,20},{20,24},{24,28},{28,32},{32,36}... | collective-permute-start | bytes 98312 | tf_op jit(solution)/shard_map/ppermute | solution.py:410
  35.6 0.8 %collective-permute-done.edge_ref = bf16[16,1024]{1,0:T(8,128)(2,1)S(1)} collective-permute-done((bf16[16,1024]{1,0:T(8,128)(2,1)S(1)}, bf16[16,1024]{1,0:T(8,128)(2,1)S(1)}, u32[]{:S(2)}, u32[]{:S(2)}) %collective-permute-start) | collective-permute-done | bytes 32800 | tf_op jit(solution)/shard_map/ppermute | solution.py:410
  36.4 1.2 %shard_map.85.query_ref = f32[128,1024]{1,0:T(8,128)S(1)} custom-call(bf16[3,128,1024]{2,1,0:T(8,128)(2,1)} %streams_ref.3, bf16[16,1024]{1,0:T(8,128)(2,1)S(1)} %collective-permute-done.edge_ref, f32[3,3,1024]{2,1,0:T(4,128)S(1)} %get-tuple-element.24.taps_ref, bf16[1024,1152]{1,0:T(8,128)(2,1)S(1)} %get-tuple-element.29.held_ref), custom_call_target="tpu_custom_call" | custom-call | tf_op jit(solution)/shard_map/pallas_call | solution.py:416
  37.6 4.8 %all-to-all-done.1 = bf16[32,32,128]{2,1,0:T(8,128)(2,1)S(1)} async-done(((bf16[32,32,128]{2,1,0:T(8,128)(2,1)}), bf16[32,32,128]{2,1,0:T(8,128)(2,1)S(1)}, u32[]{:S(2)}, u32[]{:S(2)}) %all-to-all-start.1) | async-done | bytes 262176 | tf_op jit(solution)/shard_map/all_to_all | solution.py:424
  42.4 0.0 copy-start.2
  42.4 0.5 shard_map.86
  43.0 0.0 copy-start.1
  43.0 1.6 %collective-permute-start.3 = (bf16[128,1152]{1,0:T(8,128)(2,1)S(1)}, bf16[128,1152]{1,0:T(8,128)(2,1)S(1)}, u32[]{:S(2)}, u32[]{:S(2)}) collective-permute-start(bf16[128,1152]{1,0:T(8,128)(2,1)S(1)} %get-tuple-element.35), channel_id=1, source_target_pairs={{0,1},{1,2},{2,3},{3,0},{4,5},{5,6},{6,7},{7,4},{8,9},{9,10},{10,1... | collective-permute-start | bytes 884744 | tf_op jit(solution)/shard_map/ppermute | solution.py:332
  44.6 0.0 copy-done.2
  44.6 0.4 shard_map.89
  45.1 0.0 copy-start
  45.1 2.4 %collective-permute-start.4 = (bf16[128,896]{1,0:T(8,128)(2,1)S(1)}, bf16[128,896]{1,0:T(8,128)(2,1)S(1)}, u32[]{:S(2)}, u32[]{:S(2)}) collective-permute-start(bf16[128,896]{1,0:T(8,128)(2,1)S(1)} %shard_map.89), channel_id=1, source_target_pairs={{0,3},{1,0},{2,1},{3,2},{4,7},{5,4},{6,5},{7,6},{8,11},{9,8},{10,9... | collective-permute-start | bytes 688136 | tf_op jit(solution)/shard_map/ppermute | solution.py:334
  47.5 0.0 copy-done.1
  47.5 0.8 %shard_map.87 = (bf16[128,896]{1,0:T(8,128)(2,1)S(1)}, bf16[128,1152]{1,0:T(8,128)(2,1)S(1)}) custom-call(bf16[128,1024]{1,0:T(8,128)(2,1)S(1)} %get-tuple-element.30.rows_ref, bf16[1024,2048]{1,0:T(8,128)(2,1)S(1)} %copy-done.1), custom_call_target="tpu_custom_call" | custom-call | flops 2147483648 | bytes 2097152 | tf_op jit(solution)/shard_map/pallas_call | solution.py:317
  48.3 0.1 collective-permute-start.1
  48.4 3.2 %collective-permute-start.2 = (bf16[128,1152]{1,0:T(8,128)(2,1)S(1)}, bf16[128,1152]{1,0:T(8,128)(2,1)S(1)}, u32[]{:S(2)}, u32[]{:S(2)}) collective-permute-start(bf16[128,1152]{1,0:T(8,128)(2,1)S(1)} %get-tuple-element.33), channel_id=1, source_target_pairs={{0,3},{1,0},{2,1},{3,2},{4,7},{5,4},{6,5},{7,6},{8,11},{9,8},{10,9... | collective-permute-start | bytes 884744 | tf_op jit(solution)/shard_map/ppermute | solution.py:337
  51.6 2.0 %collective-permute-done.4.far_down_ref = bf16[128,896]{1,0:T(8,128)(2,1)S(1)} collective-permute-done((bf16[128,896]{1,0:T(8,128)(2,1)S(1)}, bf16[128,896]{1,0:T(8,128)(2,1)S(1)}, u32[]{:S(2)}, u32[]{:S(2)}) %collective-permute-start.4) | collective-permute-done | bytes 229408 | tf_op jit(solution)/shard_map/ppermute | solution.py:334
  53.6 0.5 collective-permute-done.3.far_up_ref
  54.1 0.0 copy-done
  54.1 0.8 %shard_map.90 = (bf16[128,1152]{1,0:T(8,128)(2,1)S(1)}, bf16[128,896]{1,0:T(8,128)(2,1)S(1)}) custom-call(bf16[128,1024]{1,0:T(8,128)(2,1)S(1)} %get-tuple-element.30.rows_ref, bf16[1024,2048]{1,0:T(8,128)(2,1)S(1)} %copy-done, bf16[128,1152]{1,0:T(8,128)(2,1)S(1)} %collective-permute-done.3.far_up_ref, bf16[128,896]{1,0:T(8,128)(2,1)S(1)} %collective-permute-done.4.far_down_ref), custom_call_target="tpu_custom_call" | custom-call | flops 2147483648 | bytes 2097152 | tf_op jit(solution)/shard_map/pallas_call | solution.py:317
  54.9 1.2 %collective-permute-start.5 = (bf16[128,1152]{1,0:T(8,128)(2,1)S(1)}, bf16[128,1152]{1,0:T(8,128)(2,1)S(1)}, u32[]{:S(2)}, u32[]{:S(2)}) collective-permute-start(bf16[128,1152]{1,0:T(8,128)(2,1)S(1)} %get-tuple-element.37), channel_id=1, source_target_pairs={{0,1},{1,2},{2,3},{3,0},{4,5},{5,6},{6,7},{7,4},{8,9},{9,10},{10,1... | collective-permute-start | bytes 884744 | tf_op jit(solution)/shard_map/ppermute | solution.py:339
  56.1 2.1 %collective-permute-start.6 = (bf16[128,896]{1,0:T(8,128)(2,1)S(1)}, bf16[128,896]{1,0:T(8,128)(2,1)S(1)}, u32[]{:S(2)}, u32[]{:S(2)}) collective-permute-start(bf16[128,896]{1,0:T(8,128)(2,1)S(1)} %get-tuple-element.38), channel_id=1, source_target_pairs={{0,3},{1,0},{2,1},{3,2},{4,7},{5,4},{6,5},{7,6},{8,11},{9,8},{10,9... | collective-permute-start | bytes 688136 | tf_op jit(solution)/shard_map/ppermute | solution.py:340
  58.2 0.8 %collective-permute-done.1.near_up_ref = bf16[128,896]{1,0:T(8,128)(2,1)S(1)} collective-permute-done((bf16[128,896]{1,0:T(8,128)(2,1)S(1)}, bf16[128,896]{1,0:T(8,128)(2,1)S(1)}, u32[]{:S(2)}, u32[]{:S(2)}) %collective-permute-start.1) | collective-permute-done | bytes 229408 | tf_op jit(solution)/shard_map/ppermute | solution.py:336
  59.0 0.9 %collective-permute-done.2.near_down_ref = bf16[128,1152]{1,0:T(8,128)(2,1)S(1)} collective-permute-done((bf16[128,1152]{1,0:T(8,128)(2,1)S(1)}, bf16[128,1152]{1,0:T(8,128)(2,1)S(1)}, u32[]{:S(2)}, u32[]{:S(2)}) %collective-permute-start.2) | collective-permute-done | bytes 294944 | tf_op jit(solution)/shard_map/ppermute | solution.py:337
  60.0 2.7 %shard_map.88.own_ref = f32[128,2048]{1,0:T(8,128)S(1)} custom-call(bf16[128,1024]{1,0:T(8,128)(2,1)S(1)} %get-tuple-element.30.rows_ref, bf16[128,896]{1,0:T(8,128)(2,1)S(1)} %collective-permute-done.1.near_up_ref, bf16[128,1152]{1,0:T(8,128)(2,1)S(1)} %collective-permute-done.2.near_down_ref, bf16[1024,8192]{1,0:T(8,128)(2,1)} %weights_ref.3), custom_call_target="tpu_custom_call" | custom-call | flops 2147483648 | bytes 2097152 | tf_op jit(solution)/shard_map/pallas_call | solution.py:302
  62.7 1.4 %collective-permute-done.6.both_down_ref = bf16[128,896]{1,0:T(8,128)(2,1)S(1)} collective-permute-done((bf16[128,896]{1,0:T(8,128)(2,1)S(1)}, bf16[128,896]{1,0:T(8,128)(2,1)S(1)}, u32[]{:S(2)}, u32[]{:S(2)}) %collective-permute-start.6) | collective-permute-done | bytes 229408 | tf_op jit(solution)/shard_map/ppermute | solution.py:340
  64.0 0.7 %collective-permute-done.5.both_up_ref = bf16[128,1152]{1,0:T(8,128)(2,1)S(1)} collective-permute-done((bf16[128,1152]{1,0:T(8,128)(2,1)S(1)}, bf16[128,1152]{1,0:T(8,128)(2,1)S(1)}, u32[]{:S(2)}, u32[]{:S(2)}) %collective-permute-start.5) | collective-permute-done | bytes 294944 | tf_op jit(solution)/shard_map/ppermute | solution.py:339
  64.8 0.9 %shard_map.91 = bf16[128,2048]{1,0:T(8,128)(2,1)} custom-call(f32[128,2048]{1,0:T(8,128)S(1)} %shard_map.88.own_ref, bf16[128,1152]{1,0:T(8,128)(2,1)S(1)} %collective-permute-done.5.both_up_ref, bf16[128,896]{1,0:T(8,128)(2,1)S(1)} %collective-permute-done.6.both_down_ref), custom_call_target="tpu_custom_call" | custom-call | tf_op jit(solution)/shard_map/pallas_call | solution.py:342
  (2 shorter events, 0.0 us)
Async XLA Ops:
  2.2 22.8 %all-to-all-start = ((bf16[32,96,128]{2,1,0:T(8,128)(2,1)}), bf16[32,96,128]{2,1,0:T(8,128)(2,1)S(1)}, u32[]{:S(2)}, u32[]{:S(2)}) async-start(bf16[32,96,128]{2,1,0:T(8,128)(2,1)} %get-tuple-element.22), calls=%async_computation | async-start | bytes 1572864 | tf_op jit(solution)/shard_map/all_to_all | solution.py:409
  29.6 12.8 %all-to-all-start.1 = ((bf16[32,32,128]{2,1,0:T(8,128)(2,1)}), bf16[32,32,128]{2,1,0:T(8,128)(2,1)S(1)}, u32[]{:S(2)}, u32[]{:S(2)}) async-start(bf16[32,32,128]{2,1,0:T(8,128)(2,1)} %get-tuple-element.28), calls=%async_computation.1 | async-start | bytes 524288 | tf_op jit(solution)/shard_map/all_to_all | solution.py:424
  33.5 2.9 %collective-permute-start = (bf16[16,1024]{1,0:T(8,128)(2,1)S(1)}, bf16[16,1024]{1,0:T(8,128)(2,1)S(1)}, u32[]{:S(2)}, u32[]{:S(2)}) collective-permute-start(bf16[16,1024]{1,0:T(8,128)(2,1)S(1)} %get-tuple-element.23.refs_0_), channel_id=1, source_target_pairs={{0,4},{4,8},{8,12},{12,16},{16,20},{20,24},{24,28},{28,32},{32,36}... | collective-permute-start | bytes 98312 | tf_op jit(solution)/shard_map/ppermute | solution.py:410
  42.4 2.2 %copy-start.2 = (bf16[1024,896]{1,0:T(8,128)(2,1)S(1)}, bf16[1024,896]{1,0:T(8,128)(2,1)}, u32[]{:S(2)}) copy-start(bf16[1024,896]{1,0:T(8,128)(2,1)} %get-tuple-element.36.rest_ref) | copy-start | bytes 5505028
  43.0 4.5 %copy-start.1 = (bf16[1024,2048]{1,0:T(8,128)(2,1)S(1)}, bf16[1024,2048]{1,0:T(8,128)(2,1)}, u32[]{:S(2)}) copy-start(bf16[1024,2048]{1,0:T(8,128)(2,1)} %get-tuple-element.31.near_ref) | copy-start | bytes 12582916
  43.0 11.1 %collective-permute-start.3 = (bf16[128,1152]{1,0:T(8,128)(2,1)S(1)}, bf16[128,1152]{1,0:T(8,128)(2,1)S(1)}, u32[]{:S(2)}, u32[]{:S(2)}) collective-permute-start(bf16[128,1152]{1,0:T(8,128)(2,1)S(1)} %get-tuple-element.35), channel_id=1, source_target_pairs={{0,1},{1,2},{2,3},{3,0},{4,5},{5,6},{6,7},{7,4},{8,9},{9,10},{10,1... | collective-permute-start | bytes 884744 | tf_op jit(solution)/shard_map/ppermute | solution.py:332
  45.1 9.0 %copy-start = (bf16[1024,2048]{1,0:T(8,128)(2,1)S(1)}, bf16[1024,2048]{1,0:T(8,128)(2,1)}, u32[]{:S(2)}) copy-start(bf16[1024,2048]{1,0:T(8,128)(2,1)} %get-tuple-element.34.later_ref) | copy-start | bytes 12582916
  45.1 8.5 %collective-permute-start.4 = (bf16[128,896]{1,0:T(8,128)(2,1)S(1)}, bf16[128,896]{1,0:T(8,128)(2,1)S(1)}, u32[]{:S(2)}, u32[]{:S(2)}) collective-permute-start(bf16[128,896]{1,0:T(8,128)(2,1)S(1)} %shard_map.89), channel_id=1, source_target_pairs={{0,3},{1,0},{2,1},{3,2},{4,7},{5,4},{6,5},{7,6},{8,11},{9,8},{10,9... | collective-permute-start | bytes 688136 | tf_op jit(solution)/shard_map/ppermute | solution.py:334
  48.3 10.7 %collective-permute-start.1 = (bf16[128,896]{1,0:T(8,128)(2,1)S(1)}, bf16[128,896]{1,0:T(8,128)(2,1)S(1)}, u32[]{:S(2)}, u32[]{:S(2)}) collective-permute-start(bf16[128,896]{1,0:T(8,128)(2,1)S(1)} %get-tuple-element.32), channel_id=1, source_target_pairs={{0,1},{1,2},{2,3},{3,0},{4,5},{5,6},{6,7},{7,4},{8,9},{9,10},{10,1... | collective-permute-start | bytes 688136 | tf_op jit(solution)/shard_map/ppermute | solution.py:336
  48.4 11.6 %collective-permute-start.2 = (bf16[128,1152]{1,0:T(8,128)(2,1)S(1)}, bf16[128,1152]{1,0:T(8,128)(2,1)S(1)}, u32[]{:S(2)}, u32[]{:S(2)}) collective-permute-start(bf16[128,1152]{1,0:T(8,128)(2,1)S(1)} %get-tuple-element.33), channel_id=1, source_target_pairs={{0,3},{1,0},{2,1},{3,2},{4,7},{5,4},{6,5},{7,6},{8,11},{9,8},{10,9... | collective-permute-start | bytes 884744 | tf_op jit(solution)/shard_map/ppermute | solution.py:337
  54.9 9.8 %collective-permute-start.5 = (bf16[128,1152]{1,0:T(8,128)(2,1)S(1)}, bf16[128,1152]{1,0:T(8,128)(2,1)S(1)}, u32[]{:S(2)}, u32[]{:S(2)}) collective-permute-start(bf16[128,1152]{1,0:T(8,128)(2,1)S(1)} %get-tuple-element.37), channel_id=1, source_target_pairs={{0,1},{1,2},{2,3},{3,0},{4,5},{5,6},{6,7},{7,4},{8,9},{9,10},{10,1... | collective-permute-start | bytes 884744 | tf_op jit(solution)/shard_map/ppermute | solution.py:339
  56.1 7.9 %collective-permute-start.6 = (bf16[128,896]{1,0:T(8,128)(2,1)S(1)}, bf16[128,896]{1,0:T(8,128)(2,1)S(1)}, u32[]{:S(2)}, u32[]{:S(2)}) collective-permute-start(bf16[128,896]{1,0:T(8,128)(2,1)S(1)} %get-tuple-element.38), channel_id=1, source_target_pairs={{0,3},{1,0},{2,1},{3,2},{4,7},{5,4},{6,5},{7,6},{8,11},{9,8},{10,9... | collective-permute-start | bytes 688136 | tf_op jit(solution)/shard_map/ppermute | solution.py:340

commit v6 on v5

--- a/solution.py
+++ b/solution.py
@@ -69,7 +69,7 @@
     return [plus(a, b) for a, b in zip(even, odd)] + [minus(a, b) for a, b in zip(even, odd)]
 
 
-def exchange_kernel(streams_ref, filter_ref, out_ref, edge_ref, rows_ref, taps_ref, sems):
+def exchange_kernel(streams_ref, filter_ref, out_ref, edge_ref, rows_ref, taps_ref, packed_ref, sems, out_sems):
     copies = [pltpu.make_async_copy(streams_ref.at[i + 1], rows_ref.at[i], sems.at[i]) for i in range(SENT - 1)]
     copies.append(pltpu.make_async_copy(filter_ref, taps_ref, sems.at[SENT - 1]))
     edge = pltpu.make_async_copy(streams_ref.at[0, ROWS - EDGE :], edge_ref, sems.at[SENT])
@@ -77,14 +77,20 @@
         copy.start()
     edge.start()
     wide = 8 * GROUP
+    leaving = []
     for j, copy in enumerate(copies):
         copy.wait()
         for first in range(0, PARTS * GROUP, wide):
             here = slice(first, first + wide)
             block = rows_ref[j, :, here] if j < SENT - 1 else taps_ref[:, here].astype(bf16)
             parts = pl.ds(first // GROUP, wide // GROUP)
-            out_ref[parts, j * GROUP : (j + 1) * GROUP, :] = block.T.reshape(wide // GROUP, GROUP, ROWS)
+            packed_ref[parts, j * GROUP : (j + 1) * GROUP, :] = block.T.reshape(wide // GROUP, GROUP, ROWS)
+        own = (slice(None), slice(j * GROUP, (j + 1) * GROUP))
+        leaving.append(pltpu.make_async_copy(packed_ref.at[own], out_ref.at[own], out_sems.at[j]))
+        leaving[-1].start()
     edge.wait()
+    for copy in leaving:
+        copy.wait()
 
 
 def stage_kernel(*refs):
@@ -281,11 +287,19 @@
         out_ref[:, start:stop] = part_of(rows_ref, held_ref, start, stop) + arrived.astype(f32)
 
 
-def last_kernel(own_ref, both_up_ref, both_down_ref, out_ref):
-    for part, arrived_ref in ((slice(0, UP), both_up_ref), (slice(UP, WIDE), both_down_ref)):
-        out_ref[:, part] = (own_ref[:, part] + arrived_ref[...].astype(f32)).astype(bf16)
-
-
+def last_kernel(own_ref, both_up_ref, both_down_ref, out_ref, rows_ref, sems):
+    copies = []
+    for start in range(0, ROWS, LAST):
+        here = slice(start, start + LAST)
+        for part, arrived_ref in ((slice(0, UP), both_up_ref), (slice(UP, WIDE), both_down_ref)):
+            rows_ref[here, part] = (own_ref[here, part] + arrived_ref[here, :].astype(f32)).astype(bf16)
+        copies.append(pltpu.make_async_copy(rows_ref.at[here], out_ref.at[here], sems.at[start // LAST]))
+        copies[-1].start()
+    for copy in copies:
+        copy.wait()
+
+
+LAST = 32
 TABLES = 4
 RING = 4
 WIDE = 2048
@@ -342,8 +356,9 @@
     return pl.pallas_call(
         last_kernel,
         in_specs=[VMEM] * 3,
-        out_specs=VMEM,
+        out_specs=HBM,
         out_shape=jax.ShapeDtypeStruct((ROWS, WIDE), bf16),
+        scratch_shapes=[pltpu.VMEM((ROWS, WIDE), bf16), pltpu.SemaphoreType.DMA((ROWS // LAST,))],
         compiler_params=pltpu.CompilerParams(vmem_limit_bytes=16 * 2**20),
     )(own, both_up, both_down)
 
@@ -392,15 +407,17 @@
     packed, edge = pl.pallas_call(
         exchange_kernel,
         in_specs=[HBM, HBM],
-        out_specs=[VMEM, VMEM],
+        out_specs=[HBM, VMEM],
         out_shape=[
-            pltpu.VMEM((PARTS, SENT * GROUP, ROWS), bf16),
+            pltpu.HBM((PARTS, SENT * GROUP, ROWS), bf16),
             pltpu.VMEM((EDGE, channels), bf16),
         ],
         scratch_shapes=[
             pltpu.VMEM((SENT - 1, ROWS, channels), bf16),
             pltpu.VMEM((ROWS, channels), f32),
+            pltpu.VMEM((PARTS, SENT * GROUP, ROWS), bf16),
             pltpu.SemaphoreType.DMA((SENT + 1,)),
+            pltpu.SemaphoreType.DMA((SENT,)),
         ],
         compiler_params=pltpu.CompilerParams(vmem_limit_bytes=8 * 2**20),
     )(streams, pltpu.with_memory_space_constraint(long_filter, pltpu.HBM))

time: 66 us -> 65.9 us (level)
  no operation moved by 1% of the time
where the time goes in v6:
time: 65.9 us; the launch traced here: 65.5 us
  starting transfers between devices  24.8 us (38%)
  Pallas kernels  21.6 us (33%)
  waiting for transfers between devices  17.9 us (27%)
  local copies, waits for them, and re-layouts  1.02 us (2%)
    all_to_all x1, starting transfers between devices, on_device(): arrived = lax.all_to_all(packed, 'seq', 0, 0, tiled=True)  8.26 us
    pallas_call x1, Pallas kernels, stage(): pl.pallas_call(stage_kernel, in_specs=[pl.BlockSpec(memory_space=pl.ANY)]...  7.74 us
    all_to_all x1, waiting for transfers between devices, on_device(): arrived = lax.all_to_all(packed, 'seq', 0, 0, tiled=True)  5.93 us
    all_to_all x1, waiting for transfers between devices, on_device(): outer = lax.all_to_all(outer, 'seq', 0, 0, tiled=True)  4.82 us
    pallas_call x1, Pallas kernels, convolve(): pl.pallas_call(conv_kernel, in_specs=[VMEM] * 6 + [HBM], out_specs=[VMEM,...  4.4 us
    all_to_all x1, starting transfers between devices, on_device(): outer = lax.all_to_all(outer, 'seq', 0, 0, tiled=True)  3.88 us
    ppermute x1, starting transfers between devices, project(): near_down = lax.ppermute(near_down, 'ch', down)  3.22 us
    pallas_call x1, Pallas kernels, share(): pl.pallas_call(kernel, in_specs=[VMEM] * (len(arrays) - 1) + [HBM], out_s...  2.7 us
  transfers between devices with their start and end apart: 9, of which 9 were waited for; matrix products, arithmetic and copies ran while one was open for 1% of the time, Pallas kernels for 21%

profile of v6, /device:TPU:0, one launch (start us, length us, event | category | flops | bytes accessed | tf_op | source)
XLA Modules:
  0.0 65.5 jit_solution(4175990821325414994)
XLA Ops:
  0.0 2.1 %shard_map.82 = (bf16[32,96,128]{2,1,0:T(8,128)(2,1)}, bf16[16,1024]{1,0:T(8,128)(2,1)S(1)}) custom-call(bf16[3,128,1024]{2,1,0:T(8,128)(2,1)} %streams_ref.3, f32[128,1024]{1,0:T(8,128)} %filter_ref.1), custom_call_target="tpu_custom_call" | custom-call | tf_op jit(solution)/shard_map/pallas_call | solution.py:407
  2.1 8.3 %all-to-all-start = ((bf16[32,96,128]{2,1,0:T(8,128)(2,1)}), bf16[32,96,128]{2,1,0:T(8,128)(2,1)S(1)}, u32[]{:S(2)}, u32[]{:S(2)}) async-start(bf16[32,96,128]{2,1,0:T(8,128)(2,1)} %get-tuple-element.22), calls=%async_computation | async-start | bytes 1572864 | tf_op jit(solution)/shard_map/all_to_all | solution.py:426
  10.4 7.7 %shard_map.83 = (bf16[256,256]{1,0:T(8,128)(2,1)S(1)}, bf16[256,256]{1,0:T(8,128)(2,1)S(1)}, f32[32,2,128]{2,1,0:T(2,128)S(1)}, f32[3,3,1024]{2,1,0:T(4,128)S(1)...) custom-call(bf16[16,1024]{1,0:T(8,128)(2,1)S(1)} %get-tuple-element.23.refs_0_, ...), custom_call_target="tpu_custom_call" | custom-call | tf_op jit(solution)/shard_map/pallas_call | solution.py:369
  18.2 0.8 %dynamic_slice.7 = f32[32]{0:T(128)S(1)} dynamic-slice(f32[1024]{0:T(1024)} %param.11, s32[]{:T(128)S(6)} %select_n.4), dynamic_slice_sizes={32} | dynamic-slice | bytes 260 | tf_op jit(solution)/shard_map/dynamic_slice | solution.py:431
  18.9 0.1 constant_dynamic-slice_fusion
  19.0 5.9 %all-to-all-done.x_ref = bf16[32,96,128]{2,1,0:T(8,128)(2,1)S(1)} async-done(((bf16[32,96,128]{2,1,0:T(8,128)(2,1)}), bf16[32,96,128]{2,1,0:T(8,128)(2,1)S(1)}, u32[]{:S(2)}, u32[]{:S(2)}) %all-to-all-start) | async-done | bytes 786464 | tf_op jit(solution)/shard_map/all_to_all | solution.py:426
  24.9 0.1 broadcast_in_dim.5.skip_ref
  25.0 0.1 broadcast_in_dim.4.taps_ref
  25.1 4.4 %shard_map.84 = (bf16[32,32,128]{2,1,0:T(8,128)(2,1)}, bf16[1024,1152]{1,0:T(8,128)(2,1)S(1)}) custom-call(bf16[32,96,128]{2,1,0:T(8,128)(2,1)S(1)} %all-to-all-done.x_ref, f32[6,32,128]{2,1,0:T(8,128)S(1)} %broadcast_in_dim.4.taps_ref, f32[32,128]{1,0:T(8,128)S(1)} %broadcast_in_dim.5.skip_ref, bf16[256,256]{1,0:T(8,128)(2,1)S(1)} %get-tuple-element.25.high_ref, ...), custom_call_target="tpu_custom_call" | custom-call | tf_op jit(solution)/shard_map/pallas_call | solution.py:384
  29.5 3.9 %all-to-all-start.1 = ((bf16[32,32,128]{2,1,0:T(8,128)(2,1)}), bf16[32,32,128]{2,1,0:T(8,128)(2,1)S(1)}, u32[]{:S(2)}, u32[]{:S(2)}) async-start(bf16[32,32,128]{2,1,0:T(8,128)(2,1)} %get-tuple-element.28), calls=%async_computation.1 | async-start | bytes 524288 | tf_op jit(solution)/shard_map/all_to_all | solution.py:441
  33.4 2.1 %collective-permute-start = (bf16[16,1024]{1,0:T(8,128)(2,1)S(1)}, bf16[16,1024]{1,0:T(8,128)(2,1)S(1)}, u32[]{:S(2)}, u32[]{:S(2)}) collective-permute-start(bf16[16,1024]{1,0:T(8,128)(2,1)S(1)} %get-tuple-element.23.refs_0_), channel_id=1, source_target_pairs={{0,4},{4,8},{8,12},{12,16},{16,20},{20,24},{24,28},{28,32},{32,36}... | collective-permute-start | bytes 98312 | tf_op jit(solution)/shard_map/ppermute | solution.py:427
  35.5 0.8 %collective-permute-done.edge_ref = bf16[16,1024]{1,0:T(8,128)(2,1)S(1)} collective-permute-done((bf16[16,1024]{1,0:T(8,128)(2,1)S(1)}, bf16[16,1024]{1,0:T(8,128)(2,1)S(1)}, u32[]{:S(2)}, u32[]{:S(2)}) %collective-permute-start) | collective-permute-done | bytes 32800 | tf_op jit(solution)/shard_map/ppermute | solution.py:427
  36.3 1.2 %shard_map.85.query_ref = f32[128,1024]{1,0:T(8,128)S(1)} custom-call(bf16[3,128,1024]{2,1,0:T(8,128)(2,1)} %streams_ref.3, bf16[16,1024]{1,0:T(8,128)(2,1)S(1)} %collective-permute-done.edge_ref, f32[3,3,1024]{2,1,0:T(4,128)S(1)} %get-tuple-element.24.taps_ref, bf16[1024,1152]{1,0:T(8,128)(2,1)S(1)} %get-tuple-element.29.held_ref), custom_call_target="tpu_custom_call" | custom-call | tf_op jit(solution)/shard_map/pallas_call | solution.py:433
  37.5 4.8 %all-to-all-done.1 = bf16[32,32,128]{2,1,0:T(8,128)(2,1)S(1)} async-done(((bf16[32,32,128]{2,1,0:T(8,128)(2,1)}), bf16[32,32,128]{2,1,0:T(8,128)(2,1)S(1)}, u32[]{:S(2)}, u32[]{:S(2)}) %all-to-all-start.1) | async-done | bytes 262176 | tf_op jit(solution)/shard_map/all_to_all | solution.py:441
  42.3 0.0 copy-start.2
  42.3 0.5 shard_map.86
  42.9 0.0 copy-start.1
  42.9 1.6 %collective-permute-start.3 = (bf16[128,1152]{1,0:T(8,128)(2,1)S(1)}, bf16[128,1152]{1,0:T(8,128)(2,1)S(1)}, u32[]{:S(2)}, u32[]{:S(2)}) collective-permute-start(bf16[128,1152]{1,0:T(8,128)(2,1)S(1)} %get-tuple-element.35), channel_id=1, source_target_pairs={{0,1},{1,2},{2,3},{3,0},{4,5},{5,6},{6,7},{7,4},{8,9},{9,10},{10,1... | collective-permute-start | bytes 884744 | tf_op jit(solution)/shard_map/ppermute | solution.py:346
  44.5 0.0 copy-done.2
  44.5 0.4 shard_map.89
  45.0 0.0 copy-start
  45.0 2.4 %collective-permute-start.4 = (bf16[128,896]{1,0:T(8,128)(2,1)S(1)}, bf16[128,896]{1,0:T(8,128)(2,1)S(1)}, u32[]{:S(2)}, u32[]{:S(2)}) collective-permute-start(bf16[128,896]{1,0:T(8,128)(2,1)S(1)} %shard_map.89), channel_id=1, source_target_pairs={{0,3},{1,0},{2,1},{3,2},{4,7},{5,4},{6,5},{7,6},{8,11},{9,8},{10,9... | collective-permute-start | bytes 688136 | tf_op jit(solution)/shard_map/ppermute | solution.py:348
  47.4 0.0 copy-done.1
  47.4 0.8 %shard_map.87 = (bf16[128,896]{1,0:T(8,128)(2,1)S(1)}, bf16[128,1152]{1,0:T(8,128)(2,1)S(1)}) custom-call(bf16[128,1024]{1,0:T(8,128)(2,1)S(1)} %get-tuple-element.30.rows_ref, bf16[1024,2048]{1,0:T(8,128)(2,1)S(1)} %copy-done.1), custom_call_target="tpu_custom_call" | custom-call | flops 2147483648 | bytes 2097152 | tf_op jit(solution)/shard_map/pallas_call | solution.py:331
  48.2 0.1 collective-permute-start.1
  48.2 3.2 %collective-permute-start.2 = (bf16[128,1152]{1,0:T(8,128)(2,1)S(1)}, bf16[128,1152]{1,0:T(8,128)(2,1)S(1)}, u32[]{:S(2)}, u32[]{:S(2)}) collective-permute-start(bf16[128,1152]{1,0:T(8,128)(2,1)S(1)} %get-tuple-element.33), channel_id=1, source_target_pairs={{0,3},{1,0},{2,1},{3,2},{4,7},{5,4},{6,5},{7,6},{8,11},{9,8},{10,9... | collective-permute-start | bytes 884744 | tf_op jit(solution)/shard_map/ppermute | solution.py:351
  51.5 2.1 %collective-permute-done.4.far_down_ref = bf16[128,896]{1,0:T(8,128)(2,1)S(1)} collective-permute-done((bf16[128,896]{1,0:T(8,128)(2,1)S(1)}, bf16[128,896]{1,0:T(8,128)(2,1)S(1)}, u32[]{:S(2)}, u32[]{:S(2)}) %collective-permute-start.4) | collective-permute-done | bytes 229408 | tf_op jit(solution)/shard_map/ppermute | solution.py:348
  53.5 0.4 collective-permute-done.3.far_up_ref
  54.0 0.0 copy-done
  54.0 0.8 %shard_map.90 = (bf16[128,1152]{1,0:T(8,128)(2,1)S(1)}, bf16[128,896]{1,0:T(8,128)(2,1)S(1)}) custom-call(bf16[128,1024]{1,0:T(8,128)(2,1)S(1)} %get-tuple-element.30.rows_ref, bf16[1024,2048]{1,0:T(8,128)(2,1)S(1)} %copy-done, bf16[128,1152]{1,0:T(8,128)(2,1)S(1)} %collective-permute-done.3.far_up_ref, bf16[128,896]{1,0:T(8,128)(2,1)S(1)} %collective-permute-done.4.far_down_ref), custom_call_target="tpu_custom_call" | custom-call | flops 2147483648 | bytes 2097152 | tf_op jit(solution)/shard_map/pallas_call | solution.py:331
  54.8 1.2 %collective-permute-start.5 = (bf16[128,1152]{1,0:T(8,128)(2,1)S(1)}, bf16[128,1152]{1,0:T(8,128)(2,1)S(1)}, u32[]{:S(2)}, u32[]{:S(2)}) collective-permute-start(bf16[128,1152]{1,0:T(8,128)(2,1)S(1)} %get-tuple-element.37), channel_id=1, source_target_pairs={{0,1},{1,2},{2,3},{3,0},{4,5},{5,6},{6,7},{7,4},{8,9},{9,10},{10,1... | collective-permute-start | bytes 884744 | tf_op jit(solution)/shard_map/ppermute | solution.py:353
  56.0 2.1 %collective-permute-start.6 = (bf16[128,896]{1,0:T(8,128)(2,1)S(1)}, bf16[128,896]{1,0:T(8,128)(2,1)S(1)}, u32[]{:S(2)}, u32[]{:S(2)}) collective-permute-start(bf16[128,896]{1,0:T(8,128)(2,1)S(1)} %get-tuple-element.38), channel_id=1, source_target_pairs={{0,3},{1,0},{2,1},{3,2},{4,7},{5,4},{6,5},{7,6},{8,11},{9,8},{10,9... | collective-permute-start | bytes 688136 | tf_op jit(solution)/shard_map/ppermute | solution.py:354
  58.1 0.8 %collective-permute-done.1.near_up_ref = bf16[128,896]{1,0:T(8,128)(2,1)S(1)} collective-permute-done((bf16[128,896]{1,0:T(8,128)(2,1)S(1)}, bf16[128,896]{1,0:T(8,128)(2,1)S(1)}, u32[]{:S(2)}, u32[]{:S(2)}) %collective-permute-start.1) | collective-permute-done | bytes 229408 | tf_op jit(solution)/shard_map/ppermute | solution.py:350
  58.9 1.0 %collective-permute-done.2.near_down_ref = bf16[128,1152]{1,0:T(8,128)(2,1)S(1)} collective-permute-done((bf16[128,1152]{1,0:T(8,128)(2,1)S(1)}, bf16[128,1152]{1,0:T(8,128)(2,1)S(1)}, u32[]{:S(2)}, u32[]{:S(2)}) %collective-permute-start.2) | collective-permute-done | bytes 294944 | tf_op jit(solution)/shard_map/ppermute | solution.py:351
  59.8 2.7 %shard_map.88.own_ref = f32[128,2048]{1,0:T(8,128)S(1)} custom-call(bf16[128,1024]{1,0:T(8,128)(2,1)S(1)} %get-tuple-element.30.rows_ref, bf16[128,896]{1,0:T(8,128)(2,1)S(1)} %collective-permute-done.1.near_up_ref, bf16[128,1152]{1,0:T(8,128)(2,1)S(1)} %collective-permute-done.2.near_down_ref, bf16[1024,8192]{1,0:T(8,128)(2,1)} %weights_ref.3), custom_call_target="tpu_custom_call" | custom-call | flops 2147483648 | bytes 2097152 | tf_op jit(solution)/shard_map/pallas_call | solution.py:316
  62.6 1.3 %collective-permute-done.6.both_down_ref = bf16[128,896]{1,0:T(8,128)(2,1)S(1)} collective-permute-done((bf16[128,896]{1,0:T(8,128)(2,1)S(1)}, bf16[128,896]{1,0:T(8,128)(2,1)S(1)}, u32[]{:S(2)}, u32[]{:S(2)}) %collective-permute-start.6) | collective-permute-done | bytes 229408 | tf_op jit(solution)/shard_map/ppermute | solution.py:354
  63.9 0.7 %collective-permute-done.5.both_up_ref = bf16[128,1152]{1,0:T(8,128)(2,1)S(1)} collective-permute-done((bf16[128,1152]{1,0:T(8,128)(2,1)S(1)}, bf16[128,1152]{1,0:T(8,128)(2,1)S(1)}, u32[]{:S(2)}, u32[]{:S(2)}) %collective-permute-start.5) | collective-permute-done | bytes 294944 | tf_op jit(solution)/shard_map/ppermute | solution.py:353
  64.6 0.8 %shard_map.91 = bf16[128,2048]{1,0:T(8,128)(2,1)} custom-call(f32[128,2048]{1,0:T(8,128)S(1)} %shard_map.88.own_ref, bf16[128,1152]{1,0:T(8,128)(2,1)S(1)} %collective-permute-done.5.both_up_ref, bf16[128,896]{1,0:T(8,128)(2,1)S(1)} %collective-permute-done.6.both_down_ref), custom_call_target="tpu_custom_call" | custom-call | tf_op jit(solution)/shard_map/pallas_call | solution.py:356
  (2 shorter events, 0.0 us)
Async XLA Ops:
  2.1 22.8 %all-to-all-start = ((bf16[32,96,128]{2,1,0:T(8,128)(2,1)}), bf16[32,96,128]{2,1,0:T(8,128)(2,1)S(1)}, u32[]{:S(2)}, u32[]{:S(2)}) async-start(bf16[32,96,128]{2,1,0:T(8,128)(2,1)} %get-tuple-element.22), calls=%async_computation | async-start | bytes 1572864 | tf_op jit(solution)/shard_map/all_to_all | solution.py:426
  29.5 12.8 %all-to-all-start.1 = ((bf16[32,32,128]{2,1,0:T(8,128)(2,1)}), bf16[32,32,128]{2,1,0:T(8,128)(2,1)S(1)}, u32[]{:S(2)}, u32[]{:S(2)}) async-start(bf16[32,32,128]{2,1,0:T(8,128)(2,1)} %get-tuple-element.28), calls=%async_computation.1 | async-start | bytes 524288 | tf_op jit(solution)/shard_map/all_to_all | solution.py:441
  33.4 2.9 %collective-permute-start = (bf16[16,1024]{1,0:T(8,128)(2,1)S(1)}, bf16[16,1024]{1,0:T(8,128)(2,1)S(1)}, u32[]{:S(2)}, u32[]{:S(2)}) collective-permute-start(bf16[16,1024]{1,0:T(8,128)(2,1)S(1)} %get-tuple-element.23.refs_0_), channel_id=1, source_target_pairs={{0,4},{4,8},{8,12},{12,16},{16,20},{20,24},{24,28},{28,32},{32,36}... | collective-permute-start | bytes 98312 | tf_op jit(solution)/shard_map/ppermute | solution.py:427
  42.3 2.2 %copy-start.2 = (bf16[1024,896]{1,0:T(8,128)(2,1)S(1)}, bf16[1024,896]{1,0:T(8,128)(2,1)}, u32[]{:S(2)}) copy-start(bf16[1024,896]{1,0:T(8,128)(2,1)} %get-tuple-element.36.rest_ref) | copy-start | bytes 5505028
  42.9 4.5 %copy-start.1 = (bf16[1024,2048]{1,0:T(8,128)(2,1)S(1)}, bf16[1024,2048]{1,0:T(8,128)(2,1)}, u32[]{:S(2)}) copy-start(bf16[1024,2048]{1,0:T(8,128)(2,1)} %get-tuple-element.31.near_ref) | copy-start | bytes 12582916
  42.9 11.1 %collective-permute-start.3 = (bf16[128,1152]{1,0:T(8,128)(2,1)S(1)}, bf16[128,1152]{1,0:T(8,128)(2,1)S(1)}, u32[]{:S(2)}, u32[]{:S(2)}) collective-permute-start(bf16[128,1152]{1,0:T(8,128)(2,1)S(1)} %get-tuple-element.35), channel_id=1, source_target_pairs={{0,1},{1,2},{2,3},{3,0},{4,5},{5,6},{6,7},{7,4},{8,9},{9,10},{10,1... | collective-permute-start | bytes 884744 | tf_op jit(solution)/shard_map/ppermute | solution.py:346
  45.0 9.0 %copy-start = (bf16[1024,2048]{1,0:T(8,128)(2,1)S(1)}, bf16[1024,2048]{1,0:T(8,128)(2,1)}, u32[]{:S(2)}) copy-start(bf16[1024,2048]{1,0:T(8,128)(2,1)} %get-tuple-element.34.later_ref) | copy-start | bytes 12582916
  45.0 8.5 %collective-permute-start.4 = (bf16[128,896]{1,0:T(8,128)(2,1)S(1)}, bf16[128,896]{1,0:T(8,128)(2,1)S(1)}, u32[]{:S(2)}, u32[]{:S(2)}) collective-permute-start(bf16[128,896]{1,0:T(8,128)(2,1)S(1)} %shard_map.89), channel_id=1, source_target_pairs={{0,3},{1,0},{2,1},{3,2},{4,7},{5,4},{6,5},{7,6},{8,11},{9,8},{10,9... | collective-permute-start | bytes 688136 | tf_op jit(solution)/shard_map/ppermute | solution.py:348
  48.2 10.7 %collective-permute-start.1 = (bf16[128,896]{1,0:T(8,128)(2,1)S(1)}, bf16[128,896]{1,0:T(8,128)(2,1)S(1)}, u32[]{:S(2)}, u32[]{:S(2)}) collective-permute-start(bf16[128,896]{1,0:T(8,128)(2,1)S(1)} %get-tuple-element.32), channel_id=1, source_target_pairs={{0,1},{1,2},{2,3},{3,0},{4,5},{5,6},{6,7},{7,4},{8,9},{9,10},{10,1... | collective-permute-start | bytes 688136 | tf_op jit(solution)/shard_map/ppermute | solution.py:350
  48.2 11.6 %collective-permute-start.2 = (bf16[128,1152]{1,0:T(8,128)(2,1)S(1)}, bf16[128,1152]{1,0:T(8,128)(2,1)S(1)}, u32[]{:S(2)}, u32[]{:S(2)}) collective-permute-start(bf16[128,1152]{1,0:T(8,128)(2,1)S(1)} %get-tuple-element.33), channel_id=1, source_target_pairs={{0,3},{1,0},{2,1},{3,2},{4,7},{5,4},{6,5},{7,6},{8,11},{9,8},{10,9... | collective-permute-start | bytes 884744 | tf_op jit(solution)/shard_map/ppermute | solution.py:351
  54.8 9.8 %collective-permute-start.5 = (bf16[128,1152]{1,0:T(8,128)(2,1)S(1)}, bf16[128,1152]{1,0:T(8,128)(2,1)S(1)}, u32[]{:S(2)}, u32[]{:S(2)}) collective-permute-start(bf16[128,1152]{1,0:T(8,128)(2,1)S(1)} %get-tuple-element.37), channel_id=1, source_target_pairs={{0,1},{1,2},{2,3},{3,0},{4,5},{5,6},{6,7},{7,4},{8,9},{9,10},{10,1... | collective-permute-start | bytes 884744 | tf_op jit(solution)/shard_map/ppermute | solution.py:353
  56.0 7.9 %collective-permute-start.6 = (bf16[128,896]{1,0:T(8,128)(2,1)S(1)}, bf16[128,896]{1,0:T(8,128)(2,1)S(1)}, u32[]{:S(2)}, u32[]{:S(2)}) collective-permute-start(bf16[128,896]{1,0:T(8,128)(2,1)S(1)} %get-tuple-element.38), channel_id=1, source_target_pairs={{0,3},{1,0},{2,1},{3,2},{4,7},{5,4},{6,5},{7,6},{8,11},{9,8},{10,9... | collective-permute-start | bytes 688136 | tf_op jit(solution)/shard_map/ppermute | solution.py:354

commit v7 on v6

--- a/solution.py
+++ b/solution.py
@@ -270,14 +270,12 @@
         down_ref[:, start:stop] = part_of(rows_ref, near_ref, start, stop).astype(bf16)
 
 
-def adding_kernel(rows_ref, later_ref, far_up_ref, far_down_ref, up_ref, down_ref):
-    for start, stop in LEFT:
-        total = part_of(rows_ref, later_ref, start, stop)
-        up_ref[:, start:stop] = (total + far_up_ref[:, start:stop].astype(f32)).astype(bf16)
-    for start, stop in RIGHT:
-        here = slice(start - UP, stop - UP)
-        total = part_of(rows_ref, later_ref, start, stop)
-        down_ref[:, here] = (total + far_down_ref[:, here].astype(f32)).astype(bf16)
+def adding_kernel(rows_ref, held_ref, arrived_ref, out_ref, *, pieces):
+    first = pieces[0][0]
+    for start, stop in pieces:
+        here = slice(start - first, stop - first)
+        total = part_of(rows_ref, held_ref, start, stop)
+        out_ref[:, here] = (total + arrived_ref[:, here].astype(f32)).astype(bf16)
 
 
 def own_kernel(rows_ref, near_up_ref, near_down_ref, weights_ref, out_ref, held_ref, sems):
@@ -349,8 +347,9 @@
     near_up, near_down = plain(near_kernel, (rows, near), [right, left])
     near_up = lax.ppermute(near_up, "ch", up)
     near_down = lax.ppermute(near_down, "ch", down)
-    both_up, both_down = plain(adding_kernel, (rows, later, far_up, far_down), [left, right])
+    (both_up,) = plain(functools.partial(adding_kernel, pieces=LEFT), (rows, later, far_up), [left])
     both_up = lax.ppermute(both_up, "ch", up)
+    (both_down,) = plain(functools.partial(adding_kernel, pieces=RIGHT), (rows, later, far_down), [right])
     both_down = lax.ppermute(both_down, "ch", down)
     (own,) = share(own_kernel, (rows, near_up, near_down, weights), [((ROWS, WIDE), f32)], WIDE)
     return pl.pallas_call(

time: 65.9 us -> 65.9 us (level)
    ppermute x1, waiting for transfers between devices: 2.05 us -> 0.01 us  [project(): far_down = lax.ppermute(far_down, 'ch', down)]
    ppermute x1, waiting for transfers between devices: 0.45 us -> 2.49 us  [project(): far_up = lax.ppermute(far_up, 'ch', up)]
    ppermute x1, starting transfers between devices: 2.11 us -> 2.95 us  [project(): both_down = lax.ppermute(both_down, 'ch', down)]
    ppermute x1, starting transfers between devices: 1.2 us -> 0.43 us  [project(): both_up = lax.ppermute(both_up, 'ch', up)]
    pallas_call x4 -> x5, Pallas kernels: 2.61 us -> 2.8 us  [plain(): pl.pallas_call(kernel, in_specs=[VMEM] * len(arrays), out_specs=[VMEM] *...]
  transfers between devices with their start and end apart: 9 -> 9, of which waited for: 9 -> 8; matrix products, arithmetic and copies ran while one was open for 1% -> 1% of each run, Pallas kernels for 21% -> 21%
where the time goes in v7:
time: 65.9 us; the launch traced here: 65.5 us
  starting transfers between devices  24.9 us (38%)
  Pallas kernels  21.8 us (33%)
  waiting for transfers between devices  17.6 us (27%)
  local copies, waits for them, and re-layouts  1.02 us (2%)
    all_to_all x1, starting transfers between devices, on_device(): arrived = lax.all_to_all(packed, 'seq', 0, 0, tiled=True)  8.26 us
    pallas_call x1, Pallas kernels, stage(): pl.pallas_call(stage_kernel, in_specs=[pl.BlockSpec(memory_space=pl.ANY)]...  7.75 us
    all_to_all x1, waiting for transfers between devices, on_device(): arrived = lax.all_to_all(packed, 'seq', 0, 0, tiled=True)  5.92 us
    all_to_all x1, waiting for transfers between devices, on_device(): outer = lax.all_to_all(outer, 'seq', 0, 0, tiled=True)  4.82 us
    pallas_call x1, Pallas kernels, convolve(): pl.pallas_call(conv_kernel, in_specs=[VMEM] * 6 + [HBM], out_specs=[VMEM,...  4.4 us
    all_to_all x1, starting transfers between devices, on_device(): outer = lax.all_to_all(outer, 'seq', 0, 0, tiled=True)  3.88 us
    ppermute x1, starting transfers between devices, project(): near_down = lax.ppermute(near_down, 'ch', down)  3.22 us
    ppermute x1, starting transfers between devices, project(): both_down = lax.ppermute(both_down, 'ch', down)  2.95 us
  transfers between devices with their start and end apart: 9, of which 8 were waited for; matrix products, arithmetic and copies ran while one was open for 1% of the time, Pallas kernels for 21%

profile of v7, /device:TPU:0, one launch (start us, length us, event | category | flops | bytes accessed | tf_op | source)
XLA Modules:
  0.0 65.5 jit_solution(2138801740766181748)
XLA Ops:
  0.0 2.1 %shard_map.82 = (bf16[32,96,128]{2,1,0:T(8,128)(2,1)}, bf16[16,1024]{1,0:T(8,128)(2,1)S(1)}) custom-call(bf16[3,128,1024]{2,1,0:T(8,128)(2,1)} %streams_ref.3, f32[128,1024]{1,0:T(8,128)} %filter_ref.1), custom_call_target="tpu_custom_call" | custom-call | tf_op jit(solution)/shard_map/pallas_call | solution.py:406
  2.1 8.3 %all-to-all-start = ((bf16[32,96,128]{2,1,0:T(8,128)(2,1)}), bf16[32,96,128]{2,1,0:T(8,128)(2,1)S(1)}, u32[]{:S(2)}, u32[]{:S(2)}) async-start(bf16[32,96,128]{2,1,0:T(8,128)(2,1)} %get-tuple-element.20), calls=%async_computation | async-start | bytes 1572864 | tf_op jit(solution)/shard_map/all_to_all | solution.py:425
  10.4 7.7 %shard_map.83 = (bf16[256,256]{1,0:T(8,128)(2,1)S(1)}, bf16[256,256]{1,0:T(8,128)(2,1)S(1)}, f32[32,2,128]{2,1,0:T(2,128)S(1)}, f32[3,3,1024]{2,1,0:T(4,128)S(1)...) custom-call(bf16[16,1024]{1,0:T(8,128)(2,1)S(1)} %get-tuple-element.21.refs_0_, ...), custom_call_target="tpu_custom_call" | custom-call | tf_op jit(solution)/shard_map/pallas_call | solution.py:368
  18.2 0.8 %dynamic_slice.7 = f32[32]{0:T(128)S(1)} dynamic-slice(f32[1024]{0:T(1024)} %param.11, s32[]{:T(128)S(6)} %select_n.4), dynamic_slice_sizes={32} | dynamic-slice | bytes 260 | tf_op jit(solution)/shard_map/dynamic_slice | solution.py:430
  19.0 0.1 constant_dynamic-slice_fusion
  19.0 5.9 %all-to-all-done.x_ref = bf16[32,96,128]{2,1,0:T(8,128)(2,1)S(1)} async-done(((bf16[32,96,128]{2,1,0:T(8,128)(2,1)}), bf16[32,96,128]{2,1,0:T(8,128)(2,1)S(1)}, u32[]{:S(2)}, u32[]{:S(2)}) %all-to-all-start) | async-done | bytes 786464 | tf_op jit(solution)/shard_map/all_to_all | solution.py:425
  24.9 0.1 broadcast_in_dim.5.skip_ref
  25.0 0.1 broadcast_in_dim.4.taps_ref
  25.1 4.4 %shard_map.84 = (bf16[32,32,128]{2,1,0:T(8,128)(2,1)}, bf16[1024,1152]{1,0:T(8,128)(2,1)S(1)}) custom-call(bf16[32,96,128]{2,1,0:T(8,128)(2,1)S(1)} %all-to-all-done.x_ref, f32[6,32,128]{2,1,0:T(8,128)S(1)} %broadcast_in_dim.4.taps_ref, f32[32,128]{1,0:T(8,128)S(1)} %broadcast_in_dim.5.skip_ref, bf16[256,256]{1,0:T(8,128)(2,1)S(1)} %get-tuple-element.23.high_ref, ...), custom_call_target="tpu_custom_call" | custom-call | tf_op jit(solution)/shard_map/pallas_call | solution.py:383
  29.5 3.9 %all-to-all-start.1 = ((bf16[32,32,128]{2,1,0:T(8,128)(2,1)}), bf16[32,32,128]{2,1,0:T(8,128)(2,1)S(1)}, u32[]{:S(2)}, u32[]{:S(2)}) async-start(bf16[32,32,128]{2,1,0:T(8,128)(2,1)} %get-tuple-element.26), calls=%async_computation.1 | async-start | bytes 524288 | tf_op jit(solution)/shard_map/all_to_all | solution.py:440
  33.4 2.1 %collective-permute-start = (bf16[16,1024]{1,0:T(8,128)(2,1)S(1)}, bf16[16,1024]{1,0:T(8,128)(2,1)S(1)}, u32[]{:S(2)}, u32[]{:S(2)}) collective-permute-start(bf16[16,1024]{1,0:T(8,128)(2,1)S(1)} %get-tuple-element.21.refs_0_), channel_id=1, source_target_pairs={{0,4},{4,8},{8,12},{12,16},{16,20},{20,24},{24,28},{28,32},{32,36}... | collective-permute-start | bytes 98312 | tf_op jit(solution)/shard_map/ppermute | solution.py:426
  35.5 0.8 %collective-permute-done.edge_ref = bf16[16,1024]{1,0:T(8,128)(2,1)S(1)} collective-permute-done((bf16[16,1024]{1,0:T(8,128)(2,1)S(1)}, bf16[16,1024]{1,0:T(8,128)(2,1)S(1)}, u32[]{:S(2)}, u32[]{:S(2)}) %collective-permute-start) | collective-permute-done | bytes 32800 | tf_op jit(solution)/shard_map/ppermute | solution.py:426
  36.3 1.2 %shard_map.85.query_ref = f32[128,1024]{1,0:T(8,128)S(1)} custom-call(bf16[3,128,1024]{2,1,0:T(8,128)(2,1)} %streams_ref.3, bf16[16,1024]{1,0:T(8,128)(2,1)S(1)} %collective-permute-done.edge_ref, f32[3,3,1024]{2,1,0:T(4,128)S(1)} %get-tuple-element.22.taps_ref, bf16[1024,1152]{1,0:T(8,128)(2,1)S(1)} %get-tuple-element.27.held_ref), custom_call_target="tpu_custom_call" | custom-call | tf_op jit(solution)/shard_map/pallas_call | solution.py:432
  37.5 4.8 %all-to-all-done.1 = bf16[32,32,128]{2,1,0:T(8,128)(2,1)S(1)} async-done(((bf16[32,32,128]{2,1,0:T(8,128)(2,1)}), bf16[32,32,128]{2,1,0:T(8,128)(2,1)S(1)}, u32[]{:S(2)}, u32[]{:S(2)}) %all-to-all-start.1) | async-done | bytes 262176 | tf_op jit(solution)/shard_map/all_to_all | solution.py:440
  42.3 0.0 copy-start.2
  42.3 0.5 shard_map.86
  42.9 0.0 copy-start.1
  42.9 1.6 %collective-permute-start.3 = (bf16[128,1152]{1,0:T(8,128)(2,1)S(1)}, bf16[128,1152]{1,0:T(8,128)(2,1)S(1)}, u32[]{:S(2)}, u32[]{:S(2)}) collective-permute-start(bf16[128,1152]{1,0:T(8,128)(2,1)S(1)} %get-tuple-element.33), channel_id=1, source_target_pairs={{0,1},{1,2},{2,3},{3,0},{4,5},{5,6},{6,7},{7,4},{8,9},{9,10},{10,1... | collective-permute-start | bytes 884744 | tf_op jit(solution)/shard_map/ppermute | solution.py:344
  44.5 0.0 copy-done.2
  44.5 0.4 shard_map.90
  45.0 0.0 copy-start
  45.0 2.4 %collective-permute-start.5 = (bf16[128,896]{1,0:T(8,128)(2,1)S(1)}, bf16[128,896]{1,0:T(8,128)(2,1)S(1)}, u32[]{:S(2)}, u32[]{:S(2)}) collective-permute-start(bf16[128,896]{1,0:T(8,128)(2,1)S(1)} %shard_map.90), channel_id=1, source_target_pairs={{0,3},{1,0},{2,1},{3,2},{4,7},{5,4},{6,5},{7,6},{8,11},{9,8},{10,9... | collective-permute-start | bytes 688136 | tf_op jit(solution)/shard_map/ppermute | solution.py:346
  47.4 0.0 copy-done.1
  47.4 0.8 %shard_map.87 = (bf16[128,896]{1,0:T(8,128)(2,1)S(1)}, bf16[128,1152]{1,0:T(8,128)(2,1)S(1)}) custom-call(bf16[128,1024]{1,0:T(8,128)(2,1)S(1)} %get-tuple-element.28.rows_ref, bf16[1024,2048]{1,0:T(8,128)(2,1)S(1)} %copy-done.1), custom_call_target="tpu_custom_call" | custom-call | flops 2147483648 | bytes 2097152 | tf_op jit(solution)/shard_map/pallas_call | solution.py:329
  48.2 0.1 collective-permute-start.1
  48.3 3.2 %collective-permute-start.2 = (bf16[128,1152]{1,0:T(8,128)(2,1)S(1)}, bf16[128,1152]{1,0:T(8,128)(2,1)S(1)}, u32[]{:S(2)}, u32[]{:S(2)}) collective-permute-start(bf16[128,1152]{1,0:T(8,128)(2,1)S(1)} %get-tuple-element.31), channel_id=1, source_target_pairs={{0,3},{1,0},{2,1},{3,2},{4,7},{5,4},{6,5},{7,6},{8,11},{9,8},{10,9... | collective-permute-start | bytes 884744 | tf_op jit(solution)/shard_map/ppermute | solution.py:349
  51.5 2.5 %collective-permute-done.3.arrived_ref = bf16[128,1152]{1,0:T(8,128)(2,1)S(1)} collective-permute-done((bf16[128,1152]{1,0:T(8,128)(2,1)S(1)}, bf16[128,1152]{1,0:T(8,128)(2,1)S(1)}, u32[]{:S(2)}, u32[]{:S(2)}) %collective-permute-start.3) | collective-permute-done | bytes 294944 | tf_op jit(solution)/shard_map/ppermute | solution.py:344
  54.0 0.0 copy-done
  54.0 0.5 shard_map.89
  54.5 0.4 collective-permute-start.4
  55.0 0.0 collective-permute-done.5.arrived_ref
  55.0 0.5 shard_map.91
  55.4 2.9 %collective-permute-start.6 = (bf16[128,896]{1,0:T(8,128)(2,1)S(1)}, bf16[128,896]{1,0:T(8,128)(2,1)S(1)}, u32[]{:S(2)}, u32[]{:S(2)}) collective-permute-start(bf16[128,896]{1,0:T(8,128)(2,1)S(1)} %shard_map.91), channel_id=1, source_target_pairs={{0,3},{1,0},{2,1},{3,2},{4,7},{5,4},{6,5},{7,6},{8,11},{9,8},{10,9... | collective-permute-start | bytes 688136 | tf_op jit(solution)/shard_map/ppermute | solution.py:353
  58.4 0.5 collective-permute-done.1.near_up_ref
  58.9 1.0 %collective-permute-done.2.near_down_ref = bf16[128,1152]{1,0:T(8,128)(2,1)S(1)} collective-permute-done((bf16[128,1152]{1,0:T(8,128)(2,1)S(1)}, bf16[128,1152]{1,0:T(8,128)(2,1)S(1)}, u32[]{:S(2)}, u32[]{:S(2)}) %collective-permute-start.2) | collective-permute-done | bytes 294944 | tf_op jit(solution)/shard_map/ppermute | solution.py:349
  59.8 2.7 %shard_map.88.own_ref = f32[128,2048]{1,0:T(8,128)S(1)} custom-call(bf16[128,1024]{1,0:T(8,128)(2,1)S(1)} %get-tuple-element.28.rows_ref, bf16[128,896]{1,0:T(8,128)(2,1)S(1)} %collective-permute-done.1.near_up_ref, bf16[128,1152]{1,0:T(8,128)(2,1)S(1)} %collective-permute-done.2.near_down_ref, bf16[1024,8192]{1,0:T(8,128)(2,1)} %weights_ref.3), custom_call_target="tpu_custom_call" | custom-call | flops 2147483648 | bytes 2097152 | tf_op jit(solution)/shard_map/pallas_call | solution.py:314
  62.6 1.3 %collective-permute-done.6.both_down_ref = bf16[128,896]{1,0:T(8,128)(2,1)S(1)} collective-permute-done((bf16[128,896]{1,0:T(8,128)(2,1)S(1)}, bf16[128,896]{1,0:T(8,128)(2,1)S(1)}, u32[]{:S(2)}, u32[]{:S(2)}) %collective-permute-start.6) | collective-permute-done | bytes 229408 | tf_op jit(solution)/shard_map/ppermute | solution.py:353
  63.9 0.7 %collective-permute-done.4.both_up_ref = bf16[128,1152]{1,0:T(8,128)(2,1)S(1)} collective-permute-done((bf16[128,1152]{1,0:T(8,128)(2,1)S(1)}, bf16[128,1152]{1,0:T(8,128)(2,1)S(1)}, u32[]{:S(2)}, u32[]{:S(2)}) %collective-permute-start.4) | collective-permute-done | bytes 294944 | tf_op jit(solution)/shard_map/ppermute | solution.py:351
  64.6 0.8 %shard_map.92 = bf16[128,2048]{1,0:T(8,128)(2,1)} custom-call(f32[128,2048]{1,0:T(8,128)S(1)} %shard_map.88.own_ref, bf16[128,1152]{1,0:T(8,128)(2,1)S(1)} %collective-permute-done.4.both_up_ref, bf16[128,896]{1,0:T(8,128)(2,1)S(1)} %collective-permute-done.6.both_down_ref), custom_call_target="tpu_custom_call" | custom-call | tf_op jit(solution)/shard_map/pallas_call | solution.py:355
  (2 shorter events, 0.0 us)
Async XLA Ops:
  2.1 22.8 %all-to-all-start = ((bf16[32,96,128]{2,1,0:T(8,128)(2,1)}), bf16[32,96,128]{2,1,0:T(8,128)(2,1)S(1)}, u32[]{:S(2)}, u32[]{:S(2)}) async-start(bf16[32,96,128]{2,1,0:T(8,128)(2,1)} %get-tuple-element.20), calls=%async_computation | async-start | bytes 1572864 | tf_op jit(solution)/shard_map/all_to_all | solution.py:425
  29.5 12.8 %all-to-all-start.1 = ((bf16[32,32,128]{2,1,0:T(8,128)(2,1)}), bf16[32,32,128]{2,1,0:T(8,128)(2,1)S(1)}, u32[]{:S(2)}, u32[]{:S(2)}) async-start(bf16[32,32,128]{2,1,0:T(8,128)(2,1)} %get-tuple-element.26), calls=%async_computation.1 | async-start | bytes 524288 | tf_op jit(solution)/shard_map/all_to_all | solution.py:440
  33.4 2.9 %collective-permute-start = (bf16[16,1024]{1,0:T(8,128)(2,1)S(1)}, bf16[16,1024]{1,0:T(8,128)(2,1)S(1)}, u32[]{:S(2)}, u32[]{:S(2)}) collective-permute-start(bf16[16,1024]{1,0:T(8,128)(2,1)S(1)} %get-tuple-element.21.refs_0_), channel_id=1, source_target_pairs={{0,4},{4,8},{8,12},{12,16},{16,20},{20,24},{24,28},{28,32},{32,36}... | collective-permute-start | bytes 98312 | tf_op jit(solution)/shard_map/ppermute | solution.py:426
  42.3 2.2 %copy-start.2 = (bf16[1024,896]{1,0:T(8,128)(2,1)S(1)}, bf16[1024,896]{1,0:T(8,128)(2,1)}, u32[]{:S(2)}) copy-start(bf16[1024,896]{1,0:T(8,128)(2,1)} %get-tuple-element.34.rest_ref) | copy-start | bytes 5505028
  42.9 4.5 %copy-start.1 = (bf16[1024,2048]{1,0:T(8,128)(2,1)S(1)}, bf16[1024,2048]{1,0:T(8,128)(2,1)}, u32[]{:S(2)}) copy-start(bf16[1024,2048]{1,0:T(8,128)(2,1)} %get-tuple-element.29.near_ref) | copy-start | bytes 12582916
  42.9 11.1 %collective-permute-start.3 = (bf16[128,1152]{1,0:T(8,128)(2,1)S(1)}, bf16[128,1152]{1,0:T(8,128)(2,1)S(1)}, u32[]{:S(2)}, u32[]{:S(2)}) collective-permute-start(bf16[128,1152]{1,0:T(8,128)(2,1)S(1)} %get-tuple-element.33), channel_id=1, source_target_pairs={{0,1},{1,2},{2,3},{3,0},{4,5},{5,6},{6,7},{7,4},{8,9},{9,10},{10,1... | collective-permute-start | bytes 884744 | tf_op jit(solution)/shard_map/ppermute | solution.py:344
  45.0 9.0 %copy-start = (bf16[1024,2048]{1,0:T(8,128)(2,1)S(1)}, bf16[1024,2048]{1,0:T(8,128)(2,1)}, u32[]{:S(2)}) copy-start(bf16[1024,2048]{1,0:T(8,128)(2,1)} %get-tuple-element.32.held_ref) | copy-start | bytes 12582916
  45.0 10.0 %collective-permute-start.5 = (bf16[128,896]{1,0:T(8,128)(2,1)S(1)}, bf16[128,896]{1,0:T(8,128)(2,1)S(1)}, u32[]{:S(2)}, u32[]{:S(2)}) collective-permute-start(bf16[128,896]{1,0:T(8,128)(2,1)S(1)} %shard_map.90), channel_id=1, source_target_pairs={{0,3},{1,0},{2,1},{3,2},{4,7},{5,4},{6,5},{7,6},{8,11},{9,8},{10,9... | collective-permute-start | bytes 688136 | tf_op jit(solution)/shard_map/ppermute | solution.py:346
  48.2 10.7 %collective-permute-start.1 = (bf16[128,896]{1,0:T(8,128)(2,1)S(1)}, bf16[128,896]{1,0:T(8,128)(2,1)S(1)}, u32[]{:S(2)}, u32[]{:S(2)}) collective-permute-start(bf16[128,896]{1,0:T(8,128)(2,1)S(1)} %get-tuple-element.30), channel_id=1, source_target_pairs={{0,1},{1,2},{2,3},{3,0},{4,5},{5,6},{6,7},{7,4},{8,9},{9,10},{10,1... | collective-permute-start | bytes 688136 | tf_op jit(solution)/shard_map/ppermute | solution.py:348
  48.3 11.6 %collective-permute-start.2 = (bf16[128,1152]{1,0:T(8,128)(2,1)S(1)}, bf16[128,1152]{1,0:T(8,128)(2,1)S(1)}, u32[]{:S(2)}, u32[]{:S(2)}) collective-permute-start(bf16[128,1152]{1,0:T(8,128)(2,1)S(1)} %get-tuple-element.31), channel_id=1, source_target_pairs={{0,3},{1,0},{2,1},{3,2},{4,7},{5,4},{6,5},{7,6},{8,11},{9,8},{10,9... | collective-permute-start | bytes 884744 | tf_op jit(solution)/shard_map/ppermute | solution.py:349
  54.5 10.1 %collective-permute-start.4 = (bf16[128,1152]{1,0:T(8,128)(2,1)S(1)}, bf16[128,1152]{1,0:T(8,128)(2,1)S(1)}, u32[]{:S(2)}, u32[]{:S(2)}) collective-permute-start(bf16[128,1152]{1,0:T(8,128)(2,1)S(1)} %shard_map.89), channel_id=1, source_target_pairs={{0,1},{1,2},{2,3},{3,0},{4,5},{5,6},{6,7},{7,4},{8,9},{9,10},{10,1... | collective-permute-start | bytes 884744 | tf_op jit(solution)/shard_map/ppermute | solution.py:351
  55.4 8.5 %collective-permute-start.6 = (bf16[128,896]{1,0:T(8,128)(2,1)S(1)}, bf16[128,896]{1,0:T(8,128)(2,1)S(1)}, u32[]{:S(2)}, u32[]{:S(2)}) collective-permute-start(bf16[128,896]{1,0:T(8,128)(2,1)S(1)} %shard_map.91), channel_id=1, source_target_pairs={{0,3},{1,0},{2,1},{3,2},{4,7},{5,4},{6,5},{7,6},{8,11},{9,8},{10,9... | collective-permute-start | bytes 688136 | tf_op jit(solution)/shard_map/ppermute | solution.py:353

commit v8 on v6

--- a/solution.py
+++ b/solution.py
@@ -97,7 +97,7 @@
     sems, bounce_ref = refs[-1], refs[-2]
     tables_in, weights_ref = refs[1 : 1 + TABLES], refs[1 + TABLES]
     tables_out = refs[2 + TABLES : 2 + 2 * TABLES]
-    rest_ref, near_ref, later_ref = refs[-5:-2]
+    rest_ref, near_ref = refs[-4:-2]
     copies = [
         pltpu.make_async_copy(source, target, sems.at[i]) for i, (source, target) in enumerate(zip(tables_in, tables_out))
     ]
@@ -106,7 +106,6 @@
     count, arriving = TABLES, []
     for target_ref, at, away, pieces, first in (
         (near_ref, 0, 1, RIGHT, 0), (near_ref, 0, RING - 1, LEFT, 0), (rest_ref, WIDE, 2, RIGHT, UP),
-        (later_ref, 2 * WIDE - UP, 1, LEFT, 0), (later_ref, 2 * WIDE - UP, RING - 1, RIGHT, 0),
     ):
         held_ref = bounce_ref.at[:, at : at + target_ref.shape[1]]
         for start, stop, copy in fetch(weights_ref, held_ref, sems.at[count:], away, pieces, first):
@@ -118,6 +117,19 @@
         onward.start()
         copies.append(onward)
     for copy in copies:
+        copy.wait()
+
+
+def later_kernel(held_ref, weights_ref, later_ref, bounce_ref, sems):
+    arriving = fetch(weights_ref, bounce_ref, sems, 1, LEFT)
+    arriving += fetch(weights_ref, bounce_ref, sems.at[len(LEFT) :], RING - 1, RIGHT)
+    leaving = []
+    for i, (start, stop, copy) in enumerate(arriving):
+        copy.wait()
+        here = slice(start, stop)
+        leaving.append(pltpu.make_async_copy(bounce_ref.at[:, here], later_ref.at[:, here], sems.at[i]))
+        leaving[-1].start()
+    for copy in leaving:
         copy.wait()
 
 
@@ -140,7 +152,7 @@
 
 
 def conv_kernel(
-    x_ref, taps_ref, skip_ref, high_ref, low_ref, twists_ref, weights_ref,
+    x_ref, taps_ref, skip_ref, high_ref, low_ref, twists_ref, edge_ref, weights_ref,
     out_ref, held_ref, gated_ref, first_ref, left_ref, back_ref, sems,
 ):
     copies = fetch(weights_ref, held_ref, sems, 2, LEFT)
@@ -252,7 +264,7 @@
     return jnp.dot(rows_ref[...], held_ref[:, start:stop], preferred_element_type=f32)
 
 
-def mixing_kernel(outer_ref, query_ref, held_ref, up_ref, rows_ref):
+def mixing_kernel(outer_ref, query_ref, held_ref, later_ref, up_ref, rows_ref):
     rows_ref[...] = (query_ref[...] * outer_ref[...].T.astype(f32)).astype(bf16)
     for start, stop in LEFT:
         up_ref[:, start:stop] = part_of(rows_ref, held_ref, start, stop).astype(bf16)
@@ -327,10 +339,10 @@
     )(*arrays)
 
 
-def plain(kernel, arrays, outs):
+def plain(kernel, arrays, outs, last=VMEM):
     return pl.pallas_call(
         kernel,
-        in_specs=[VMEM] * len(arrays),
+        in_specs=[VMEM] * (len(arrays) - 1) + [last],
         out_specs=[VMEM] * len(outs),
         out_shape=[pltpu.VMEM(shape, dtype) for shape, dtype in outs],
         cost_estimate=pl.CostEstimate(flops=2**31, bytes_accessed=2**21, transcendentals=0),
@@ -342,7 +354,7 @@
     up = [(i, (i + 1) % RING) for i in range(RING)]
     down = [(i, (i - 1) % RING) for i in range(RING)]
     left, right = ((ROWS, UP), bf16), ((ROWS, WIDE - UP), bf16)
-    far_up, rows = plain(mixing_kernel, (outer, query, held), [left, (query.shape, bf16)])
+    far_up, rows = plain(mixing_kernel, (outer, query, held, pltpu.with_memory_space_constraint(later, pltpu.HBM)), [left, (query.shape, bf16)], HBM)
     far_up = lax.ppermute(far_up, "ch", up)
     (far_down,) = plain(far_kernel, (rows, rest), [right])
     far_down = lax.ppermute(far_down, "ch", down)
@@ -365,15 +377,15 @@
 
 def stage(after, weights, *arrays):
     arrays = [pltpu.with_memory_space_constraint(array, pltpu.HBM) for array in arrays]
-    parts = [pltpu.HBM((weights.shape[0], wide), bf16) for wide in (WIDE - UP, WIDE, WIDE)]
+    parts = [pltpu.HBM((weights.shape[0], wide), bf16) for wide in (WIDE - UP, WIDE)]
     return pl.pallas_call(
         stage_kernel,
         in_specs=[pl.BlockSpec(memory_space=pl.ANY)] + [HBM] * (len(arrays) + 1),
         out_specs=[VMEM] * len(arrays) + [HBM] * len(parts),
         out_shape=[pltpu.VMEM(array.shape, array.dtype) for array in arrays] + parts,
         scratch_shapes=[
-            pltpu.VMEM((weights.shape[0], 3 * WIDE - UP), bf16),
-            pltpu.SemaphoreType.DMA((len(arrays) + 2 * len(LEFT) + 3 * len(RIGHT),)),
+            pltpu.VMEM((weights.shape[0], 2 * WIDE - UP), bf16),
+            pltpu.SemaphoreType.DMA((len(arrays) + len(LEFT) + 2 * len(RIGHT),)),
         ],
         compiler_params=pltpu.CompilerParams(vmem_limit_bytes=16 * 2**20),
     )(after, *arrays, weights)
@@ -383,7 +395,7 @@
     channels = arrays[-1].shape[0]
     return pl.pallas_call(
         conv_kernel,
-        in_specs=[VMEM] * 6 + [HBM],
+        in_specs=[VMEM] * 7 + [HBM],
         out_specs=[VMEM, VMEM],
         out_shape=[
             pltpu.VMEM((PARTS, GROUP, ROWS), bf16),
@@ -429,7 +441,18 @@
     taps = lax.dynamic_slice_in_dim(short_taps[1:].reshape((SENT - 1) * SHORT, channels), first, GROUP, 1)
     taps = jnp.broadcast_to(taps[:, :, None], ((SENT - 1) * SHORT, GROUP, ROWS))
     skip = jnp.broadcast_to(lax.dynamic_slice_in_dim(skip_gain, first, GROUP, 0)[:, None], (GROUP, ROWS))
-    outer, held = convolve(arrived, taps, skip, high, low, twists, weights)
+    outer, held = convolve(arrived, taps, skip, high, low, twists, edge, weights)
+    later = pl.pallas_call(
+        later_kernel,
+        in_specs=[VMEM, HBM],
+        out_specs=HBM,
+        out_shape=pltpu.HBM((channels, WIDE), bf16),
+        scratch_shapes=[
+            pltpu.VMEM((channels, WIDE), bf16),
+            pltpu.SemaphoreType.DMA((len(LEFT + RIGHT),)),
+        ],
+        compiler_params=pltpu.CompilerParams(vmem_limit_bytes=8 * 2**20),
+    )(held, weights)
     query = pl.pallas_call(
         query_kernel,
         in_specs=[HBM, VMEM, VMEM, VMEM],
@@ -439,7 +462,7 @@
         compiler_params=pltpu.CompilerParams(vmem_limit_bytes=8 * 2**20),
     )(streams, edge, short_taps, held)
     outer = lax.all_to_all(outer, "seq", 0, 0, tiled=True)
-    return project(outer.reshape(channels, ROWS), query, weights, held, *parts)
+    return project(outer.reshape(channels, ROWS), query, weights, held, *parts, later)
 
 
 def solution(mesh):

time: 65.9 us -> 65.9 us (level)
  waiting for transfers between devices: 17.9 us -> 16.7 us
  Pallas kernels: 21.6 us -> 22.7 us
    pallas_call x5 -> x6, Pallas kernels: 7.01 us -> 10.4 us  [the longest x1 4.4 us: convolve(): pl.pallas_call(conv_kernel, in_specs=[VMEM] * 7 + [HBM], out_specs=[VMEM,...]
    pallas_call x1, Pallas kernels: 7.74 us -> 5.43 us  [stage(): pl.pallas_call(stage_kernel, in_specs=[pl.BlockSpec(memory_space=pl.ANY)]...]
    ppermute x1, waiting for transfers between devices: 0.84 us -> 0.01 us  [on_device(): edge = lax.ppermute(edge, 'seq', [(i, i + 1) for i in range(PARTS - 1)])]
  transfers between devices with their start and end apart: 9 -> 9, of which waited for: 9 -> 8; matrix products, arithmetic and copies ran while one was open for 1% -> 1% of each run, Pallas kernels for 21% -> 23%
where the time goes in v8:
time: 65.9 us; the launch traced here: 65.5 us
  starting transfers between devices  25 us (38%)
  Pallas kernels  22.7 us (34%)
  waiting for transfers between devices  16.7 us (25%)
  local copies, waits for them, and re-layouts  1.02 us (2%)
    all_to_all x1, starting transfers between devices, on_device(): arrived = lax.all_to_all(packed, 'seq', 0, 0, tiled=True)  8.26 us
    all_to_all x1, waiting for transfers between devices, on_device(): arrived = lax.all_to_all(packed, 'seq', 0, 0, tiled=True)  6.04 us
    pallas_call x1, Pallas kernels, stage(): pl.pallas_call(stage_kernel, in_specs=[pl.BlockSpec(memory_space=pl.ANY)]...  5.43 us
    pallas_call x1, Pallas kernels, convolve(): pl.pallas_call(conv_kernel, in_specs=[VMEM] * 7 + [HBM], out_specs=[VMEM,...  4.4 us
    all_to_all x1, waiting for transfers between devices, on_device(): outer = lax.all_to_all(outer, 'seq', 0, 0, tiled=True)  4.3 us
    all_to_all x1, starting transfers between devices, on_device(): outer = lax.all_to_all(outer, 'seq', 0, 0, tiled=True)  3.89 us
    pallas_call x1, Pallas kernels, on_device(): pl.pallas_call(later_kernel, in_specs=[VMEM, HBM], out_specs=HBM, out_sha...  3.41 us
    ppermute x1, starting transfers between devices, project(): near_down = lax.ppermute(near_down, 'ch', down)  3.22 us
  transfers between devices with their start and end apart: 9, of which 8 were waited for; matrix products, arithmetic and copies ran while one was open for 1% of the time, Pallas kernels for 23%

profile of v8, /device:TPU:0, one launch (start us, length us, event | category | flops | bytes accessed | tf_op | source)
XLA Modules:
  0.0 65.5 jit_solution(1554060795691325784)
XLA Ops:
  0.0 2.1 %shard_map.82 = (bf16[32,96,128]{2,1,0:T(8,128)(2,1)}, bf16[16,1024]{1,0:T(8,128)(2,1)S(1)}) custom-call(bf16[3,128,1024]{2,1,0:T(8,128)(2,1)} %streams_ref.3, f32[128,1024]{1,0:T(8,128)} %filter_ref.1), custom_call_target="tpu_custom_call" | custom-call | tf_op jit(solution)/shard_map/pallas_call | solution.py:419
  2.1 8.3 %all-to-all-start = ((bf16[32,96,128]{2,1,0:T(8,128)(2,1)}), bf16[32,96,128]{2,1,0:T(8,128)(2,1)S(1)}, u32[]{:S(2)}, u32[]{:S(2)}) async-start(bf16[32,96,128]{2,1,0:T(8,128)(2,1)} %get-tuple-element.21), calls=%async_computation | async-start | bytes 1572864 | tf_op jit(solution)/shard_map/all_to_all | solution.py:438
  10.4 2.2 %collective-permute-start = (bf16[16,1024]{1,0:T(8,128)(2,1)S(1)}, bf16[16,1024]{1,0:T(8,128)(2,1)S(1)}, u32[]{:S(2)}, u32[]{:S(2)}) collective-permute-start(bf16[16,1024]{1,0:T(8,128)(2,1)S(1)} %get-tuple-element.22.refs_0_), channel_id=1, source_target_pairs={{0,4},{4,8},{8,12},{12,16},{16,20},{20,24},{24,28},{28,32},{32,36}... | collective-permute-start | bytes 98312 | tf_op jit(solution)/shard_map/ppermute | solution.py:439
  12.6 5.4 %shard_map.83 = (bf16[256,256]{1,0:T(8,128)(2,1)S(1)}, bf16[256,256]{1,0:T(8,128)(2,1)S(1)}, f32[32,2,128]{2,1,0:T(2,128)S(1)}, f32[3,3,1024]{2,1,0:T(4,128)S(1)...) custom-call(bf16[16,1024]{1,0:T(8,128)(2,1)S(1)} %get-tuple-element.22.refs_0_, ...), custom_call_target="tpu_custom_call" | custom-call | tf_op jit(solution)/shard_map/pallas_call | solution.py:381
  18.0 0.1 constant_dynamic-slice_fusion
  18.1 0.8 %dynamic_slice.7 = f32[32]{0:T(128)S(1)} dynamic-slice(f32[1024]{0:T(1024)} %param.11, s32[]{:T(128)S(6)} %select_n.4), dynamic_slice_sizes={32} | dynamic-slice | bytes 260 | tf_op jit(solution)/shard_map/dynamic_slice | solution.py:443
  18.9 0.0 collective-permute-done.edge_ref
  18.9 6.0 %all-to-all-done.x_ref = bf16[32,96,128]{2,1,0:T(8,128)(2,1)S(1)} async-done(((bf16[32,96,128]{2,1,0:T(8,128)(2,1)}), bf16[32,96,128]{2,1,0:T(8,128)(2,1)S(1)}, u32[]{:S(2)}, u32[]{:S(2)}) %all-to-all-start) | async-done | bytes 786464 | tf_op jit(solution)/shard_map/all_to_all | solution.py:438
  24.9 0.1 broadcast_in_dim.5.skip_ref
  25.0 0.1 broadcast_in_dim.4.taps_ref
  25.1 4.4 %shard_map.84 = (bf16[32,32,128]{2,1,0:T(8,128)(2,1)}, bf16[1024,1152]{1,0:T(8,128)(2,1)S(1)}) custom-call(bf16[32,96,128]{2,1,0:T(8,128)(2,1)S(1)} %all-to-all-done.x_ref, f32[6,32,128]{2,1,0:T(8,128)S(1)} %broadcast_in_dim.4.taps_ref, f32[32,128]{1,0:T(8,128)S(1)} %broadcast_in_dim.5.skip_ref, bf16[256,256]{1,0:T(8,128)(2,1)S(1)} %get-tuple-element.24.high_ref, ...), custom_call_target="tpu_custom_call" | custom-call | tf_op jit(solution)/shard_map/pallas_call | solution.py:396
  29.5 3.9 %all-to-all-start.1 = ((bf16[32,32,128]{2,1,0:T(8,128)(2,1)}), bf16[32,32,128]{2,1,0:T(8,128)(2,1)S(1)}, u32[]{:S(2)}, u32[]{:S(2)}) async-start(bf16[32,32,128]{2,1,0:T(8,128)(2,1)} %get-tuple-element.27), calls=%async_computation.1 | async-start | bytes 524288 | tf_op jit(solution)/shard_map/all_to_all | solution.py:464
  33.4 3.4 %shard_map.86.later_ref = bf16[1024,2048]{1,0:T(8,128)(2,1)} custom-call(bf16[1024,1152]{1,0:T(8,128)(2,1)S(1)} %get-tuple-element.28.held_ref, bf16[1024,8192]{1,0:T(8,128)(2,1)} %weights_ref.5), custom_call_target="tpu_custom_call" | custom-call | tf_op jit(solution)/shard_map/pallas_call | solution.py:445
  36.8 1.2 %shard_map.85.query_ref = f32[128,1024]{1,0:T(8,128)S(1)} custom-call(bf16[3,128,1024]{2,1,0:T(8,128)(2,1)} %streams_ref.3, bf16[16,1024]{1,0:T(8,128)(2,1)S(1)} %collective-permute-done.edge_ref, f32[3,3,1024]{2,1,0:T(4,128)S(1)} %get-tuple-element.23.taps_ref, bf16[1024,1152]{1,0:T(8,128)(2,1)S(1)} %get-tuple-element.28.held_ref), custom_call_target="tpu_custom_call" | custom-call | tf_op jit(solution)/shard_map/pallas_call | solution.py:456
  38.0 4.3 %all-to-all-done.1 = bf16[32,32,128]{2,1,0:T(8,128)(2,1)S(1)} async-done(((bf16[32,32,128]{2,1,0:T(8,128)(2,1)}), bf16[32,32,128]{2,1,0:T(8,128)(2,1)S(1)}, u32[]{:S(2)}, u32[]{:S(2)}) %all-to-all-start.1) | async-done | bytes 262176 | tf_op jit(solution)/shard_map/all_to_all | solution.py:464
  42.3 0.0 copy-start.2
  42.3 0.5 shard_map.87
  42.8 0.0 copy-start.1
  42.9 1.6 %collective-permute-start.3 = (bf16[128,1152]{1,0:T(8,128)(2,1)S(1)}, bf16[128,1152]{1,0:T(8,128)(2,1)S(1)}, u32[]{:S(2)}, u32[]{:S(2)}) collective-permute-start(bf16[128,1152]{1,0:T(8,128)(2,1)S(1)} %get-tuple-element.33), channel_id=1, source_target_pairs={{0,1},{1,2},{2,3},{3,0},{4,5},{5,6},{6,7},{7,4},{8,9},{9,10},{10,1... | collective-permute-start | bytes 884744 | tf_op jit(solution)/shard_map/ppermute | solution.py:358
  44.5 0.0 copy-done.2
  44.5 0.4 shard_map.90
  45.0 0.0 copy-start
  45.0 2.4 %collective-permute-start.4 = (bf16[128,896]{1,0:T(8,128)(2,1)S(1)}, bf16[128,896]{1,0:T(8,128)(2,1)S(1)}, u32[]{:S(2)}, u32[]{:S(2)}) collective-permute-start(bf16[128,896]{1,0:T(8,128)(2,1)S(1)} %shard_map.90), channel_id=1, source_target_pairs={{0,3},{1,0},{2,1},{3,2},{4,7},{5,4},{6,5},{7,6},{8,11},{9,8},{10,9... | collective-permute-start | bytes 688136 | tf_op jit(solution)/shard_map/ppermute | solution.py:360
  47.3 0.0 copy-done.1
  47.4 0.8 %shard_map.88 = (bf16[128,896]{1,0:T(8,128)(2,1)S(1)}, bf16[128,1152]{1,0:T(8,128)(2,1)S(1)}) custom-call(bf16[128,1024]{1,0:T(8,128)(2,1)S(1)} %get-tuple-element.29.rows_ref, bf16[1024,2048]{1,0:T(8,128)(2,1)S(1)} %copy-done.1), custom_call_target="tpu_custom_call" | custom-call | flops 2147483648 | bytes 2097152 | tf_op jit(solution)/shard_map/pallas_call | solution.py:343
  48.2 0.1 collective-permute-start.1
  48.2 3.2 %collective-permute-start.2 = (bf16[128,1152]{1,0:T(8,128)(2,1)S(1)}, bf16[128,1152]{1,0:T(8,128)(2,1)S(1)}, u32[]{:S(2)}, u32[]{:S(2)}) collective-permute-start(bf16[128,1152]{1,0:T(8,128)(2,1)S(1)} %get-tuple-element.32), channel_id=1, source_target_pairs={{0,3},{1,0},{2,1},{3,2},{4,7},{5,4},{6,5},{7,6},{8,11},{9,8},{10,9... | collective-permute-start | bytes 884744 | tf_op jit(solution)/shard_map/ppermute | solution.py:363
  51.5 2.0 %collective-permute-done.4.far_down_ref = bf16[128,896]{1,0:T(8,128)(2,1)S(1)} collective-permute-done((bf16[128,896]{1,0:T(8,128)(2,1)S(1)}, bf16[128,896]{1,0:T(8,128)(2,1)S(1)}, u32[]{:S(2)}, u32[]{:S(2)}) %collective-permute-start.4) | collective-permute-done | bytes 229408 | tf_op jit(solution)/shard_map/ppermute | solution.py:360
  53.5 0.4 collective-permute-done.3.far_up_ref
  54.0 0.0 copy-done
  54.0 0.8 %shard_map.91 = (bf16[128,1152]{1,0:T(8,128)(2,1)S(1)}, bf16[128,896]{1,0:T(8,128)(2,1)S(1)}) custom-call(bf16[128,1024]{1,0:T(8,128)(2,1)S(1)} %get-tuple-element.29.rows_ref, bf16[1024,2048]{1,0:T(8,128)(2,1)S(1)} %copy-done, bf16[128,1152]{1,0:T(8,128)(2,1)S(1)} %collective-permute-done.3.far_up_ref, bf16[128,896]{1,0:T(8,128)(2,1)S(1)} %collective-permute-done.4.far_down_ref), custom_call_target="tpu_custom_call" | custom-call | flops 2147483648 | bytes 2097152 | tf_op jit(solution)/shard_map/pallas_call | solution.py:343
  54.8 1.2 %collective-permute-start.5 = (bf16[128,1152]{1,0:T(8,128)(2,1)S(1)}, bf16[128,1152]{1,0:T(8,128)(2,1)S(1)}, u32[]{:S(2)}, u32[]{:S(2)}) collective-permute-start(bf16[128,1152]{1,0:T(8,128)(2,1)S(1)} %get-tuple-element.35), channel_id=1, source_target_pairs={{0,1},{1,2},{2,3},{3,0},{4,5},{5,6},{6,7},{7,4},{8,9},{9,10},{10,1... | collective-permute-start | bytes 884744 | tf_op jit(solution)/shard_map/ppermute | solution.py:365
  56.0 2.1 %collective-permute-start.6 = (bf16[128,896]{1,0:T(8,128)(2,1)S(1)}, bf16[128,896]{1,0:T(8,128)(2,1)S(1)}, u32[]{:S(2)}, u32[]{:S(2)}) collective-permute-start(bf16[128,896]{1,0:T(8,128)(2,1)S(1)} %get-tuple-element.36), channel_id=1, source_target_pairs={{0,3},{1,0},{2,1},{3,2},{4,7},{5,4},{6,5},{7,6},{8,11},{9,8},{10,9... | collective-permute-start | bytes 688136 | tf_op jit(solution)/shard_map/ppermute | solution.py:366
  58.1 0.8 %collective-permute-done.1.near_up_ref = bf16[128,896]{1,0:T(8,128)(2,1)S(1)} collective-permute-done((bf16[128,896]{1,0:T(8,128)(2,1)S(1)}, bf16[128,896]{1,0:T(8,128)(2,1)S(1)}, u32[]{:S(2)}, u32[]{:S(2)}) %collective-permute-start.1) | collective-permute-done | bytes 229408 | tf_op jit(solution)/shard_map/ppermute | solution.py:362
  58.9 1.0 %collective-permute-done.2.near_down_ref = bf16[128,1152]{1,0:T(8,128)(2,1)S(1)} collective-permute-done((bf16[128,1152]{1,0:T(8,128)(2,1)S(1)}, bf16[128,1152]{1,0:T(8,128)(2,1)S(1)}, u32[]{:S(2)}, u32[]{:S(2)}) %collective-permute-start.2) | collective-permute-done | bytes 294944 | tf_op jit(solution)/shard_map/ppermute | solution.py:363
  59.8 2.7 %shard_map.89.own_ref = f32[128,2048]{1,0:T(8,128)S(1)} custom-call(bf16[128,1024]{1,0:T(8,128)(2,1)S(1)} %get-tuple-element.29.rows_ref, bf16[128,896]{1,0:T(8,128)(2,1)S(1)} %collective-permute-done.1.near_up_ref, bf16[128,1152]{1,0:T(8,128)(2,1)S(1)} %collective-permute-done.2.near_down_ref, bf16[1024,8192]{1,0:T(8,128)(2,1)} %weights_ref.5), custom_call_target="tpu_custom_call" | custom-call | flops 2147483648 | bytes 2097152 | tf_op jit(solution)/shard_map/pallas_call | solution.py:328
  62.5 1.3 %collective-permute-done.6.both_down_ref = bf16[128,896]{1,0:T(8,128)(2,1)S(1)} collective-permute-done((bf16[128,896]{1,0:T(8,128)(2,1)S(1)}, bf16[128,896]{1,0:T(8,128)(2,1)S(1)}, u32[]{:S(2)}, u32[]{:S(2)}) %collective-permute-start.6) | collective-permute-done | bytes 229408 | tf_op jit(solution)/shard_map/ppermute | solution.py:366
  63.9 0.7 %collective-permute-done.5.both_up_ref = bf16[128,1152]{1,0:T(8,128)(2,1)S(1)} collective-permute-done((bf16[128,1152]{1,0:T(8,128)(2,1)S(1)}, bf16[128,1152]{1,0:T(8,128)(2,1)S(1)}, u32[]{:S(2)}, u32[]{:S(2)}) %collective-permute-start.5) | collective-permute-done | bytes 294944 | tf_op jit(solution)/shard_map/ppermute | solution.py:365
  64.6 0.8 %shard_map.92 = bf16[128,2048]{1,0:T(8,128)(2,1)} custom-call(f32[128,2048]{1,0:T(8,128)S(1)} %shard_map.89.own_ref, bf16[128,1152]{1,0:T(8,128)(2,1)S(1)} %collective-permute-done.5.both_up_ref, bf16[128,896]{1,0:T(8,128)(2,1)S(1)} %collective-permute-done.6.both_down_ref), custom_call_target="tpu_custom_call" | custom-call | tf_op jit(solution)/shard_map/pallas_call | solution.py:368
  (2 shorter events, 0.0 us)
Async XLA Ops:
  2.1 22.8 %all-to-all-start = ((bf16[32,96,128]{2,1,0:T(8,128)(2,1)}), bf16[32,96,128]{2,1,0:T(8,128)(2,1)S(1)}, u32[]{:S(2)}, u32[]{:S(2)}) async-start(bf16[32,96,128]{2,1,0:T(8,128)(2,1)} %get-tuple-element.21), calls=%async_computation | async-start | bytes 1572864 | tf_op jit(solution)/shard_map/all_to_all | solution.py:438
  10.4 8.5 %collective-permute-start = (bf16[16,1024]{1,0:T(8,128)(2,1)S(1)}, bf16[16,1024]{1,0:T(8,128)(2,1)S(1)}, u32[]{:S(2)}, u32[]{:S(2)}) collective-permute-start(bf16[16,1024]{1,0:T(8,128)(2,1)S(1)} %get-tuple-element.22.refs_0_), channel_id=1, source_target_pairs={{0,4},{4,8},{8,12},{12,16},{16,20},{20,24},{24,28},{28,32},{32,36}... | collective-permute-start | bytes 98312 | tf_op jit(solution)/shard_map/ppermute | solution.py:439
  29.5 12.8 %all-to-all-start.1 = ((bf16[32,32,128]{2,1,0:T(8,128)(2,1)}), bf16[32,32,128]{2,1,0:T(8,128)(2,1)S(1)}, u32[]{:S(2)}, u32[]{:S(2)}) async-start(bf16[32,32,128]{2,1,0:T(8,128)(2,1)} %get-tuple-element.27), calls=%async_computation.1 | async-start | bytes 524288 | tf_op jit(solution)/shard_map/all_to_all | solution.py:464
  42.3 2.2 %copy-start.2 = (bf16[1024,896]{1,0:T(8,128)(2,1)S(1)}, bf16[1024,896]{1,0:T(8,128)(2,1)}, u32[]{:S(2)}) copy-start(bf16[1024,896]{1,0:T(8,128)(2,1)} %get-tuple-element.34.rest_ref) | copy-start | bytes 5505028
  42.8 4.5 %copy-start.1 = (bf16[1024,2048]{1,0:T(8,128)(2,1)S(1)}, bf16[1024,2048]{1,0:T(8,128)(2,1)}, u32[]{:S(2)}) copy-start(bf16[1024,2048]{1,0:T(8,128)(2,1)} %get-tuple-element.30.near_ref) | copy-start | bytes 12582916
  42.9 11.1 %collective-permute-start.3 = (bf16[128,1152]{1,0:T(8,128)(2,1)S(1)}, bf16[128,1152]{1,0:T(8,128)(2,1)S(1)}, u32[]{:S(2)}, u32[]{:S(2)}) collective-permute-start(bf16[128,1152]{1,0:T(8,128)(2,1)S(1)} %get-tuple-element.33), channel_id=1, source_target_pairs={{0,1},{1,2},{2,3},{3,0},{4,5},{5,6},{6,7},{7,4},{8,9},{9,10},{10,1... | collective-permute-start | bytes 884744 | tf_op jit(solution)/shard_map/ppermute | solution.py:358
  45.0 9.0 %copy-start = (bf16[1024,2048]{1,0:T(8,128)(2,1)S(1)}, bf16[1024,2048]{1,0:T(8,128)(2,1)}, u32[]{:S(2)}) copy-start(bf16[1024,2048]{1,0:T(8,128)(2,1)} %shard_map.86.later_ref) | copy-start | bytes 12582916
  45.0 8.5 %collective-permute-start.4 = (bf16[128,896]{1,0:T(8,128)(2,1)S(1)}, bf16[128,896]{1,0:T(8,128)(2,1)S(1)}, u32[]{:S(2)}, u32[]{:S(2)}) collective-permute-start(bf16[128,896]{1,0:T(8,128)(2,1)S(1)} %shard_map.90), channel_id=1, source_target_pairs={{0,3},{1,0},{2,1},{3,2},{4,7},{5,4},{6,5},{7,6},{8,11},{9,8},{10,9... | collective-permute-start | bytes 688136 | tf_op jit(solution)/shard_map/ppermute | solution.py:360
  48.2 10.7 %collective-permute-start.1 = (bf16[128,896]{1,0:T(8,128)(2,1)S(1)}, bf16[128,896]{1,0:T(8,128)(2,1)S(1)}, u32[]{:S(2)}, u32[]{:S(2)}) collective-permute-start(bf16[128,896]{1,0:T(8,128)(2,1)S(1)} %get-tuple-element.31), channel_id=1, source_target_pairs={{0,1},{1,2},{2,3},{3,0},{4,5},{5,6},{6,7},{7,4},{8,9},{9,10},{10,1... | collective-permute-start | bytes 688136 | tf_op jit(solution)/shard_map/ppermute | solution.py:362
  48.2 11.6 %collective-permute-start.2 = (bf16[128,1152]{1,0:T(8,128)(2,1)S(1)}, bf16[128,1152]{1,0:T(8,128)(2,1)S(1)}, u32[]{:S(2)}, u32[]{:S(2)}) collective-permute-start(bf16[128,1152]{1,0:T(8,128)(2,1)S(1)} %get-tuple-element.32), channel_id=1, source_target_pairs={{0,3},{1,0},{2,1},{3,2},{4,7},{5,4},{6,5},{7,6},{8,11},{9,8},{10,9... | collective-permute-start | bytes 884744 | tf_op jit(solution)/shard_map/ppermute | solution.py:363
  54.8 9.8 %collective-permute-start.5 = (bf16[128,1152]{1,0:T(8,128)(2,1)S(1)}, bf16[128,1152]{1,0:T(8,128)(2,1)S(1)}, u32[]{:S(2)}, u32[]{:S(2)}) collective-permute-start(bf16[128,1152]{1,0:T(8,128)(2,1)S(1)} %get-tuple-element.35), channel_id=1, source_target_pairs={{0,1},{1,2},{2,3},{3,0},{4,5},{5,6},{6,7},{7,4},{8,9},{9,10},{10,1... | collective-permute-start | bytes 884744 | tf_op jit(solution)/shard_map/ppermute | solution.py:365
  56.0 7.9 %collective-permute-start.6 = (bf16[128,896]{1,0:T(8,128)(2,1)S(1)}, bf16[128,896]{1,0:T(8,128)(2,1)S(1)}, u32[]{:S(2)}, u32[]{:S(2)}) collective-permute-start(bf16[128,896]{1,0:T(8,128)(2,1)S(1)} %get-tuple-element.36), channel_id=1, source_target_pairs={{0,3},{1,0},{2,1},{3,2},{4,7},{5,4},{6,5},{7,6},{8,11},{9,8},{10,9... | collective-permute-start | bytes 688136 | tf_op jit(solution)/shard_map/ppermute | solution.py:366

commit v9 on v6

--- a/solution.py
+++ b/solution.py
@@ -141,7 +141,7 @@
 
 def conv_kernel(
     x_ref, taps_ref, skip_ref, high_ref, low_ref, twists_ref, weights_ref,
-    out_ref, held_ref, gated_ref, first_ref, left_ref, back_ref, sems,
+    out_ref, held_ref, gated_ref, first_ref, left_ref, back_ref, outer_ref, sems, out_sems,
 ):
     copies = fetch(weights_ref, held_ref, sems, 2, LEFT)
     lane = lax.broadcasted_iota(jnp.int32, (SLAB, ROWS), 1)
@@ -207,6 +207,10 @@
         left_ref[0, 1, rows, :] = jnp.concatenate([real[1], imag[1]], axis=1)
     for rows in blocks:
         back_ref[rows, :] = product(left_ref[0, 0, rows, :], left_ref[0, 1, rows, :])
+
+    def leaving(step):
+        here = pl.ds(pl.multiple_of(step * SLAB, SLAB), SLAB)
+        return pltpu.make_async_copy(outer_ref.at[:, here, :], out_ref.at[:, here, :], out_sems.at[step])
 
     @pl.loop(0, GROUP // SLAB)
     def _(step):
@@ -231,8 +235,11 @@
                 conv = real * math.cos(angle) - imag * math.sin(angle) if q else real
                 s = a + 8 * q
                 gated = gated_ref[s, pl.ds(offset, SLAB), :]
-                out_ref[s, pl.ds(offset, SLAB), :] = (conv + skip * gated).astype(bf16)
-
+                outer_ref[s, pl.ds(offset, SLAB), :] = (conv + skip * gated).astype(bf16)
+        leaving(step).start()
+
+    for step in range(GROUP // SLAB):
+        leaving(step).wait()
     for _, _, copy in copies:
         copy.wait()
 
@@ -384,9 +391,9 @@
     return pl.pallas_call(
         conv_kernel,
         in_specs=[VMEM] * 6 + [HBM],
-        out_specs=[VMEM, VMEM],
+        out_specs=[HBM, VMEM],
         out_shape=[
-            pltpu.VMEM((PARTS, GROUP, ROWS), bf16),
+            pltpu.HBM((PARTS, GROUP, ROWS), bf16),
             pltpu.VMEM((channels, UP), bf16),
         ],
         scratch_shapes=[
@@ -394,7 +401,9 @@
             pltpu.VMEM((4, 8, 2, SLAB, ROWS), f32),
             pltpu.VMEM((2, 2, PARTS * GROUP, 2 * ROWS), bf16),
             pltpu.VMEM((PARTS * GROUP, 2 * ROWS), f32),
+            pltpu.VMEM((PARTS, GROUP, ROWS), bf16),
             pltpu.SemaphoreType.DMA((len(LEFT),)),
+            pltpu.SemaphoreType.DMA((GROUP // SLAB,)),
         ],
         compiler_params=pltpu.CompilerParams(vmem_limit_bytes=16 * 2**20),
     )(*arrays)

time: 65.9 us -> 65.8 us (level)
  no operation moved by 1% of the time
where the time goes in v9:
time: 65.8 us; the launch traced here: 65.4 us
  starting transfers between devices  24.8 us (38%)
  Pallas kernels  21.5 us (33%)
  waiting for transfers between devices  17.9 us (27%)
  local copies, waits for them, and re-layouts  1.02 us (2%)
    all_to_all x1, starting transfers between devices, on_device(): arrived = lax.all_to_all(packed, 'seq', 0, 0, tiled=True)  8.26 us
    pallas_call x1, Pallas kernels, stage(): pl.pallas_call(stage_kernel, in_specs=[pl.BlockSpec(memory_space=pl.ANY)]...  7.74 us
    all_to_all x1, waiting for transfers between devices, on_device(): arrived = lax.all_to_all(packed, 'seq', 0, 0, tiled=True)  5.93 us
    all_to_all x1, waiting for transfers between devices, on_device(): outer = lax.all_to_all(outer, 'seq', 0, 0, tiled=True)  4.82 us
    pallas_call x1, Pallas kernels, convolve(): pl.pallas_call(conv_kernel, in_specs=[VMEM] * 6 + [HBM], out_specs=[HBM,...  4.37 us
    all_to_all x1, starting transfers between devices, on_device(): outer = lax.all_to_all(outer, 'seq', 0, 0, tiled=True)  3.88 us
    ppermute x1, starting transfers between devices, project(): near_down = lax.ppermute(near_down, 'ch', down)  3.22 us
    pallas_call x1, Pallas kernels, share(): pl.pallas_call(kernel, in_specs=[VMEM] * (len(arrays) - 1) + [HBM], out_s...  2.7 us
  transfers between devices with their start and end apart: 9, of which 9 were waited for; matrix products, arithmetic and copies ran while one was open for 1% of the time, Pallas kernels for 21%

profile of v9, /device:TPU:0, one launch (start us, length us, event | category | flops | bytes accessed | tf_op | source)
XLA Modules:
  0.0 65.4 jit_solution(12696242439257173666)
XLA Ops:
  0.0 2.1 %shard_map.82 = (bf16[32,96,128]{2,1,0:T(8,128)(2,1)}, bf16[16,1024]{1,0:T(8,128)(2,1)S(1)}) custom-call(bf16[3,128,1024]{2,1,0:T(8,128)(2,1)} %streams_ref.3, f32[128,1024]{1,0:T(8,128)} %filter_ref.1), custom_call_target="tpu_custom_call" | custom-call | tf_op jit(solution)/shard_map/pallas_call | solution.py:416
  2.1 8.3 %all-to-all-start = ((bf16[32,96,128]{2,1,0:T(8,128)(2,1)}), bf16[32,96,128]{2,1,0:T(8,128)(2,1)S(1)}, u32[]{:S(2)}, u32[]{:S(2)}) async-start(bf16[32,96,128]{2,1,0:T(8,128)(2,1)} %get-tuple-element.22), calls=%async_computation | async-start | bytes 1572864 | tf_op jit(solution)/shard_map/all_to_all | solution.py:435
  10.4 7.7 %shard_map.83 = (bf16[256,256]{1,0:T(8,128)(2,1)S(1)}, bf16[256,256]{1,0:T(8,128)(2,1)S(1)}, f32[32,2,128]{2,1,0:T(2,128)S(1)}, f32[3,3,1024]{2,1,0:T(4,128)S(1)...) custom-call(bf16[16,1024]{1,0:T(8,128)(2,1)S(1)} %get-tuple-element.23.refs_0_, ...), custom_call_target="tpu_custom_call" | custom-call | tf_op jit(solution)/shard_map/pallas_call | solution.py:376
  18.2 0.8 %dynamic_slice.7 = f32[32]{0:T(128)S(1)} dynamic-slice(f32[1024]{0:T(1024)} %param.11, s32[]{:T(128)S(6)} %select_n.4), dynamic_slice_sizes={32} | dynamic-slice | bytes 260 | tf_op jit(solution)/shard_map/dynamic_slice | solution.py:440
  18.9 0.1 constant_dynamic-slice_fusion
  19.0 5.9 %all-to-all-done.x_ref = bf16[32,96,128]{2,1,0:T(8,128)(2,1)S(1)} async-done(((bf16[32,96,128]{2,1,0:T(8,128)(2,1)}), bf16[32,96,128]{2,1,0:T(8,128)(2,1)S(1)}, u32[]{:S(2)}, u32[]{:S(2)}) %all-to-all-start) | async-done | bytes 786464 | tf_op jit(solution)/shard_map/all_to_all | solution.py:435
  24.9 0.1 broadcast_in_dim.5.skip_ref
  25.0 0.1 broadcast_in_dim.4.taps_ref
  25.1 4.4 %shard_map.84 = (bf16[32,32,128]{2,1,0:T(8,128)(2,1)}, bf16[1024,1152]{1,0:T(8,128)(2,1)S(1)}) custom-call(bf16[32,96,128]{2,1,0:T(8,128)(2,1)S(1)} %all-to-all-done.x_ref, f32[6,32,128]{2,1,0:T(8,128)S(1)} %broadcast_in_dim.4.taps_ref, f32[32,128]{1,0:T(8,128)S(1)} %broadcast_in_dim.5.skip_ref, bf16[256,256]{1,0:T(8,128)(2,1)S(1)} %get-tuple-element.25.high_ref, ...), custom_call_target="tpu_custom_call" | custom-call | tf_op jit(solution)/shard_map/pallas_call | solution.py:391
  29.5 3.9 %all-to-all-start.1 = ((bf16[32,32,128]{2,1,0:T(8,128)(2,1)}), bf16[32,32,128]{2,1,0:T(8,128)(2,1)S(1)}, u32[]{:S(2)}, u32[]{:S(2)}) async-start(bf16[32,32,128]{2,1,0:T(8,128)(2,1)} %get-tuple-element.28), calls=%async_computation.1 | async-start | bytes 524288 | tf_op jit(solution)/shard_map/all_to_all | solution.py:450
  33.4 2.1 %collective-permute-start = (bf16[16,1024]{1,0:T(8,128)(2,1)S(1)}, bf16[16,1024]{1,0:T(8,128)(2,1)S(1)}, u32[]{:S(2)}, u32[]{:S(2)}) collective-permute-start(bf16[16,1024]{1,0:T(8,128)(2,1)S(1)} %get-tuple-element.23.refs_0_), channel_id=1, source_target_pairs={{0,4},{4,8},{8,12},{12,16},{16,20},{20,24},{24,28},{28,32},{32,36}... | collective-permute-start | bytes 98312 | tf_op jit(solution)/shard_map/ppermute | solution.py:436
  35.4 0.8 %collective-permute-done.edge_ref = bf16[16,1024]{1,0:T(8,128)(2,1)S(1)} collective-permute-done((bf16[16,1024]{1,0:T(8,128)(2,1)S(1)}, bf16[16,1024]{1,0:T(8,128)(2,1)S(1)}, u32[]{:S(2)}, u32[]{:S(2)}) %collective-permute-start) | collective-permute-done | bytes 32800 | tf_op jit(solution)/shard_map/ppermute | solution.py:436
  36.3 1.2 %shard_map.85.query_ref = f32[128,1024]{1,0:T(8,128)S(1)} custom-call(bf16[3,128,1024]{2,1,0:T(8,128)(2,1)} %streams_ref.3, bf16[16,1024]{1,0:T(8,128)(2,1)S(1)} %collective-permute-done.edge_ref, f32[3,3,1024]{2,1,0:T(4,128)S(1)} %get-tuple-element.24.taps_ref, bf16[1024,1152]{1,0:T(8,128)(2,1)S(1)} %get-tuple-element.29.held_ref), custom_call_target="tpu_custom_call" | custom-call | tf_op jit(solution)/shard_map/pallas_call | solution.py:442
  37.5 4.8 %all-to-all-done.1 = bf16[32,32,128]{2,1,0:T(8,128)(2,1)S(1)} async-done(((bf16[32,32,128]{2,1,0:T(8,128)(2,1)}), bf16[32,32,128]{2,1,0:T(8,128)(2,1)S(1)}, u32[]{:S(2)}, u32[]{:S(2)}) %all-to-all-start.1) | async-done | bytes 262176 | tf_op jit(solution)/shard_map/all_to_all | solution.py:450
  42.3 0.0 copy-start.2
  42.3 0.5 shard_map.86
  42.8 0.0 copy-start.1
  42.8 1.6 %collective-permute-start.3 = (bf16[128,1152]{1,0:T(8,128)(2,1)S(1)}, bf16[128,1152]{1,0:T(8,128)(2,1)S(1)}, u32[]{:S(2)}, u32[]{:S(2)}) collective-permute-start(bf16[128,1152]{1,0:T(8,128)(2,1)S(1)} %get-tuple-element.35), channel_id=1, source_target_pairs={{0,1},{1,2},{2,3},{3,0},{4,5},{5,6},{6,7},{7,4},{8,9},{9,10},{10,1... | collective-permute-start | bytes 884744 | tf_op jit(solution)/shard_map/ppermute | solution.py:353
  44.5 0.0 copy-done.2
  44.5 0.5 shard_map.89
  44.9 0.0 copy-start
  45.0 2.4 %collective-permute-start.4 = (bf16[128,896]{1,0:T(8,128)(2,1)S(1)}, bf16[128,896]{1,0:T(8,128)(2,1)S(1)}, u32[]{:S(2)}, u32[]{:S(2)}) collective-permute-start(bf16[128,896]{1,0:T(8,128)(2,1)S(1)} %shard_map.89), channel_id=1, source_target_pairs={{0,3},{1,0},{2,1},{3,2},{4,7},{5,4},{6,5},{7,6},{8,11},{9,8},{10,9... | collective-permute-start | bytes 688136 | tf_op jit(solution)/shard_map/ppermute | solution.py:355
  47.3 0.0 copy-done.1
  47.3 0.8 %shard_map.87 = (bf16[128,896]{1,0:T(8,128)(2,1)S(1)}, bf16[128,1152]{1,0:T(8,128)(2,1)S(1)}) custom-call(bf16[128,1024]{1,0:T(8,128)(2,1)S(1)} %get-tuple-element.30.rows_ref, bf16[1024,2048]{1,0:T(8,128)(2,1)S(1)} %copy-done.1), custom_call_target="tpu_custom_call" | custom-call | flops 2147483648 | bytes 2097152 | tf_op jit(solution)/shard_map/pallas_call | solution.py:338
  48.1 0.1 collective-permute-start.1
  48.2 3.2 %collective-permute-start.2 = (bf16[128,1152]{1,0:T(8,128)(2,1)S(1)}, bf16[128,1152]{1,0:T(8,128)(2,1)S(1)}, u32[]{:S(2)}, u32[]{:S(2)}) collective-permute-start(bf16[128,1152]{1,0:T(8,128)(2,1)S(1)} %get-tuple-element.33), channel_id=1, source_target_pairs={{0,3},{1,0},{2,1},{3,2},{4,7},{5,4},{6,5},{7,6},{8,11},{9,8},{10,9... | collective-permute-start | bytes 884744 | tf_op jit(solution)/shard_map/ppermute | solution.py:358
  51.4 2.1 %collective-permute-done.4.far_down_ref = bf16[128,896]{1,0:T(8,128)(2,1)S(1)} collective-permute-done((bf16[128,896]{1,0:T(8,128)(2,1)S(1)}, bf16[128,896]{1,0:T(8,128)(2,1)S(1)}, u32[]{:S(2)}, u32[]{:S(2)}) %collective-permute-start.4) | collective-permute-done | bytes 229408 | tf_op jit(solution)/shard_map/ppermute | solution.py:355
  53.5 0.4 collective-permute-done.3.far_up_ref
  53.9 0.0 copy-done
  53.9 0.8 %shard_map.90 = (bf16[128,1152]{1,0:T(8,128)(2,1)S(1)}, bf16[128,896]{1,0:T(8,128)(2,1)S(1)}) custom-call(bf16[128,1024]{1,0:T(8,128)(2,1)S(1)} %get-tuple-element.30.rows_ref, bf16[1024,2048]{1,0:T(8,128)(2,1)S(1)} %copy-done, bf16[128,1152]{1,0:T(8,128)(2,1)S(1)} %collective-permute-done.3.far_up_ref, bf16[128,896]{1,0:T(8,128)(2,1)S(1)} %collective-permute-done.4.far_down_ref), custom_call_target="tpu_custom_call" | custom-call | flops 2147483648 | bytes 2097152 | tf_op jit(solution)/shard_map/pallas_call | solution.py:338
  54.8 1.2 %collective-permute-start.5 = (bf16[128,1152]{1,0:T(8,128)(2,1)S(1)}, bf16[128,1152]{1,0:T(8,128)(2,1)S(1)}, u32[]{:S(2)}, u32[]{:S(2)}) collective-permute-start(bf16[128,1152]{1,0:T(8,128)(2,1)S(1)} %get-tuple-element.37), channel_id=1, source_target_pairs={{0,1},{1,2},{2,3},{3,0},{4,5},{5,6},{6,7},{7,4},{8,9},{9,10},{10,1... | collective-permute-start | bytes 884744 | tf_op jit(solution)/shard_map/ppermute | solution.py:360
  56.0 2.1 %collective-permute-start.6 = (bf16[128,896]{1,0:T(8,128)(2,1)S(1)}, bf16[128,896]{1,0:T(8,128)(2,1)S(1)}, u32[]{:S(2)}, u32[]{:S(2)}) collective-permute-start(bf16[128,896]{1,0:T(8,128)(2,1)S(1)} %get-tuple-element.38), channel_id=1, source_target_pairs={{0,3},{1,0},{2,1},{3,2},{4,7},{5,4},{6,5},{7,6},{8,11},{9,8},{10,9... | collective-permute-start | bytes 688136 | tf_op jit(solution)/shard_map/ppermute | solution.py:361
  58.1 0.8 %collective-permute-done.1.near_up_ref = bf16[128,896]{1,0:T(8,128)(2,1)S(1)} collective-permute-done((bf16[128,896]{1,0:T(8,128)(2,1)S(1)}, bf16[128,896]{1,0:T(8,128)(2,1)S(1)}, u32[]{:S(2)}, u32[]{:S(2)}) %collective-permute-start.1) | collective-permute-done | bytes 229408 | tf_op jit(solution)/shard_map/ppermute | solution.py:357
  58.9 1.0 %collective-permute-done.2.near_down_ref = bf16[128,1152]{1,0:T(8,128)(2,1)S(1)} collective-permute-done((bf16[128,1152]{1,0:T(8,128)(2,1)S(1)}, bf16[128,1152]{1,0:T(8,128)(2,1)S(1)}, u32[]{:S(2)}, u32[]{:S(2)}) %collective-permute-start.2) | collective-permute-done | bytes 294944 | tf_op jit(solution)/shard_map/ppermute | solution.py:358
  59.8 2.7 %shard_map.88.own_ref = f32[128,2048]{1,0:T(8,128)S(1)} custom-call(bf16[128,1024]{1,0:T(8,128)(2,1)S(1)} %get-tuple-element.30.rows_ref, bf16[128,896]{1,0:T(8,128)(2,1)S(1)} %collective-permute-done.1.near_up_ref, bf16[128,1152]{1,0:T(8,128)(2,1)S(1)} %collective-permute-done.2.near_down_ref, bf16[1024,8192]{1,0:T(8,128)(2,1)} %weights_ref.3), custom_call_target="tpu_custom_call" | custom-call | flops 2147483648 | bytes 2097152 | tf_op jit(solution)/shard_map/pallas_call | solution.py:323
  62.5 1.3 %collective-permute-done.6.both_down_ref = bf16[128,896]{1,0:T(8,128)(2,1)S(1)} collective-permute-done((bf16[128,896]{1,0:T(8,128)(2,1)S(1)}, bf16[128,896]{1,0:T(8,128)(2,1)S(1)}, u32[]{:S(2)}, u32[]{:S(2)}) %collective-permute-start.6) | collective-permute-done | bytes 229408 | tf_op jit(solution)/shard_map/ppermute | solution.py:361
  63.9 0.7 %collective-permute-done.5.both_up_ref = bf16[128,1152]{1,0:T(8,128)(2,1)S(1)} collective-permute-done((bf16[128,1152]{1,0:T(8,128)(2,1)S(1)}, bf16[128,1152]{1,0:T(8,128)(2,1)S(1)}, u32[]{:S(2)}, u32[]{:S(2)}) %collective-permute-start.5) | collective-permute-done | bytes 294944 | tf_op jit(solution)/shard_map/ppermute | solution.py:360
  64.6 0.8 %shard_map.91 = bf16[128,2048]{1,0:T(8,128)(2,1)} custom-call(f32[128,2048]{1,0:T(8,128)S(1)} %shard_map.88.own_ref, bf16[128,1152]{1,0:T(8,128)(2,1)S(1)} %collective-permute-done.5.both_up_ref, bf16[128,896]{1,0:T(8,128)(2,1)S(1)} %collective-permute-done.6.both_down_ref), custom_call_target="tpu_custom_call" | custom-call | tf_op jit(solution)/shard_map/pallas_call | solution.py:363
  (2 shorter events, 0.0 us)
Async XLA Ops:
  2.1 22.8 %all-to-all-start = ((bf16[32,96,128]{2,1,0:T(8,128)(2,1)}), bf16[32,96,128]{2,1,0:T(8,128)(2,1)S(1)}, u32[]{:S(2)}, u32[]{:S(2)}) async-start(bf16[32,96,128]{2,1,0:T(8,128)(2,1)} %get-tuple-element.22), calls=%async_computation | async-start | bytes 1572864 | tf_op jit(solution)/shard_map/all_to_all | solution.py:435
  29.5 12.8 %all-to-all-start.1 = ((bf16[32,32,128]{2,1,0:T(8,128)(2,1)}), bf16[32,32,128]{2,1,0:T(8,128)(2,1)S(1)}, u32[]{:S(2)}, u32[]{:S(2)}) async-start(bf16[32,32,128]{2,1,0:T(8,128)(2,1)} %get-tuple-element.28), calls=%async_computation.1 | async-start | bytes 524288 | tf_op jit(solution)/shard_map/all_to_all | solution.py:450
  33.4 2.9 %collective-permute-start = (bf16[16,1024]{1,0:T(8,128)(2,1)S(1)}, bf16[16,1024]{1,0:T(8,128)(2,1)S(1)}, u32[]{:S(2)}, u32[]{:S(2)}) collective-permute-start(bf16[16,1024]{1,0:T(8,128)(2,1)S(1)} %get-tuple-element.23.refs_0_), channel_id=1, source_target_pairs={{0,4},{4,8},{8,12},{12,16},{16,20},{20,24},{24,28},{28,32},{32,36}... | collective-permute-start | bytes 98312 | tf_op jit(solution)/shard_map/ppermute | solution.py:436
  42.3 2.2 %copy-start.2 = (bf16[1024,896]{1,0:T(8,128)(2,1)S(1)}, bf16[1024,896]{1,0:T(8,128)(2,1)}, u32[]{:S(2)}) copy-start(bf16[1024,896]{1,0:T(8,128)(2,1)} %get-tuple-element.36.rest_ref) | copy-start | bytes 5505028
  42.8 4.5 %copy-start.1 = (bf16[1024,2048]{1,0:T(8,128)(2,1)S(1)}, bf16[1024,2048]{1,0:T(8,128)(2,1)}, u32[]{:S(2)}) copy-start(bf16[1024,2048]{1,0:T(8,128)(2,1)} %get-tuple-element.31.near_ref) | copy-start | bytes 12582916
  42.8 11.1 %collective-permute-start.3 = (bf16[128,1152]{1,0:T(8,128)(2,1)S(1)}, bf16[128,1152]{1,0:T(8,128)(2,1)S(1)}, u32[]{:S(2)}, u32[]{:S(2)}) collective-permute-start(bf16[128,1152]{1,0:T(8,128)(2,1)S(1)} %get-tuple-element.35), channel_id=1, source_target_pairs={{0,1},{1,2},{2,3},{3,0},{4,5},{5,6},{6,7},{7,4},{8,9},{9,10},{10,1... | collective-permute-start | bytes 884744 | tf_op jit(solution)/shard_map/ppermute | solution.py:353
  44.9 9.0 %copy-start = (bf16[1024,2048]{1,0:T(8,128)(2,1)S(1)}, bf16[1024,2048]{1,0:T(8,128)(2,1)}, u32[]{:S(2)}) copy-start(bf16[1024,2048]{1,0:T(8,128)(2,1)} %get-tuple-element.34.later_ref) | copy-start | bytes 12582916
  45.0 8.5 %collective-permute-start.4 = (bf16[128,896]{1,0:T(8,128)(2,1)S(1)}, bf16[128,896]{1,0:T(8,128)(2,1)S(1)}, u32[]{:S(2)}, u32[]{:S(2)}) collective-permute-start(bf16[128,896]{1,0:T(8,128)(2,1)S(1)} %shard_map.89), channel_id=1, source_target_pairs={{0,3},{1,0},{2,1},{3,2},{4,7},{5,4},{6,5},{7,6},{8,11},{9,8},{10,9... | collective-permute-start | bytes 688136 | tf_op jit(solution)/shard_map/ppermute | solution.py:355
  48.1 10.7 %collective-permute-start.1 = (bf16[128,896]{1,0:T(8,128)(2,1)S(1)}, bf16[128,896]{1,0:T(8,128)(2,1)S(1)}, u32[]{:S(2)}, u32[]{:S(2)}) collective-permute-start(bf16[128,896]{1,0:T(8,128)(2,1)S(1)} %get-tuple-element.32), channel_id=1, source_target_pairs={{0,1},{1,2},{2,3},{3,0},{4,5},{5,6},{6,7},{7,4},{8,9},{9,10},{10,1... | collective-permute-start | bytes 688136 | tf_op jit(solution)/shard_map/ppermute | solution.py:357
  48.2 11.6 %collective-permute-start.2 = (bf16[128,1152]{1,0:T(8,128)(2,1)S(1)}, bf16[128,1152]{1,0:T(8,128)(2,1)S(1)}, u32[]{:S(2)}, u32[]{:S(2)}) collective-permute-start(bf16[128,1152]{1,0:T(8,128)(2,1)S(1)} %get-tuple-element.33), channel_id=1, source_target_pairs={{0,3},{1,0},{2,1},{3,2},{4,7},{5,4},{6,5},{7,6},{8,11},{9,8},{10,9... | collective-permute-start | bytes 884744 | tf_op jit(solution)/shard_map/ppermute | solution.py:358
  54.8 9.8 %collective-permute-start.5 = (bf16[128,1152]{1,0:T(8,128)(2,1)S(1)}, bf16[128,1152]{1,0:T(8,128)(2,1)S(1)}, u32[]{:S(2)}, u32[]{:S(2)}) collective-permute-start(bf16[128,1152]{1,0:T(8,128)(2,1)S(1)} %get-tuple-element.37), channel_id=1, source_target_pairs={{0,1},{1,2},{2,3},{3,0},{4,5},{5,6},{6,7},{7,4},{8,9},{9,10},{10,1... | collective-permute-start | bytes 884744 | tf_op jit(solution)/shard_map/ppermute | solution.py:360
  56.0 7.9 %collective-permute-start.6 = (bf16[128,896]{1,0:T(8,128)(2,1)S(1)}, bf16[128,896]{1,0:T(8,128)(2,1)S(1)}, u32[]{:S(2)}, u32[]{:S(2)}) collective-permute-start(bf16[128,896]{1,0:T(8,128)(2,1)S(1)} %get-tuple-element.38), channel_id=1, source_target_pairs={{0,3},{1,0},{2,1},{3,2},{4,7},{5,4},{6,5},{7,6},{8,11},{9,8},{10,9... | collective-permute-start | bytes 688136 | tf_op jit(solution)/shard_map/ppermute | solution.py:361
